TPU v7x, 32 devices: a whole 2x2x4 slice. The times are simulated.
32 devices in a mesh: parts: 2 (over y), shard: 4 (over z), ckpt: 2 (over x), sub: 2 (over core).
Axes of the slice: x: 2, y: 2, z: 4, core: 2. Of those that a mesh axis runs over, the one named last changes fastest.
Arguments:
- train_grads: bfloat16 [2, 6144, 16384], P('ckpt', ('parts', 'shard'), 'sub'), parts along dimension 1, may hold values from -0.046875 to 0.046875
- query_grads: float32 [2, 256, 16384], P('ckpt', ('parts', 'shard'), 'sub'), parts along dimension 1, may hold values from -6 to 6
- precond: float32 [2, 16384], P('ckpt', 'sub'), may hold values from 0.3 to 3
- learn_rates: float32 [64], replicated, may hold values from 0.25 to 2.5
- ckpt_order: int32 [2], replicated, may hold values from 0 to 63
Outputs:
- scores: float32 [128, 6144], P(('ckpt', 'sub'), ('parts', 'shard')), parts along dimension 1
There are 2 independent parts, one for each index of `parts`. A program takes and returns all parts, laid end to end along the dimension named above; an argument that names none is the same for every part. Nothing has to cross between parts.
All inputs are finite; a program needn't handle non-finite values.
Results may differ from a plain program's by a relative error of at most 0.0029.
Values may be sent and summed in bfloat16 or wider, within the bound.
No kernel may reach another device: no remote copies, remote signals or barrier semaphores. Data moves between devices by JAX's collectives and lax.ppermute only.
A program may use at most 128 MiB of HBM per device.

v0:
```python
import jax
import jax.numpy as jnp
from jax import lax
from jax.sharding import PartitionSpec as P


def score_rows(block_rows, train_local):
    return lax.dot_general(
        block_rows, train_local, (((1,), (1,)), ((), ())), preferred_element_type=jnp.float32
    )


def per_device(train_grads, query_grads, precond, learn_rates, ckpt_order):
    train_local = train_grads[0]
    query_local = query_grads[0]
    holder = lax.axis_index("ckpt")
    count = ckpt_order.shape[0]
    positions = jnp.arange(count, dtype=jnp.int32)
    number = jnp.sum(jnp.where(positions == holder, ckpt_order, 0))
    table_steps = jnp.arange(learn_rates.shape[0], dtype=jnp.int32)
    step_rate = jnp.sum(jnp.where(table_steps == number, learn_rates, 0.0))
    scaled = (lax.all_gather(query_local, "shard", axis=0, tiled=True) * precond).astype(
        jnp.bfloat16
    )
    partial_value = score_rows(scaled, train_local)
    weighted = partial_value * step_rate
    totals = lax.psum(weighted, ("ckpt", "sub"))
    groups = lax.axis_size(("ckpt", "sub"))
    share = totals.shape[0] // groups
    result = lax.dynamic_slice_in_dim(totals, lax.axis_index(("ckpt", "sub")) * share, share, 0)
    return result


def solution(mesh):
    return jax.shard_map(
        per_device,
        mesh=mesh,
        in_specs=(
            P("ckpt", ("parts", "shard"), "sub"),
            P("ckpt", ("parts", "shard"), "sub"),
            P("ckpt", "sub"),
            P(),
            P(),
        ),
        out_specs=P(("ckpt", "sub"), ("parts", "shard")),
        check_vma=False,
    )
```

profile of v0, /device:TPU:1, one launch (start us, length us, event | category | flops | bytes accessed | tf_op | source)
XLA Modules:
  0.0 141.4 jit_solution(13012951916172336209)
XLA Ops:
  6.5 0.0 all-gather.3.cloned.1.call-start
  6.5 0.7 all-gather.3.cloned.1.call-update
  7.3 0.0 all-reduce.2.cloned.1.call-start
  7.3 1.3 fusion.10
  8.6 1.9 %fusion.11 = f32[]{:T(128)} fusion(f32[64]{0:T(128)} %param.8, s32[]{:T(128)} %fusion.10), kind=kLoop, calls=%fused_computation.9 | loop fusion | flops 191 | bytes 264 | tf_op jit(solution)/shard_map/reduce_sum | solution.py:21
  10.5 81.3 %all-gather.3.cloned.1.call-done = f32[1,128,8192]{2,1,0:T(8,128)} async-done(((f32[1,32,8192]{2,1,0:T(8,128)}), f32[1,128,8192]{2,1,0:T(8,128)}) %all-gather.3.cloned.1.call-update) | async-done | bytes 4194320 | tf_op jit(solution)/shard_map/all_gather | solution.py:22
  91.8 11.4 %fusion.5 = f32[128,768]{1,0:T(8,128)} fusion(bf16[1,768,8192]{2,1,0:T(8,128)(2,1)} %param.5, f32[1,128,8192]{2,1,0:T(8,128)} %all-gather.3.cloned.1.call-done, f32[8192]{0:T(1024)} %bitcast.13, f32[]{:T(128)} %fusion.11), kind=kOutput, calls=%fused_computation.5 | convolution fusion | flops 1612808192 | bytes 17203204 | tf_op jit(solution)/shard_map/dot_general | solution.py:8
  103.3 0.0 all-reduce.2.cloned.1.call-update
  103.3 29.7 %all-reduce.2.cloned.1.call-done = f32[128,768]{1,0:T(8,128)} async-done(((f32[128,768]{1,0:T(8,128)}), f32[128,768]{1,0:T(8,128)}) %all-reduce.2.cloned.1.call-update) | async-done | bytes 393232 | tf_op jit(solution)/shard_map/psum | solution.py:27
  133.0 1.5 %constant_dynamic-slice_fusion = f32[32,768]{1,0:T(8,128)} fusion(f32[128,768]{1,0:T(8,128)} %all-reduce.2.cloned.1.call-done, s32[]{:T(128)S(6)} %select_n.13), kind=kLoop, calls=%fused_computation.10 | loop fusion | bytes 196612 | tf_op jit(solution)/shard_map/dynamic_slice | solution.py:30
Async XLA Ops:
  6.5 85.3 %all-gather.3.cloned.1.call-start = ((), (), s32[]{:S(2)}) async-start(), calls=%async_computation.1 | async-start | bytes 5242880 | tf_op jit(solution)/shard_map/all_gather | solution.py:22
  7.3 125.7 %all-reduce.2.cloned.1.call-start = ((), (), s32[]{:S(2)}) async-start(), calls=%async_computation | async-start | bytes 786432 | tf_op jit(solution)/shard_map/psum | solution.py:27
Sparse Core Ops, SparseCore 0:
  8.9 82.8 all-gather.2
  103.4 29.5 all-reduce.1
where the time goes:
time: 144 us; the launch traced here: 141 us
  waiting for transfers between devices  112 us (78%)
  between operations  13.4 us (9%)
  matrix products  11.4 us (8%)
  other arithmetic  3.19 us (2%)
  local copies, waits for them, and re-layouts  1.54 us (1%)
    all_gather x1, waiting for transfers between devices, per_device(): lax.all_gather(query_local, 'shard', axis=0, tiled=True) * precond  81.3 us
    psum x1, waiting for transfers between devices, per_device(): totals = lax.psum(weighted, ('ckpt', 'sub'))  29.7 us
    dot_general x1, matrix products, score_rows(): lax.dot_general(block_rows, train_local, (((1,), (1,)), ((), ())), prefer...  11.4 us
  transfers between devices with their start and end apart: 2, of which 2 were waited for; matrix products, arithmetic and copies ran while one was open for 2% of the time, Pallas kernels for 0%

commit v1 on v0

v1 whole, which is shorter than its diff:
```python
import jax
import jax.numpy as jnp
from jax import lax
from jax.sharding import PartitionSpec as P

CHUNKS = 4
AXES = ("parts", "shard", "ckpt", "sub")


def line_ring(n):
    odd = list(range(1, n, 2))
    even = list(range(0, n, 2))
    return [0] + odd + even[:0:-1]


def ring_position(z, n):
    return jnp.where(z == 0, 0, jnp.where(z % 2 == 1, (z + 1) // 2, n - z // 2))


def score_rows(block_rows, train_rows):
    return lax.dot_general(
        block_rows, train_rows, (((1,), (1,)), ((), ())), preferred_element_type=jnp.float32
    )


def per_device(sizes, train_grads, query_grads, precond, learn_rates, ckpt_order):
    train_local = train_grads[0]
    query_local = query_grads[0]
    parts, shards, ckpts, subs = sizes
    groups = ckpts * subs
    ring = line_ring(shards)
    place = {z: i for i, z in enumerate(ring)}
    hops = [(ring[i], ring[(i + 1) % shards]) for i in range(shards)] if shards > 1 else []
    per_group = shards // groups

    width = query_local.shape[1] // CHUNKS
    current = [
        (query_local[:, j * width : (j + 1) * width] * precond[:, j * width : (j + 1) * width]).astype(jnp.bfloat16)
        for j in range(CHUNKS)
    ]

    holder = lax.axis_index("ckpt")
    positions = jnp.arange(ckpt_order.shape[0], dtype=jnp.int32)
    number = jnp.sum(jnp.where(positions == holder, ckpt_order, 0))
    table_steps = jnp.arange(learn_rates.shape[0], dtype=jnp.int32)
    step_rate = jnp.sum(jnp.where(table_steps == number, learn_rates, 0.0))

    sums = []
    for step in range(shards):
        total = None
        following = []
        for j in range(CHUNKS):
            if step < shards - 1:
                following.append(lax.ppermute(current[j], "shard", hops))
            piece = score_rows(current[j], train_local[:, j * width : (j + 1) * width])
            total = piece if total is None else total + piece
        sums.append(total)
        current = following

    me = lax.axis_index("shard")
    my_place = ring_position(me, shards)
    my_group = lax.axis_index(("ckpt", "sub"))

    def blocks_of(group):
        rows = []
        for k in range(per_group):
            step = (my_place - ring_position(group * per_group + k, shards)) % shards
            value = jnp.zeros_like(sums[0])
            for s in range(shards - 1):
                value = jnp.where(step == s, sums[s], value)
            rows.append(value)
        return jnp.concatenate(rows, axis=0) * step_rate

    def last_of(z):
        return ring[(place[z] + 1) % shards]

    def device(p, z, g):
        return ((p * shards + z) * ckpts + g // subs) * subs + g % subs

    result = blocks_of(my_group)
    for d in range(1, groups):
        pairs = [
            (device(p, z, g), device(p, z, (g + d) % groups))
            for p in range(parts)
            for z in range(shards)
            for g in range(groups)
            if per_group > 1 or last_of(z) != (g + d) % groups
        ]
        result = result + lax.ppermute(blocks_of((my_group + d) % groups), AXES, pairs)

    last = sums[-1] * step_rate
    late = jnp.where((last_of_traced(my_place, shards) // per_group) == my_group, last, 0.0)
    for d in range(1, groups):
        pairs = [
            (device(p, z, g), device(p, z, (g + d) % groups))
            for p in range(parts)
            for z in range(shards)
            for g in range(groups)
            if last_of(z) // per_group == (g + d) % groups
        ]
        late = late + lax.ppermute(last, AXES, pairs)
    if per_group == 1:
        return result + late
    slot = last_of_traced(my_place, shards) % per_group
    rows = late.shape[0]
    return lax.dynamic_update_slice_in_dim(
        result, lax.dynamic_slice_in_dim(result, slot * rows, rows, 0) + late, slot * rows, 0
    )


def last_of_traced(my_place, n):
    p = (my_place + 1) % n
    return jnp.where(p <= n // 2, jnp.maximum(2 * p - 1, 0), 2 * (n - p))


def solution(mesh):
    sizes = tuple(mesh.shape[a] for a in AXES)

    def run(*args):
        return per_device(sizes, *args)

    return jax.shard_map(
        run,
        mesh=mesh,
        in_specs=(
            P("ckpt", ("parts", "shard"), "sub"),
            P("ckpt", ("parts", "shard"), "sub"),
            P("ckpt", "sub"),
            P(),
            P(),
        ),
        out_specs=P(("ckpt", "sub"), ("parts", "shard")),
        check_vma=False,
    )
```

time: 144 us -> 84 us (0.58); the launches traced: 141 us -> 83.3 us
  waiting for transfers between devices: 112 us -> 11.2 us
  matrix products: 11.4 us -> 40.7 us
  starting transfers between devices: 0.04 us -> 25.8 us
  between operations: 13.4 us -> 0.26 us
    all_gather x1 -> x0, waiting for transfers between devices: 81.3 us -> none  [per_device(): lax.all_gather(query_local, 'shard', axis=0, tiled=True) * precond]
    psum x1 -> x0, waiting for transfers between devices: 29.7 us -> none  [per_device(): totals = lax.psum(weighted, ('ckpt', 'sub'))]
    dot_general x1 -> x16, matrix products: 11.4 us -> 40.7 us  [score_rows(): lax.dot_general(block_rows, train_rows, (((1,), (1,)), ((), ())), preferr...]
    ppermute x0 -> x18, starting transfers between devices: none -> 25.8 us  [the longest x12 11 us: per_device(): following.append(lax.ppermute(current[j], 'shard', hops))]
    ppermute x0 -> x18, waiting for transfers between devices: none -> 11.2 us  [the longest x12 6.43 us: per_device(): following.append(lax.ppermute(current[j], 'shard', hops))]
    dynamic_slice x1 -> x0, local copies, waits for them, and re-layouts: 1.54 us -> none  [per_device(): lax.dynamic_slice_in_dim(totals, lax.axis_index(('ckpt', 'sub')) * share,...]
  transfers between devices with their start and end apart: 2 -> 18, of which waited for: 2 -> 7; matrix products, arithmetic and copies ran while one was open for 2% -> 51% of each run, Pallas kernels for 0% -> 0%
where the time goes in v1:
time: 84 us; the launch traced here: 83.3 us
  matrix products  40.7 us (48%)
  starting transfers between devices  25.8 us (31%)
  waiting for transfers between devices  11.2 us (13%)
  other arithmetic  4.53 us (5%)
    dot_general x16, matrix products, score_rows(): lax.dot_general(block_rows, train_rows, (((1,), (1,)), ((), ())), preferr...  40.7 us
    ppermute x12, starting transfers between devices, per_device(): following.append(lax.ppermute(current[j], 'shard', hops))  11 us
    ppermute x3, starting transfers between devices, per_device(): lax.ppermute(blocks_of((my_group + d) % groups), AXES, pairs)  10.9 us
    ppermute x12, waiting for transfers between devices, per_device(): following.append(lax.ppermute(current[j], 'shard', hops))  6.43 us
    ppermute x3, waiting for transfers between devices, per_device(): late = late + lax.ppermute(last, AXES, pairs)  4.71 us
    ppermute x3, starting transfers between devices, per_device(): late = late + lax.ppermute(last, AXES, pairs)  3.88 us
  transfers between devices with their start and end apart: 18, of which 7 were waited for; matrix products, arithmetic and copies ran while one was open for 51% of the time, Pallas kernels for 0%

profile of v1, /device:TPU:1, one launch (start us, length us, event | category | flops | bytes accessed | tf_op | source)
XLA Modules:
  0.0 83.3 jit_solution(10215056505175195919)
XLA Ops:
  2.1 2.2 %collective-permute-start.4 = (bf16[32,2048]{1,0:T(8,128)(2,1)S(1)}, bf16[32,2048]{1,0:T(8,128)(2,1)S(1)}, u32[]{:S(2)}, u32[]{:S(2)}) collective-permute-start(bf16[32,2048]{1,0:T(8,128)(2,1)S(1)} %get-tuple-element.7), channel_id=1, source_target_pairs={{0,4},{4,12},{12,8},{8,0},{1,5},{5,13},{13,9},{9,1},{2,6},{6,14},{... | collective-permute-start | bytes 393224 | tf_op jit(solution)/shard_map/ppermute | solution.py:54
  4.2 2.3 %collective-permute-start.2 = (bf16[32,2048]{1,0:T(8,128)(2,1)S(1)}, bf16[32,2048]{1,0:T(8,128)(2,1)S(1)}, u32[]{:S(2)}, u32[]{:S(2)}) collective-permute-start(bf16[32,2048]{1,0:T(8,128)(2,1)S(1)} %get-tuple-element.8), channel_id=1, source_target_pairs={{0,4},{4,12},{12,8},{8,0},{1,5},{5,13},{13,9},{9,1},{2,6},{6,14},{... | collective-permute-start | bytes 393224 | tf_op jit(solution)/shard_map/ppermute | solution.py:54
  6.8 2.9 %fusion.10 = f32[32,768]{1,0:T(8,128)S(1)} fusion(bf16[32,2048]{1,0:T(8,128)(2,1)S(1)} %get-tuple-element.7, bf16[768,8192]{1,0:T(8,128)(2,1)} %bitcast.22), kind=kOutput, calls=%fused_computation.10 | convolution fusion | flops 100663296 | bytes 3375104 | tf_op jit(solution)/shard_map/dot_general | solution.py:21
  9.7 2.9 %fusion.18 = f32[32,768]{1,0:T(8,128)S(1)} fusion(bf16[32,2048]{1,0:T(8,128)(2,1)S(1)} %get-tuple-element.8, bf16[768,8192]{1,0:T(8,128)(2,1)} %bitcast.23), kind=kOutput, calls=%fused_computation.18 | convolution fusion | flops 100663296 | bytes 3375104 | tf_op jit(solution)/shard_map/dot_general | solution.py:21
  12.6 2.9 %fusion.2 = f32[32,768]{1,0:T(8,128)S(1)} fusion(bf16[32,2048]{1,0:T(8,128)(2,1)S(1)} %get-tuple-element.6, bf16[768,8192]{1,0:T(8,128)(2,1)} %bitcast.24), kind=kOutput, calls=%fused_computation.2 | convolution fusion | flops 100663296 | bytes 3375104 | tf_op jit(solution)/shard_map/dot_general | solution.py:21
  15.5 2.9 %fusion.56 = f32[32,768]{1,0:T(8,128)S(1)} fusion(f32[32,768]{1,0:T(8,128)S(1)} %fusion.2, f32[32,768]{1,0:T(8,128)S(1)} %fusion.10, f32[32,768]{1,0:T(8,128)S(1)} %fusion.18, bf16[32,2048]{1,0:T(8,128)(2,1)S(1)} %get-tuple-element.5, bf16[768,8192]{1,0:T(8,128)(2,1)} %bitcast.25), kind=kOutput, calls=%fused_computation.40 | convolution fusion | flops 100737024 | bytes 3670016 | tf_op jit(solution)/shard_map/dot_general | solution.py:21
  20.5 2.9 %fusion.12 = f32[32,768]{1,0:T(8,128)S(1)} fusion(bf16[32,2048]{1,0:T(8,128)(2,1)S(1)} %collective-permute-done.4, bf16[768,8192]{1,0:T(8,128)(2,1)} %bitcast.26), kind=kOutput, calls=%fused_computation.12 | convolution fusion | flops 100663296 | bytes 3375104 | tf_op jit(solution)/shard_map/dot_general | solution.py:21
  24.7 2.9 %fusion.20 = f32[32,768]{1,0:T(8,128)S(1)} fusion(bf16[32,2048]{1,0:T(8,128)(2,1)S(1)} %collective-permute-done.2, bf16[768,8192]{1,0:T(8,128)(2,1)} %bitcast.27), kind=kOutput, calls=%fused_computation.20 | convolution fusion | flops 100663296 | bytes 3375104 | tf_op jit(solution)/shard_map/dot_general | solution.py:21
  27.6 2.3 %collective-permute-start.3 = (bf16[32,2048]{1,0:T(8,128)(2,1)S(1)}, bf16[32,2048]{1,0:T(8,128)(2,1)S(1)}, u32[]{:S(2)}, u32[]{:S(2)}) collective-permute-start(bf16[32,2048]{1,0:T(8,128)(2,1)S(1)} %collective-permute-done.2), channel_id=1, source_target_pairs={{0,4},{4,12},{12,8},{8,0},{1,5},{5,13},{13,9},{9,1},{2,6},{6,14},{... | collective-permute-start | bytes 393224 | tf_op jit(solution)/shard_map/ppermute | solution.py:54
  30.0 2.9 %fusion.4 = f32[32,768]{1,0:T(8,128)S(1)} fusion(bf16[32,2048]{1,0:T(8,128)(2,1)S(1)} %collective-permute-done.6, bf16[768,8192]{1,0:T(8,128)(2,1)} %bitcast.28), kind=kOutput, calls=%fused_computation.4 | convolution fusion | flops 100663296 | bytes 3375104 | tf_op jit(solution)/shard_map/dot_general | solution.py:21
  33.3 3.1 %fusion.47 = f32[32,768]{1,0:T(8,128)S(1)} fusion(f32[32,768]{1,0:T(8,128)S(1)} %fusion.4, f32[32,768]{1,0:T(8,128)S(1)} %fusion.12, f32[32,768]{1,0:T(8,128)S(1)} %fusion.20, bf16[32,2048]{1,0:T(8,128)(2,1)S(1)} %collective-permute-done, bf16[768,8192]{1,0:T(8,128)(2,1)} %bitcast.29), kind=kOutput, calls=%fused_computation.37 | convolution fusion | flops 100737024 | bytes 3670016 | tf_op jit(solution)/shard_map/dot_general | solution.py:21
  37.7 2.9 %fusion.6 = f32[32,768]{1,0:T(8,128)S(1)} fusion(bf16[32,2048]{1,0:T(8,128)(2,1)S(1)} %collective-permute-done.7, bf16[768,8192]{1,0:T(8,128)(2,1)} %bitcast.30), kind=kOutput, calls=%fused_computation.6 | convolution fusion | flops 100663296 | bytes 3375104 | tf_op jit(solution)/shard_map/dot_general | solution.py:21
  40.7 3.1 %fusion.14 = f32[32,768]{1,0:T(8,128)S(1)} fusion(bf16[32,2048]{1,0:T(8,128)(2,1)S(1)} %collective-permute-done.5, bf16[768,8192]{1,0:T(8,128)(2,1)} %bitcast.31), kind=kOutput, calls=%fused_computation.14 | convolution fusion | flops 100663296 | bytes 3375104 | tf_op jit(solution)/shard_map/dot_general | solution.py:21
  43.8 2.9 %fusion.22 = f32[32,768]{1,0:T(8,128)S(1)} fusion(bf16[32,2048]{1,0:T(8,128)(2,1)S(1)} %collective-permute-done.3, bf16[768,8192]{1,0:T(8,128)(2,1)} %bitcast.32), kind=kOutput, calls=%fused_computation.22 | convolution fusion | flops 100663296 | bytes 3375104 | tf_op jit(solution)/shard_map/dot_general | solution.py:21
  46.7 3.6 %select_multiply_fusion.2 = (f32[32,768]{1,0:T(8,128)S(1)}, f32[32,768]{1,0:T(8,128)S(1)}, f32[32,768]{1,0:T(8,128)S(1)}, f32[32,768]{1,0:T(8,128)S(1)}) fusion(f32[32,768]{1,0:T(8,128)S(1)} %fusion.47, f32[32,768]{1,0:T(8,128)S(1)} %fusion.56, f32[]{:T(128)} %fusion.76, pred[]{:T(512)S(6)} %eq.110, pred[]{:T(512)S(6)} %eq.109, pred[]{:T(512)S(6)} %eq.108, ...), kind=kOutput, calls=%fused_computation.56 | convolution fusion | flops 101031936 | bytes 4162057 | tf_op jit(solution)/shard_map/dot_general | solution.py:21
  50.3 5.7 %collective-permute-start.10 = (f32[32,768]{1,0:T(8,128)S(1)}, f32[32,768]{1,0:T(8,128)S(1)}, u32[]{:S(2)}, u32[]{:S(2)}) collective-permute-start(f32[32,768]{1,0:T(8,128)S(1)} %get-tuple-element.10), channel_id=1, source_target_pairs={{0,3},{1,0},{3,2},{5,4},{6,5},{7,6},{8,11},{10,9},{11,10},{12,15},... | collective-permute-start | bytes 294920 | tf_op jit(solution)/shard_map/ppermute | solution.py:89
  56.0 2.4 %collective-permute-start.8 = (f32[32,768]{1,0:T(8,128)S(1)}, f32[32,768]{1,0:T(8,128)S(1)}, u32[]{:S(2)}, u32[]{:S(2)}) collective-permute-start(f32[32,768]{1,0:T(8,128)S(1)} %get-tuple-element.9), channel_id=1, source_target_pairs={{1,2},{2,3},{3,0},{4,5},{5,6},{7,4},{8,9},{9,10},{10,11},{12,13},{... | collective-permute-start | bytes 294920 | tf_op jit(solution)/shard_map/ppermute | solution.py:89
  58.4 2.8 %collective-permute-start.9 = (f32[32,768]{1,0:T(8,128)S(1)}, f32[32,768]{1,0:T(8,128)S(1)}, u32[]{:S(2)}, u32[]{:S(2)}) collective-permute-start(f32[32,768]{1,0:T(8,128)S(1)} %get-tuple-element.11), channel_id=1, source_target_pairs={{0,2},{1,3},{2,0},{4,6},{6,4},{7,5},{8,10},{9,11},{11,9},{13,15},{... | collective-permute-start | bytes 294920 | tf_op jit(solution)/shard_map/ppermute | solution.py:89
  61.6 1.7 %collective-permute-start.13 = (bf16[32,2048]{1,0:T(8,128)(2,1)S(1)}, bf16[32,2048]{1,0:T(8,128)(2,1)S(1)}, u32[]{:S(2)}, u32[]{:S(2)}) collective-permute-start(bf16[32,2048]{1,0:T(8,128)(2,1)S(1)} %collective-permute-done.5), channel_id=1, source_target_pairs={{0,4},{4,12},{12,8},{8,0},{1,5},{5,13},{13,9},{9,1},{2,6},{6,14},{... | collective-permute-start | bytes 393224 | tf_op jit(solution)/shard_map/ppermute | solution.py:54
  64.3 2.2 %collective-permute-done.12 = bf16[32,2048]{1,0:T(8,128)(2,1)S(1)} collective-permute-done((bf16[32,2048]{1,0:T(8,128)(2,1)S(1)}, bf16[32,2048]{1,0:T(8,128)(2,1)S(1)}, u32[]{:S(2)}, u32[]{:S(2)}) %collective-permute-start.12) | collective-permute-done | bytes 131104 | tf_op jit(solution)/shard_map/ppermute | solution.py:54
  67.6 1.8 %collective-permute-done.13 = bf16[32,2048]{1,0:T(8,128)(2,1)S(1)} collective-permute-done((bf16[32,2048]{1,0:T(8,128)(2,1)S(1)}, bf16[32,2048]{1,0:T(8,128)(2,1)S(1)}, u32[]{:S(2)}, u32[]{:S(2)}) %collective-permute-start.13) | collective-permute-done | bytes 131104 | tf_op jit(solution)/shard_map/ppermute | solution.py:54
  71.6 1.7 %fusion.68 = f32[32,768]{1,0:T(8,128)S(1)} fusion(f32[32,768]{1,0:T(8,128)S(1)} %fusion, f32[32,768]{1,0:T(8,128)S(1)} %fusion.8, f32[32,768]{1,0:T(8,128)S(1)} %fusion.16, bf16[32,2048]{1,0:T(8,128)(2,1)S(1)} %collective-permute-done.11, bf16[768,8192]{1,0:T(8,128)(2,1)S(1)} %bitcast.39, f32[]{:T(128)} %fusion.76), kind=kOutput, calls=%fused_computation.44 | convolution fusion | flops 100761600 | bytes 3670020 | tf_op jit(solution)/shard_map/dot_general | solution.py:21
  77.3 1.5 %collective-permute-done.15 = f32[32,768]{1,0:T(8,128)S(1)} collective-permute-done((f32[32,768]{1,0:T(8,128)S(1)}, f32[32,768]{1,0:T(8,128)S(1)}, u32[]{:S(2)}, u32[]{:S(2)}) %collective-permute-start.15) | collective-permute-done | bytes 98336 | tf_op jit(solution)/shard_map/ppermute | solution.py:101
  80.3 1.7 %collective-permute-done.17 = f32[32,768]{1,0:T(8,128)S(1)} collective-permute-done((f32[32,768]{1,0:T(8,128)S(1)}, f32[32,768]{1,0:T(8,128)S(1)}, u32[]{:S(2)}, u32[]{:S(2)}) %collective-permute-start.17) | collective-permute-done | bytes 98336 | tf_op jit(solution)/shard_map/ppermute | solution.py:101
  (44 shorter events, 18.7 us)
Async XLA Ops:
  0.0 18.5 %copy-start = (s32[2]{0:T(128)S(1)}, s32[2]{0:T(128)}, u32[]{:S(2)}) copy-start(s32[2]{0:T(128)} %param.9) | copy-start | bytes 28
  0.0 19.1 %copy-start.1 = (f32[64]{0:T(128)S(1)}, f32[64]{0:T(128)}, u32[]{:S(2)}) copy-start(f32[64]{0:T(128)} %param.8) | copy-start | bytes 772
  2.1 18.4 %collective-permute-start.4 = (bf16[32,2048]{1,0:T(8,128)(2,1)S(1)}, bf16[32,2048]{1,0:T(8,128)(2,1)S(1)}, u32[]{:S(2)}, u32[]{:S(2)}) collective-permute-start(bf16[32,2048]{1,0:T(8,128)(2,1)S(1)} %get-tuple-element.7), channel_id=1, source_target_pairs={{0,4},{4,12},{12,8},{8,0},{1,5},{5,13},{13,9},{9,1},{2,6},{6,14},{... | collective-permute-start | bytes 393224 | tf_op jit(solution)/shard_map/ppermute | solution.py:54
  4.2 20.5 %collective-permute-start.2 = (bf16[32,2048]{1,0:T(8,128)(2,1)S(1)}, bf16[32,2048]{1,0:T(8,128)(2,1)S(1)}, u32[]{:S(2)}, u32[]{:S(2)}) collective-permute-start(bf16[32,2048]{1,0:T(8,128)(2,1)S(1)} %get-tuple-element.8), channel_id=1, source_target_pairs={{0,4},{4,12},{12,8},{8,0},{1,5},{5,13},{13,9},{9,1},{2,6},{6,14},{... | collective-permute-start | bytes 393224 | tf_op jit(solution)/shard_map/ppermute | solution.py:54
  6.6 23.4 %collective-permute-start.6 = (bf16[32,2048]{1,0:T(8,128)(2,1)S(1)}, bf16[32,2048]{1,0:T(8,128)(2,1)S(1)}, u32[]{:S(2)}, u32[]{:S(2)}) collective-permute-start(bf16[32,2048]{1,0:T(8,128)(2,1)S(1)} %get-tuple-element.6), channel_id=1, source_target_pairs={{0,4},{4,12},{12,8},{8,0},{1,5},{5,13},{13,9},{9,1},{2,6},{6,14},{... | collective-permute-start | bytes 393224 | tf_op jit(solution)/shard_map/ppermute | solution.py:54
  6.7 26.5 %collective-permute-start = (bf16[32,2048]{1,0:T(8,128)(2,1)S(1)}, bf16[32,2048]{1,0:T(8,128)(2,1)S(1)}, u32[]{:S(2)}, u32[]{:S(2)}) collective-permute-start(bf16[32,2048]{1,0:T(8,128)(2,1)S(1)} %get-tuple-element.5), channel_id=1, source_target_pairs={{0,4},{4,12},{12,8},{8,0},{1,5},{5,13},{13,9},{9,1},{2,6},{6,14},{... | collective-permute-start | bytes 393224 | tf_op jit(solution)/shard_map/ppermute | solution.py:54
  23.4 40.0 %slice-start = ((s8[12582912]{0:T(1024)(128)(4,1)}), s8[4194304]{0:T(1024)(128)(4,1)S(1)}, s32[]{:S(2)}) async-start(s8[12582912]{0:T(1024)(128)(4,1)} %bitcast.34), calls=%async_computation | async-start | bytes 8388608
  23.4 17.3 %collective-permute-start.5 = (bf16[32,2048]{1,0:T(8,128)(2,1)S(1)}, bf16[32,2048]{1,0:T(8,128)(2,1)S(1)}, u32[]{:S(2)}, u32[]{:S(2)}) collective-permute-start(bf16[32,2048]{1,0:T(8,128)(2,1)S(1)} %collective-permute-done.4), channel_id=1, source_target_pairs={{0,4},{4,12},{12,8},{8,0},{1,5},{5,13},{13,9},{9,1},{2,6},{6,14},{... | collective-permute-start | bytes 393224 | tf_op jit(solution)/shard_map/ppermute | solution.py:54
  27.6 16.1 %collective-permute-start.3 = (bf16[32,2048]{1,0:T(8,128)(2,1)S(1)}, bf16[32,2048]{1,0:T(8,128)(2,1)S(1)}, u32[]{:S(2)}, u32[]{:S(2)}) collective-permute-start(bf16[32,2048]{1,0:T(8,128)(2,1)S(1)} %collective-permute-done.2), channel_id=1, source_target_pairs={{0,4},{4,12},{12,8},{8,0},{1,5},{5,13},{13,9},{9,1},{2,6},{6,14},{... | collective-permute-start | bytes 393224 | tf_op jit(solution)/shard_map/ppermute | solution.py:54
  32.9 30.5 %slice-start.1 = ((s8[12582912]{0:T(1024)(128)(4,1)}), s8[4194304]{0:T(1024)(128)(4,1)S(1)}, s32[]{:S(2)}) async-start(s8[12582912]{0:T(1024)(128)(4,1)} %bitcast.34), calls=%async_computation.1 | async-start | bytes 8388608
  32.9 4.8 %collective-permute-start.7 = (bf16[32,2048]{1,0:T(8,128)(2,1)S(1)}, bf16[32,2048]{1,0:T(8,128)(2,1)S(1)}, u32[]{:S(2)}, u32[]{:S(2)}) collective-permute-start(bf16[32,2048]{1,0:T(8,128)(2,1)S(1)} %collective-permute-done.6), channel_id=1, source_target_pairs={{0,4},{4,12},{12,8},{8,0},{1,5},{5,13},{13,9},{9,1},{2,6},{6,14},{... | collective-permute-start | bytes 393224 | tf_op jit(solution)/shard_map/ppermute | solution.py:54
  33.3 13.4 %collective-permute-start.1 = (bf16[32,2048]{1,0:T(8,128)(2,1)S(1)}, bf16[32,2048]{1,0:T(8,128)(2,1)S(1)}, u32[]{:S(2)}, u32[]{:S(2)}) collective-permute-start(bf16[32,2048]{1,0:T(8,128)(2,1)S(1)} %collective-permute-done), channel_id=1, source_target_pairs={{0,4},{4,12},{12,8},{8,0},{1,5},{5,13},{13,9},{9,1},{2,6},{6,14},{... | collective-permute-start | bytes 393224 | tf_op jit(solution)/shard_map/ppermute | solution.py:54
  40.6 22.8 %slice-start.2 = ((s8[12582912]{0:T(1024)(128)(4,1)}), s8[4194304]{0:T(1024)(128)(4,1)S(1)}, s32[]{:S(2)}) async-start(s8[12582912]{0:T(1024)(128)(4,1)} %bitcast.34), calls=%async_computation.2 | async-start | bytes 8388608
  40.6 21.1 %collective-permute-start.14 = (bf16[32,2048]{1,0:T(8,128)(2,1)S(1)}, bf16[32,2048]{1,0:T(8,128)(2,1)S(1)}, u32[]{:S(2)}, u32[]{:S(2)}) collective-permute-start(bf16[32,2048]{1,0:T(8,128)(2,1)S(1)} %collective-permute-done.7), channel_id=1, source_target_pairs={{0,4},{4,12},{12,8},{8,0},{1,5},{5,13},{13,9},{9,1},{2,6},{6,14},{... | collective-permute-start | bytes 393224 | tf_op jit(solution)/shard_map/ppermute | solution.py:54
  50.3 25.6 %collective-permute-start.10 = (f32[32,768]{1,0:T(8,128)S(1)}, f32[32,768]{1,0:T(8,128)S(1)}, u32[]{:S(2)}, u32[]{:S(2)}) collective-permute-start(f32[32,768]{1,0:T(8,128)S(1)} %get-tuple-element.10), channel_id=1, source_target_pairs={{0,3},{1,0},{3,2},{5,4},{6,5},{7,6},{8,11},{10,9},{11,10},{12,15},... | collective-permute-start | bytes 294920 | tf_op jit(solution)/shard_map/ppermute | solution.py:89
  56.0 21.2 %collective-permute-start.8 = (f32[32,768]{1,0:T(8,128)S(1)}, f32[32,768]{1,0:T(8,128)S(1)}, u32[]{:S(2)}, u32[]{:S(2)}) collective-permute-start(f32[32,768]{1,0:T(8,128)S(1)} %get-tuple-element.9), channel_id=1, source_target_pairs={{1,2},{2,3},{3,0},{4,5},{5,6},{7,4},{8,9},{9,10},{10,11},{12,13},{... | collective-permute-start | bytes 294920 | tf_op jit(solution)/shard_map/ppermute | solution.py:89
  58.4 18.8 %collective-permute-start.9 = (f32[32,768]{1,0:T(8,128)S(1)}, f32[32,768]{1,0:T(8,128)S(1)}, u32[]{:S(2)}, u32[]{:S(2)}) collective-permute-start(f32[32,768]{1,0:T(8,128)S(1)} %get-tuple-element.11), channel_id=1, source_target_pairs={{0,2},{1,3},{2,0},{4,6},{6,4},{7,5},{8,10},{9,11},{11,9},{13,15},{... | collective-permute-start | bytes 294920 | tf_op jit(solution)/shard_map/ppermute | solution.py:89
  61.2 5.3 %collective-permute-start.12 = (bf16[32,2048]{1,0:T(8,128)(2,1)S(1)}, bf16[32,2048]{1,0:T(8,128)(2,1)S(1)}, u32[]{:S(2)}, u32[]{:S(2)}) collective-permute-start(bf16[32,2048]{1,0:T(8,128)(2,1)S(1)} %collective-permute-done.3), channel_id=1, source_target_pairs={{0,4},{4,12},{12,8},{8,0},{1,5},{5,13},{13,9},{9,1},{2,6},{6,14},{... | collective-permute-start | bytes 393224 | tf_op jit(solution)/shard_map/ppermute | solution.py:54
  61.6 7.7 %collective-permute-start.13 = (bf16[32,2048]{1,0:T(8,128)(2,1)S(1)}, bf16[32,2048]{1,0:T(8,128)(2,1)S(1)}, u32[]{:S(2)}, u32[]{:S(2)}) collective-permute-start(bf16[32,2048]{1,0:T(8,128)(2,1)S(1)} %collective-permute-done.5), channel_id=1, source_target_pairs={{0,4},{4,12},{12,8},{8,0},{1,5},{5,13},{13,9},{9,1},{2,6},{6,14},{... | collective-permute-start | bytes 393224 | tf_op jit(solution)/shard_map/ppermute | solution.py:54
  66.6 5.0 %collective-permute-start.11 = (bf16[32,2048]{1,0:T(8,128)(2,1)S(1)}, bf16[32,2048]{1,0:T(8,128)(2,1)S(1)}, u32[]{:S(2)}, u32[]{:S(2)}) collective-permute-start(bf16[32,2048]{1,0:T(8,128)(2,1)S(1)} %collective-permute-done.1), channel_id=1, source_target_pairs={{0,4},{4,12},{12,8},{8,0},{1,5},{5,13},{13,9},{9,1},{2,6},{6,14},{... | collective-permute-start | bytes 393224 | tf_op jit(solution)/shard_map/ppermute | solution.py:54
  73.3 5.5 %collective-permute-start.15 = (f32[32,768]{1,0:T(8,128)S(1)}, f32[32,768]{1,0:T(8,128)S(1)}, u32[]{:S(2)}, u32[]{:S(2)}) collective-permute-start(f32[32,768]{1,0:T(8,128)S(1)} %fusion.68), channel_id=1, source_target_pairs={{0,1},{6,7},{11,8},{13,14},{16,17},{22,23},{27,24},{29,30}} | collective-permute-start | bytes 294920 | tf_op jit(solution)/shard_map/ppermute | solution.py:101
  74.6 5.7 %collective-permute-start.16 = (f32[32,768]{1,0:T(8,128)S(1)}, f32[32,768]{1,0:T(8,128)S(1)}, u32[]{:S(2)}, u32[]{:S(2)}) collective-permute-start(f32[32,768]{1,0:T(8,128)S(1)} %fusion.68), channel_id=1, source_target_pairs={{3,1},{5,7},{10,8},{12,14},{19,17},{21,23},{26,24},{28,30}} | collective-permute-start | bytes 294920 | tf_op jit(solution)/shard_map/ppermute | solution.py:101
  75.9 6.1 %collective-permute-start.17 = (f32[32,768]{1,0:T(8,128)S(1)}, f32[32,768]{1,0:T(8,128)S(1)}, u32[]{:S(2)}, u32[]{:S(2)}) collective-permute-start(f32[32,768]{1,0:T(8,128)S(1)} %fusion.68), channel_id=1, source_target_pairs={{2,1},{4,7},{9,8},{15,14},{18,17},{20,23},{25,24},{31,30}} | collective-permute-start | bytes 294920 | tf_op jit(solution)/shard_map/ppermute | solution.py:101

commit v2 on v0

v2 whole, which is shorter than its diff:
```python
import jax
import jax.numpy as jnp
from jax import lax
from jax.experimental import pallas as pl
from jax.experimental.pallas import tpu as pltpu
from jax.sharding import PartitionSpec as P

CHUNKS = (6, 6, 4)
AXES = ("parts", "shard", "ckpt", "sub")
VMEM = pl.BlockSpec(memory_space=pltpu.VMEM)
SMEM = pl.BlockSpec(memory_space=pltpu.SMEM)
HBM = pl.BlockSpec(memory_space=pltpu.HBM)
ANY = pl.BlockSpec(memory_space=pl.ANY)
PIECES = 4


def line_ring(n):
    odd = list(range(1, n, 2))
    even = list(range(0, n, 2))
    return [0] + odd + even[:0:-1]


def ring_position(z, n):
    return jnp.where(z == 0, 0, jnp.where(z % 2 == 1, (z + 1) // 2, n - z // 2))


def chip_at(p, n):
    return jnp.where(p <= n // 2, jnp.maximum(2 * p - 1, 0), 2 * (n - p))


def call(kernel, name, shapes, specs, args, limit=8, scratch=(), flops=0, aliases=None):
    return pl.pallas_call(
        kernel,
        in_specs=specs,
        out_specs=[VMEM] * len(shapes),
        out_shape=shapes,
        scratch_shapes=scratch,
        input_output_aliases=aliases or {},
        compiler_params=pltpu.CompilerParams(vmem_limit_bytes=limit << 20),
        cost_estimate=pl.CostEstimate(flops=flops, bytes_accessed=0, transcendentals=0),
        name=name,
    )(*args)


def times(rows, train_part):
    return lax.dot_general(
        rows, train_part, (((1,), (1,)), ((), ())), preferred_element_type=jnp.float32
    )


def condition(query, precond, spans):
    rows = query.shape[0]
    count = len(spans)
    first, total = spans[0][0], sum(width for _, width in spans)

    def kernel(query_ref, precond_ref, *refs):
        outs, (held, scale, sems) = refs[:count], refs[count:]
        copies = [pltpu.make_async_copy(precond_ref.at[:, pl.ds(first, total)], scale, sems.at[count])]
        copies += [
            pltpu.make_async_copy(
                query_ref.at[:, pl.ds(start, width)], held.at[:, pl.ds(start - first, width)], sems.at[i]
            )
            for i, (start, width) in enumerate(spans)
        ]
        for copy in copies:
            copy.start()
        copies[0].wait()
        for i, (start, width) in enumerate(spans):
            copies[i + 1].wait()
            at = pl.ds(start - first, width)
            outs[i][...] = (held[:, at] * scale[:, at]).astype(jnp.bfloat16)

    return call(
        kernel,
        "condition",
        [jax.ShapeDtypeStruct((rows, width), jnp.bfloat16) for _, width in spans],
        [HBM, HBM],
        (query, precond),
        scratch=[
            pltpu.VMEM((rows, total), jnp.float32),
            pltpu.VMEM((1, total), jnp.float32),
            pltpu.SemaphoreType.DMA((count + 1,)),
        ],
    )


def fetch(train, span):
    start, width = span
    count = train.shape[0]
    tall = count // PIECES

    def kernel(train_ref, held, sems):
        copies = [
            pltpu.make_async_copy(
                train_ref.at[pl.ds(i * tall, tall), pl.ds(start, width)], held.at[pl.ds(i * tall, tall), :], sems.at[i]
            )
            for i in range(PIECES)
        ]
        for copy in copies:
            copy.start()
        for copy in copies:
            copy.wait()

    return call(
        kernel,
        "fetch",
        [pltpu.VMEM((count, width), train.dtype)],
        [ANY],
        (train,),
        scratch=[pltpu.SemaphoreType.DMA((PIECES,))],
        flops=2 * 512 * width * count,
    )[0]


def rate_row(learn_rates, ckpt_order, columns):
    def kernel(rates_ref, order_ref, row, rates, order, sems):
        copies = [
            pltpu.make_async_copy(rates_ref, rates, sems.at[0]),
            pltpu.make_async_copy(order_ref, order, sems.at[1]),
        ]
        for copy in copies:
            copy.start()
        for copy in copies:
            copy.wait()
        row[...] = jnp.full(row.shape, rates[order[lax.axis_index("ckpt")]], jnp.float32)

    return call(
        kernel,
        "rate_row",
        [jax.ShapeDtypeStruct((1, columns), jnp.float32)],
        [ANY, ANY],
        (learn_rates, ckpt_order),
        scratch=[
            pltpu.SMEM(learn_rates.shape, learn_rates.dtype),
            pltpu.SMEM(ckpt_order.shape, ckpt_order.dtype),
            pltpu.SemaphoreType.DMA((2,)),
        ],
    )[0]


def score(blocks, train, sums, rate, forward):
    count = len(blocks)
    rows, width = blocks[0].shape
    args = [*blocks, train, *(sums or ()), *(() if rate is None else (rate,))]

    def kernel(*refs):
        given, train_ref, before = refs[:count], refs[count], refs[count + 1 : len(args)]
        outs = refs[len(args) :]
        stacked = given[0][...] if count == 1 else jnp.concatenate([ref[...] for ref in given], axis=0)
        scores = times(stacked, train_ref[...])
        for i in range(count):
            total = scores[i * rows : (i + 1) * rows]
            if sums:
                total = before[i][...] + total
            if rate is not None:
                total = total * before[-1][...]
            outs[i][...] = total

    shapes = [jax.ShapeDtypeStruct((rows, train.shape[0]), jnp.float32)] * count
    aliases = {}
    if forward:
        shapes.append(jax.ShapeDtypeStruct(blocks[-1].shape, blocks[-1].dtype))
        aliases[count - 1] = count
    results = call(
        kernel, "score", shapes, [VMEM] * len(args), args, flops=2 * 256 * width * train.shape[0], aliases=aliases
    )
    return list(results[:count]), results[count] if forward else None


def sort_out(sums, shards, groups, after):
    per_group = shards // groups
    rows, columns = sums[0].shape

    def kernel(after_ref, *refs):
        given, outs = refs[: len(sums)], refs[len(sums) :]
        my_place = ring_position(lax.axis_index("shard"), shards)
        my_group = lax.axis_index("ckpt") * lax.axis_size("sub") + lax.axis_index("sub")
        for d in range(groups):
            out = outs[1 - d % 2]
            for k in range(per_group):
                chip = (my_group ^ d) * per_group + k
                step = (my_place - ring_position(chip, shards) + shards) % shards
                at = pl.ds((d // 2 * per_group + k) * rows, rows)

                @pl.when(step == shards - 1)
                def _():
                    out[at, :] = jnp.zeros((rows, columns), jnp.float32)

                for s, ref in enumerate(given):

                    @pl.when(step == s)
                    def _():
                        out[at, :] = ref[...]

    shape = jax.ShapeDtypeStruct((groups // 2 * per_group * rows, columns), jnp.float32)
    return call(kernel, "sort_out", [shape] * 2, [ANY] + [VMEM] * len(sums), (after, *sums))


def fold(kept, received, tall):
    pieces = kept.shape[0] // tall

    def kernel(kept_ref, received_ref, *outs):
        if pieces == 1:
            outs[0][...] = kept_ref[...] + received_ref[...]
            return
        for i in range(pieces):
            at = pl.ds(i * tall, tall)
            outs[1 - i % 2][pl.ds(i // 2 * tall, tall), :] = kept_ref[at, :] + received_ref[at, :]

    shapes = [jax.ShapeDtypeStruct((max(pieces // 2, 1) * tall, kept.shape[1]), jnp.float32)] * min(pieces, 2)
    return call(kernel, "fold", shapes, [VMEM] * 2, (kept, received))


def finish(result, last, received, shards, groups):
    per_group = shards // groups
    rows = last.shape[0]

    def kernel(result_ref, last_ref, received_ref, out):
        my_place = ring_position(lax.axis_index("shard"), shards)
        my_group = lax.axis_index("ckpt") * lax.axis_size("sub") + lax.axis_index("sub")
        last_chip = chip_at((my_place + 1) % shards, shards)
        mine = last_chip // per_group == my_group
        out[...] = result_ref[...]

        @pl.when(mine)
        def _():
            at = pl.ds(pl.multiple_of(last_chip % per_group * rows, rows), rows) if per_group > 1 else slice(None)
            out[at, :] += last_ref[...] + received_ref[...]

    return call(
        kernel,
        "finish",
        [jax.ShapeDtypeStruct(result.shape, jnp.float32)],
        [VMEM] * 3,
        (result, last, received),
    )[0]


def per_device(sizes, train_grads, query_grads, precond, learn_rates, ckpt_order):
    train_local = train_grads[0]
    query_local = query_grads[0]
    parts, shards, ckpts, subs = sizes
    groups = ckpts * subs
    per_group = shards // groups
    ring = line_ring(shards)
    place = {z: i for i, z in enumerate(ring)}
    hops = [(ring[i], ring[(i + 1) % shards]) for i in range(shards)]

    unit = query_local.shape[1] // sum(CHUNKS)
    spans = [(unit * sum(CHUNKS[:j]), unit * c) for j, c in enumerate(CHUNKS)]
    query_local = pltpu.with_memory_space_constraint(query_local, pltpu.HBM)
    precond = pltpu.with_memory_space_constraint(precond, pltpu.HBM)
    train_local = pltpu.with_memory_space_constraint(train_local, pltpu.HBM)
    own = condition(query_local, precond, spans[:1]) + condition(query_local, precond, spans[1:])
    held = [fetch(train_local, span) for span in spans]
    rate = rate_row(
        pltpu.with_memory_space_constraint(learn_rates, pltpu.HBM),
        pltpu.with_memory_space_constraint(ckpt_order, pltpu.HBM),
        train_local.shape[0],
    )

    sums = []
    current = own
    for step in range(1, shards):
        current = [lax.ppermute(block, "shard", hops) for block in current]
        if step == shards - 1:
            sent, kept = sort_out(sums, shards, groups, current[0])
        total = None
        for j in range(len(CHUNKS)):
            total, current[j] = score(
                [own[j], current[j]] if step == 1 else [current[j]],
                held[j],
                total,
                rate if j == len(CHUNKS) - 1 else None,
                step < shards - 1,
            )
        sums += total

    def last_of(z):
        return ring[(place[z] + 1) % shards]

    def device(p, z, g):
        return ((p * shards + z) * ckpts + g // subs) * subs + g % subs

    def pairs(d, keep):
        return [
            (device(p, z, g), device(p, z, g ^ d))
            for p in range(parts)
            for z in range(shards)
            for g in range(groups)
            if keep(z, g ^ d)
        ]

    distances = [1 << i for i in range(groups.bit_length() - 1)]
    tall = kept.shape[0] // (groups // 2)
    for d in distances:
        received = lax.ppermute(sent, AXES, pairs(d, lambda z, g: True))
        *more, kept = fold(kept, received, tall)
        sent = more[0] if more else None

    last = sums[-1]
    for d in distances:
        received = lax.ppermute(
            last,
            AXES,
            pairs(d, lambda z, g: (last_of(z) // per_group ^ g) & (2 * d - 1) == 0),
        )
        if d < groups // 2:
            last = fold(last, received, last.shape[0])[0]
    return finish(kept, last, received, shards, groups)


def solution(mesh):
    sizes = tuple(mesh.shape[a] for a in AXES)

    def run(*args):
        return per_device(sizes, *args)

    return jax.shard_map(
        run,
        mesh=mesh,
        in_specs=(
            P("ckpt", ("parts", "shard"), "sub"),
            P("ckpt", ("parts", "shard"), "sub"),
            P("ckpt", "sub"),
            P(),
            P(),
        ),
        out_specs=P(("ckpt", "sub"), ("parts", "shard")),
        check_vma=False,
    )
```

time: 144 us -> 52.3 us (0.36); the launches traced: 141 us -> 52.1 us
  waiting for transfers between devices: 112 us -> 7.99 us
  Pallas kernels: 0 us -> 22.4 us
  starting transfers between devices: 0.04 us -> 21.5 us
  between operations: 13.4 us -> 0.16 us
  matrix products: 11.4 us -> 0 us
  other arithmetic: 3.19 us -> 0 us
  local copies, waits for them, and re-layouts: 1.54 us -> 0 us
    all_gather x1 -> x0, waiting for transfers between devices: 81.3 us -> none  [per_device(): lax.all_gather(query_local, 'shard', axis=0, tiled=True) * precond]
    psum x1 -> x0, waiting for transfers between devices: 29.7 us -> none  [per_device(): totals = lax.psum(weighted, ('ckpt', 'sub'))]
    pallas_call x0 -> x20, Pallas kernels: none -> 22.4 us  [call(): pl.pallas_call(kernel, in_specs=specs, out_specs=[VMEM] * len(shapes), ou...]
    ppermute x0 -> x13, starting transfers between devices: none -> 21.5 us  [the longest x9 11.3 us: per_device(): current = [lax.ppermute(block, 'shard', hops) for block in current]]
    dot_general x1 -> x0, matrix products: 11.4 us -> none  [score_rows(): lax.dot_general(block_rows, train_local, (((1,), (1,)), ((), ())), prefer...]
    ppermute x0 -> x13, waiting for transfers between devices: none -> 7.99 us  [the longest x2 4.28 us: per_device(): lax.ppermute(last, AXES, pairs(d, lambda z, g: (last_of(z) // per_group ^...]
    reduce_sum x2 -> x0, other arithmetic: 3.19 us -> none  [the longest x1 1.9 us: per_device(): step_rate = jnp.sum(jnp.where(table_steps == number, learn_rates, 0.0))]
    dynamic_slice x1 -> x0, local copies, waits for them, and re-layouts: 1.54 us -> none  [per_device(): lax.dynamic_slice_in_dim(totals, lax.axis_index(('ckpt', 'sub')) * share,...]
  transfers between devices with their start and end apart: 2 -> 13, of which waited for: 2 -> 5; matrix products, arithmetic and copies ran while one was open for 2% -> 0% of each run, Pallas kernels for 0% -> 40%
where the time goes in v2:
time: 52.3 us; the launch traced here: 52.1 us
  Pallas kernels  22.4 us (43%)
  starting transfers between devices  21.5 us (41%)
  waiting for transfers between devices  7.99 us (15%)
    pallas_call x20, Pallas kernels, call(): pl.pallas_call(kernel, in_specs=specs, out_specs=[VMEM] * len(shapes), ou...  22.4 us
    ppermute x9, starting transfers between devices, per_device(): current = [lax.ppermute(block, 'shard', hops) for block in current]  11.3 us
    ppermute x2, starting transfers between devices, per_device(): received = lax.ppermute(sent, AXES, pairs(d, lambda z, g: True))  7.63 us
    ppermute x2, waiting for transfers between devices, per_device(): lax.ppermute(last, AXES, pairs(d, lambda z, g: (last_of(z) // per_group ^...  4.28 us
    ppermute x9, waiting for transfers between devices, per_device(): current = [lax.ppermute(block, 'shard', hops) for block in current]  3.35 us
    ppermute x2, starting transfers between devices, per_device(): lax.ppermute(last, AXES, pairs(d, lambda z, g: (last_of(z) // per_group ^...  2.58 us
  transfers between devices with their start and end apart: 13, of which 5 were waited for; matrix products, arithmetic and copies ran while one was open for 0% of the time, Pallas kernels for 40%

profile of v2, /device:TPU:1, one launch (start us, length us, event | category | flops | bytes accessed | tf_op | source)
XLA Modules:
  0.0 52.1 jit_solution(14502136112189202950)
XLA Ops:
  0.0 1.1 %condition.2.refs_0_ = bf16[32,3072]{1,0:T(8,128)(2,1)S(1)} custom-call(f32[32,8192]{1,0:T(8,128)} %bitcast.5, f32[1,8192]{1,0:T(1,128)} %precond_ref.3), custom_call_target="tpu_custom_call" | custom-call | tf_op jit(solution)/shard_map/condition/pallas_call | solution.py:32
  1.1 2.2 %collective-permute-start = (bf16[32,3072]{1,0:T(8,128)(2,1)S(1)}, bf16[32,3072]{1,0:T(8,128)(2,1)S(1)}, u32[]{:S(2)}, u32[]{:S(2)}) collective-permute-start(bf16[32,3072]{1,0:T(8,128)(2,1)S(1)} %condition.2.refs_0_), channel_id=1, source_target_pairs={{0,4},{4,12},{12,8},{8,0},{1,5},{5,13},{13,9},{9,1},{2,6},{6,14},{... | collective-permute-start | bytes 589832 | tf_op jit(solution)/shard_map/ppermute | solution.py:265
  3.2 1.1 %condition.3 = (bf16[32,3072]{1,0:T(8,128)(2,1)S(1)}, bf16[32,2048]{1,0:T(8,128)(2,1)S(1)}) custom-call(f32[32,8192]{1,0:T(8,128)} %bitcast.6, f32[1,8192]{1,0:T(1,128)} %precond_ref.3), custom_call_target="tpu_custom_call" | custom-call | tf_op jit(solution)/shard_map/condition/pallas_call | solution.py:32
  4.4 2.4 %collective-permute-start.4 = (bf16[32,3072]{1,0:T(8,128)(2,1)S(1)}, bf16[32,3072]{1,0:T(8,128)(2,1)S(1)}, u32[]{:S(2)}, u32[]{:S(2)}) collective-permute-start(bf16[32,3072]{1,0:T(8,128)(2,1)S(1)} %get-tuple-element.29.refs_0_), channel_id=1, source_target_pairs={{0,4},{4,12},{12,8},{8,0},{1,5},{5,13},{13,9},{9,1},{2,6},{6,14},{... | collective-permute-start | bytes 589832 | tf_op jit(solution)/shard_map/ppermute | solution.py:265
  6.9 2.4 %fetch.3.refs_2_.refs_1_ = bf16[768,3072]{1,0:T(8,128)(2,1)S(1)} custom-call(bf16[768,8192]{1,0:T(8,128)(2,1)} %bitcast.2), custom_call_target="tpu_custom_call" | custom-call | flops 2415919104 | tf_op jit(solution)/shard_map/fetch/pallas_call | solution.py:32
  9.3 2.4 %fetch.5.refs_2_.refs_1_ = bf16[768,3072]{1,0:T(8,128)(2,1)S(1)} custom-call(bf16[768,8192]{1,0:T(8,128)(2,1)} %bitcast.3), custom_call_target="tpu_custom_call" | custom-call | flops 2415919104 | tf_op jit(solution)/shard_map/fetch/pallas_call | solution.py:32
  11.7 1.5 %score.9 = (f32[32,768]{1,0:T(8,128)S(1)}, f32[32,768]{1,0:T(8,128)S(1)}, bf16[32,3072]{1,0:T(8,128)(2,1)S(1)}) custom-call(bf16[32,3072]{1,0:T(8,128)(2,1)S(1)} %condition.2.refs_0_, bf16[32,3072]{1,0:T(8,128)(2,1)S(1)} %collective-permute-done.refs_1_, bf16[768,3072]{1,0:T(8,128)(2,1)S(1)} %fetch.3.refs_2_.refs_1_), custom_call_target="tpu_custom_call", output_to_operand_aliasing={{2}: (1, {})} | custom-call | flops 1207959552 | tf_op jit(solution)/shard_map/score/pallas_call | solution.py:32
  13.2 1.5 %score.11 = (f32[32,768]{1,0:T(8,128)S(1)}, f32[32,768]{1,0:T(8,128)S(1)}, bf16[32,3072]{1,0:T(8,128)(2,1)S(1)}) custom-call(bf16[32,3072]{1,0:T(8,128)(2,1)S(1)} %get-tuple-element.29.refs_0_, bf16[32,3072]{1,0:T(8,128)(2,1)S(1)} %collective-permute-done.4.refs_1_, bf16[768,3072]{1,0:T(8,128)(2,1)S(1)} %fetch.5.refs_2_.refs_1_, ...), custom_call_target="tpu_custom_call", output_to_operand_aliasing={{2}: (1, {})} | custom-call | flops 1207959552 | tf_op jit(solution)/shard_map/score/pallas_call | solution.py:32
  15.2 2.8 %collective-permute-start.1 = (bf16[32,3072]{1,0:T(8,128)(2,1)S(1)}, bf16[32,3072]{1,0:T(8,128)(2,1)S(1)}, u32[]{:S(2)}, u32[]{:S(2)}) collective-permute-start(bf16[32,3072]{1,0:T(8,128)(2,1)S(1)} %get-tuple-element.26), channel_id=1, source_target_pairs={{0,4},{4,12},{12,8},{8,0},{1,5},{5,13},{13,9},{9,1},{2,6},{6,14},{... | collective-permute-start | bytes 589832 | tf_op jit(solution)/shard_map/ppermute | solution.py:265
  18.0 1.9 %fetch.4.refs_2_.refs_1_ = bf16[768,2048]{1,0:T(8,128)(2,1)S(1)} custom-call(bf16[768,8192]{1,0:T(8,128)(2,1)} %bitcast.4), custom_call_target="tpu_custom_call" | custom-call | flops 1610612736 | tf_op jit(solution)/shard_map/fetch/pallas_call | solution.py:32
  20.6 1.1 %score.12 = (f32[32,768]{1,0:T(8,128)S(1)}, f32[32,768]{1,0:T(8,128)S(1)}, bf16[32,2048]{1,0:T(8,128)(2,1)S(1)}) custom-call(bf16[32,2048]{1,0:T(8,128)(2,1)S(1)} %get-tuple-element.28.refs_0_, bf16[32,2048]{1,0:T(8,128)(2,1)S(1)} %collective-permute-done.3.refs_1_, bf16[768,2048]{1,0:T(8,128)(2,1)S(1)} %fetch.4.refs_2_.refs_1_, ...), custom_call_target="tpu_custom_call", output_to_operand_aliasing={{2}: (1, {})} | custom-call | flops 805306368 | tf_op jit(solution)/shard_map/score/pallas_call | solution.py:32
  22.2 2.2 %collective-permute-done.1.refs_0_ = bf16[32,3072]{1,0:T(8,128)(2,1)S(1)} collective-permute-done((bf16[32,3072]{1,0:T(8,128)(2,1)S(1)}, bf16[32,3072]{1,0:T(8,128)(2,1)S(1)}, u32[]{:S(2)}, u32[]{:S(2)}) %collective-permute-start.1) | collective-permute-done | bytes 196640 | tf_op jit(solution)/shard_map/ppermute | solution.py:265
  24.4 1.4 %score.10 = (f32[32,768]{1,0:T(8,128)S(1)}, bf16[32,3072]{1,0:T(8,128)(2,1)S(1)}) custom-call(bf16[32,3072]{1,0:T(8,128)(2,1)S(1)} %collective-permute-done.1.refs_0_, bf16[768,3072]{1,0:T(8,128)(2,1)S(1)} %fetch.3.refs_2_.refs_1_), custom_call_target="tpu_custom_call", output_to_operand_aliasing={{1}: (0, {})} | custom-call | flops 1207959552 | tf_op jit(solution)/shard_map/score/pallas_call | solution.py:32
  26.4 1.4 %score.13 = (f32[32,768]{1,0:T(8,128)S(1)}, bf16[32,3072]{1,0:T(8,128)(2,1)S(1)}) custom-call(bf16[32,3072]{1,0:T(8,128)(2,1)S(1)} %collective-permute-done.6.refs_0_, bf16[768,3072]{1,0:T(8,128)(2,1)S(1)} %fetch.5.refs_2_.refs_1_, f32[32,768]{1,0:T(8,128)S(1)} %get-tuple-element.38.refs_2_), custom_call_target="tpu_custom_call", output_to_operand_aliasing={{1}: (0, {})} | custom-call | flops 1207959552 | tf_op jit(solution)/shard_map/score/pallas_call | solution.py:32
  27.8 2.0 %collective-permute-start.10 = (bf16[32,3072]{1,0:T(8,128)(2,1)S(1)}, bf16[32,3072]{1,0:T(8,128)(2,1)S(1)}, u32[]{:S(2)}, u32[]{:S(2)}) collective-permute-start(bf16[32,3072]{1,0:T(8,128)(2,1)S(1)} %get-tuple-element.46), channel_id=1, source_target_pairs={{0,4},{4,12},{12,8},{8,0},{1,5},{5,13},{13,9},{9,1},{2,6},{6,14},{... | collective-permute-start | bytes 589832 | tf_op jit(solution)/shard_map/ppermute | solution.py:265
  31.2 1.1 %collective-permute-done.2.after_ref.refs_0_ = bf16[32,3072]{1,0:T(8,128)(2,1)S(1)} collective-permute-done((bf16[32,3072]{1,0:T(8,128)(2,1)S(1)}, bf16[32,3072]{1,0:T(8,128)(2,1)S(1)}, u32[]{:S(2)}, u32[]{:S(2)}) %collective-permute-start.2) | collective-permute-done | bytes 196640 | tf_op jit(solution)/shard_map/ppermute | solution.py:265
  32.4 6.4 %collective-permute-start.7 = (f32[64,768]{1,0:T(8,128)S(1)}, f32[64,768]{1,0:T(8,128)S(1)}, u32[]{:S(2)}, u32[]{:S(2)}) collective-permute-start(f32[64,768]{1,0:T(8,128)S(1)} %get-tuple-element.42), channel_id=1, source_target_pairs={{0,1},{1,0},{2,3},{3,2},{4,5},{5,4},{6,7},{7,6},{8,9},{9,8},{10,11... | collective-permute-start | bytes 589832 | tf_op jit(solution)/shard_map/ppermute | solution.py:297
  38.8 1.4 %score.15.refs_2_ = f32[32,768]{1,0:T(8,128)S(1)} custom-call(bf16[32,3072]{1,0:T(8,128)(2,1)S(1)} %collective-permute-done.2.after_ref.refs_0_, bf16[768,3072]{1,0:T(8,128)(2,1)S(1)} %fetch.3.refs_2_.refs_1_), custom_call_target="tpu_custom_call" | custom-call | flops 1207959552 | tf_op jit(solution)/shard_map/score/pallas_call | solution.py:32
  40.2 1.5 %score.16.refs_2_ = f32[32,768]{1,0:T(8,128)S(1)} custom-call(bf16[32,3072]{1,0:T(8,128)(2,1)S(1)} %collective-permute-done.10.refs_0_, bf16[768,3072]{1,0:T(8,128)(2,1)S(1)} %fetch.5.refs_2_.refs_1_, f32[32,768]{1,0:T(8,128)S(1)} %score.15.refs_2_), custom_call_target="tpu_custom_call" | custom-call | flops 1207959552 | tf_op jit(solution)/shard_map/score/pallas_call | solution.py:32
  41.8 1.0 %score.17.kept_ref = f32[32,768]{1,0:T(8,128)S(1)} custom-call(bf16[32,2048]{1,0:T(8,128)(2,1)S(1)} %collective-permute-done.9.refs_0_, bf16[768,2048]{1,0:T(8,128)(2,1)S(1)} %fetch.4.refs_2_.refs_1_, f32[32,768]{1,0:T(8,128)S(1)} %score.16.refs_2_, f32[1,768]{1,0:T(1,128)S(1)} %rate_row.1.refs_5_.refs_3_), custom_call_target="tpu_custom_call" | custom-call | flops 805306368 | tf_op jit(solution)/shard_map/score/pallas_call | solution.py:32
  42.8 1.3 %collective-permute-start.11 = (f32[32,768]{1,0:T(8,128)S(1)}, f32[32,768]{1,0:T(8,128)S(1)}, u32[]{:S(2)}, u32[]{:S(2)}) collective-permute-start(f32[32,768]{1,0:T(8,128)S(1)} %score.17.kept_ref), channel_id=1, source_target_pairs={{0,1},{2,3},{4,5},{6,7},{9,8},{11,10},{13,12},{15,14},{16,17},{18,... | collective-permute-start | bytes 294920 | tf_op jit(solution)/shard_map/ppermute | solution.py:303
  44.1 1.3 %collective-permute-start.8 = (f32[32,768]{1,0:T(8,128)S(1)}, f32[32,768]{1,0:T(8,128)S(1)}, u32[]{:S(2)}, u32[]{:S(2)}) collective-permute-start(f32[32,768]{1,0:T(8,128)S(1)} %get-tuple-element.44), channel_id=1, source_target_pairs={{0,2},{1,3},{2,0},{3,1},{4,6},{5,7},{6,4},{7,5},{8,10},{9,11},{10,... | collective-permute-start | bytes 294920 | tf_op jit(solution)/shard_map/ppermute | solution.py:297
  46.0 1.3 %collective-permute-start.12 = (f32[32,768]{1,0:T(8,128)S(1)}, f32[32,768]{1,0:T(8,128)S(1)}, u32[]{:S(2)}, u32[]{:S(2)}) collective-permute-start(f32[32,768]{1,0:T(8,128)S(1)} %fold.5.last_ref), channel_id=1, source_target_pairs={{3,1},{5,7},{10,8},{12,14},{19,17},{21,23},{26,24},{28,30}} | collective-permute-start | bytes 294920 | tf_op jit(solution)/shard_map/ppermute | solution.py:303
  47.7 3.7 %collective-permute-done.12.received_ref = f32[32,768]{1,0:T(8,128)S(1)} collective-permute-done((f32[32,768]{1,0:T(8,128)S(1)}, f32[32,768]{1,0:T(8,128)S(1)}, u32[]{:S(2)}, u32[]{:S(2)}) %collective-permute-start.12) | collective-permute-done | bytes 98336 | tf_op jit(solution)/shard_map/ppermute | solution.py:303
  (22 shorter events, 5.6 us)
Async XLA Ops:
  1.1 10.6 %collective-permute-start = (bf16[32,3072]{1,0:T(8,128)(2,1)S(1)}, bf16[32,3072]{1,0:T(8,128)(2,1)S(1)}, u32[]{:S(2)}, u32[]{:S(2)}) collective-permute-start(bf16[32,3072]{1,0:T(8,128)(2,1)S(1)} %condition.2.refs_0_), channel_id=1, source_target_pairs={{0,4},{4,12},{12,8},{8,0},{1,5},{5,13},{13,9},{9,1},{2,6},{6,14},{... | collective-permute-start | bytes 589832 | tf_op jit(solution)/shard_map/ppermute | solution.py:265
  4.4 8.8 %collective-permute-start.4 = (bf16[32,3072]{1,0:T(8,128)(2,1)S(1)}, bf16[32,3072]{1,0:T(8,128)(2,1)S(1)}, u32[]{:S(2)}, u32[]{:S(2)}) collective-permute-start(bf16[32,3072]{1,0:T(8,128)(2,1)S(1)} %get-tuple-element.29.refs_0_), channel_id=1, source_target_pairs={{0,4},{4,12},{12,8},{8,0},{1,5},{5,13},{13,9},{9,1},{2,6},{6,14},{... | collective-permute-start | bytes 589832 | tf_op jit(solution)/shard_map/ppermute | solution.py:265
  6.7 13.9 %collective-permute-start.3 = (bf16[32,2048]{1,0:T(8,128)(2,1)S(1)}, bf16[32,2048]{1,0:T(8,128)(2,1)S(1)}, u32[]{:S(2)}, u32[]{:S(2)}) collective-permute-start(bf16[32,2048]{1,0:T(8,128)(2,1)S(1)} %get-tuple-element.28.refs_0_), channel_id=1, source_target_pairs={{0,4},{4,12},{12,8},{8,0},{1,5},{5,13},{13,9},{9,1},{2,6},{6,14},{... | collective-permute-start | bytes 393224 | tf_op jit(solution)/shard_map/ppermute | solution.py:265
  14.8 11.6 %collective-permute-start.6 = (bf16[32,3072]{1,0:T(8,128)(2,1)S(1)}, bf16[32,3072]{1,0:T(8,128)(2,1)S(1)}, u32[]{:S(2)}, u32[]{:S(2)}) collective-permute-start(bf16[32,3072]{1,0:T(8,128)(2,1)S(1)} %get-tuple-element.37), channel_id=1, source_target_pairs={{0,4},{4,12},{12,8},{8,0},{1,5},{5,13},{13,9},{9,1},{2,6},{6,14},{... | collective-permute-start | bytes 589832 | tf_op jit(solution)/shard_map/ppermute | solution.py:265
  15.2 9.2 %collective-permute-start.1 = (bf16[32,3072]{1,0:T(8,128)(2,1)S(1)}, bf16[32,3072]{1,0:T(8,128)(2,1)S(1)}, u32[]{:S(2)}, u32[]{:S(2)}) collective-permute-start(bf16[32,3072]{1,0:T(8,128)(2,1)S(1)} %get-tuple-element.26), channel_id=1, source_target_pairs={{0,4},{4,12},{12,8},{8,0},{1,5},{5,13},{13,9},{9,1},{2,6},{6,14},{... | collective-permute-start | bytes 589832 | tf_op jit(solution)/shard_map/ppermute | solution.py:265
  21.7 8.1 %collective-permute-start.5 = (bf16[32,2048]{1,0:T(8,128)(2,1)S(1)}, bf16[32,2048]{1,0:T(8,128)(2,1)S(1)}, u32[]{:S(2)}, u32[]{:S(2)}) collective-permute-start(bf16[32,2048]{1,0:T(8,128)(2,1)S(1)} %get-tuple-element.36), channel_id=1, source_target_pairs={{0,4},{4,12},{12,8},{8,0},{1,5},{5,13},{13,9},{9,1},{2,6},{6,14},{... | collective-permute-start | bytes 393224 | tf_op jit(solution)/shard_map/ppermute | solution.py:265
  25.8 6.5 %collective-permute-start.2 = (bf16[32,3072]{1,0:T(8,128)(2,1)S(1)}, bf16[32,3072]{1,0:T(8,128)(2,1)S(1)}, u32[]{:S(2)}, u32[]{:S(2)}) collective-permute-start(bf16[32,3072]{1,0:T(8,128)(2,1)S(1)} %get-tuple-element.27), channel_id=1, source_target_pairs={{0,4},{4,12},{12,8},{8,0},{1,5},{5,13},{13,9},{9,1},{2,6},{6,14},{... | collective-permute-start | bytes 589832 | tf_op jit(solution)/shard_map/ppermute | solution.py:265
  27.8 12.4 %collective-permute-start.10 = (bf16[32,3072]{1,0:T(8,128)(2,1)S(1)}, bf16[32,3072]{1,0:T(8,128)(2,1)S(1)}, u32[]{:S(2)}, u32[]{:S(2)}) collective-permute-start(bf16[32,3072]{1,0:T(8,128)(2,1)S(1)} %get-tuple-element.46), channel_id=1, source_target_pairs={{0,4},{4,12},{12,8},{8,0},{1,5},{5,13},{13,9},{9,1},{2,6},{6,14},{... | collective-permute-start | bytes 589832 | tf_op jit(solution)/shard_map/ppermute | solution.py:265
  30.8 10.9 %collective-permute-start.9 = (bf16[32,2048]{1,0:T(8,128)(2,1)S(1)}, bf16[32,2048]{1,0:T(8,128)(2,1)S(1)}, u32[]{:S(2)}, u32[]{:S(2)}) collective-permute-start(bf16[32,2048]{1,0:T(8,128)(2,1)S(1)} %get-tuple-element.45), channel_id=1, source_target_pairs={{0,4},{4,12},{12,8},{8,0},{1,5},{5,13},{13,9},{9,1},{2,6},{6,14},{... | collective-permute-start | bytes 393224 | tf_op jit(solution)/shard_map/ppermute | solution.py:265
  32.4 11.7 %collective-permute-start.7 = (f32[64,768]{1,0:T(8,128)S(1)}, f32[64,768]{1,0:T(8,128)S(1)}, u32[]{:S(2)}, u32[]{:S(2)}) collective-permute-start(f32[64,768]{1,0:T(8,128)S(1)} %get-tuple-element.42), channel_id=1, source_target_pairs={{0,1},{1,0},{2,3},{3,2},{4,5},{5,4},{6,7},{7,6},{8,9},{9,8},{10,11... | collective-permute-start | bytes 589832 | tf_op jit(solution)/shard_map/ppermute | solution.py:297
  42.8 3.2 %collective-permute-start.11 = (f32[32,768]{1,0:T(8,128)S(1)}, f32[32,768]{1,0:T(8,128)S(1)}, u32[]{:S(2)}, u32[]{:S(2)}) collective-permute-start(f32[32,768]{1,0:T(8,128)S(1)} %score.17.kept_ref), channel_id=1, source_target_pairs={{0,1},{2,3},{4,5},{6,7},{9,8},{11,10},{13,12},{15,14},{16,17},{18,... | collective-permute-start | bytes 294920 | tf_op jit(solution)/shard_map/ppermute | solution.py:303
  44.1 3.5 %collective-permute-start.8 = (f32[32,768]{1,0:T(8,128)S(1)}, f32[32,768]{1,0:T(8,128)S(1)}, u32[]{:S(2)}, u32[]{:S(2)}) collective-permute-start(f32[32,768]{1,0:T(8,128)S(1)} %get-tuple-element.44), channel_id=1, source_target_pairs={{0,2},{1,3},{2,0},{3,1},{4,6},{5,7},{6,4},{7,5},{8,10},{9,11},{10,... | collective-permute-start | bytes 294920 | tf_op jit(solution)/shard_map/ppermute | solution.py:297
  46.0 5.4 %collective-permute-start.12 = (f32[32,768]{1,0:T(8,128)S(1)}, f32[32,768]{1,0:T(8,128)S(1)}, u32[]{:S(2)}, u32[]{:S(2)}) collective-permute-start(f32[32,768]{1,0:T(8,128)S(1)} %fold.5.last_ref), channel_id=1, source_target_pairs={{3,1},{5,7},{10,8},{12,14},{19,17},{21,23},{26,24},{28,30}} | collective-permute-start | bytes 294920 | tf_op jit(solution)/shard_map/ppermute | solution.py:303

commit v3 on v2

v3 whole, which is shorter than its diff:
```python
import jax
import jax.numpy as jnp
from jax import lax
from jax.experimental import pallas as pl
from jax.experimental.pallas import tpu as pltpu
from jax.sharding import PartitionSpec as P

CHUNKS = (6, 6, 4)
QUARTERS = (4, 4, 4, 4)
VMEM = pl.BlockSpec(memory_space=pltpu.VMEM)
SMEM = pl.BlockSpec(memory_space=pltpu.SMEM)
HBM = pl.BlockSpec(memory_space=pltpu.HBM)
ANY = pl.BlockSpec(memory_space=pl.ANY)
PIECES = 4
SCALE = 0.1


def line_ring(n):
    odd = list(range(1, n, 2))
    even = list(range(0, n, 2))
    return [0] + odd + even[:0:-1]


def ring_position(z, n):
    return jnp.where(z == 0, 0, jnp.where(z % 2 == 1, (z + 1) // 2, n - z // 2))


def call(kernel, name, shapes, specs, args, limit=8, scratch=(), flops=0, aliases=None, after=()):
    args = (*args, *after)
    specs = [*specs, *[ANY] * len(after)]
    count = len(args) - len(after)

    def body(*refs):
        kernel(*refs[:count], *refs[len(args) :])

    return pl.pallas_call(
        body,
        in_specs=specs,
        out_specs=[VMEM] * len(shapes),
        out_shape=shapes,
        scratch_shapes=scratch,
        input_output_aliases=aliases or {},
        compiler_params=pltpu.CompilerParams(vmem_limit_bytes=limit << 20),
        cost_estimate=pl.CostEstimate(flops=int(SCALE * flops), bytes_accessed=0, transcendentals=0),
        name=name,
    )(*args)


def times(rows, train_part):
    return lax.dot_general(
        rows, train_part, (((1,), (1,)), ((), ())), preferred_element_type=jnp.float32
    )


def condition(query, precond, spans, after=()):
    rows = query.shape[0]
    count = len(spans)
    first, total = spans[0][0], sum(width for _, width in spans)

    def kernel(query_ref, precond_ref, *refs):
        outs, (held, scale, sems) = refs[:count], refs[count:]
        copies = [pltpu.make_async_copy(precond_ref.at[:, pl.ds(first, total)], scale, sems.at[count])]
        copies += [
            pltpu.make_async_copy(
                query_ref.at[:, pl.ds(start, width)], held.at[:, pl.ds(start - first, width)], sems.at[i]
            )
            for i, (start, width) in enumerate(spans)
        ]
        for copy in copies:
            copy.start()
        copies[0].wait()
        for i, (start, width) in enumerate(spans):
            copies[i + 1].wait()
            at = pl.ds(start - first, width)
            outs[i][...] = (held[:, at] * scale[:, at]).astype(jnp.bfloat16)

    return call(
        kernel,
        "condition",
        [jax.ShapeDtypeStruct((rows, width), jnp.bfloat16) for _, width in spans],
        [HBM, HBM],
        (query, precond),
        scratch=[
            pltpu.VMEM((rows, total), jnp.float32),
            pltpu.VMEM((1, total), jnp.float32),
            pltpu.SemaphoreType.DMA((count + 1,)),
        ],
        after=after,
    )


def fetch(train, spans, after):
    count = train.shape[0]
    tall = count // PIECES

    def kernel(train_ref, *refs):
        outs, sems = refs[:-1], refs[-1]
        copies = [
            pltpu.make_async_copy(
                train_ref.at[pl.ds(i * tall, tall), pl.ds(start, width)],
                out.at[pl.ds(i * tall, tall), :],
                sems.at[k, i],
            )
            for k, (out, (start, width)) in enumerate(zip(outs, spans))
            for i in range(PIECES)
        ]
        for copy in copies:
            copy.start()
        for copy in copies:
            copy.wait()

    return call(
        kernel,
        "fetch",
        [pltpu.VMEM((count, width), train.dtype) for _, width in spans],
        [ANY],
        (train,),
        scratch=[pltpu.SemaphoreType.DMA((len(spans), PIECES))],
        flops=2 * 512 * sum(width for _, width in spans) * count,
        after=after,
    )


def rate_row(learn_rates, ckpt_order, columns, after):
    def kernel(rates_ref, order_ref, row, rates, order, sems):
        copies = [
            pltpu.make_async_copy(rates_ref, rates, sems.at[0]),
            pltpu.make_async_copy(order_ref, order, sems.at[1]),
        ]
        for copy in copies:
            copy.start()
        for copy in copies:
            copy.wait()
        row[...] = jnp.full(row.shape, rates[order[lax.axis_index("ckpt")]], jnp.float32)

    return call(
        kernel,
        "rate_row",
        [jax.ShapeDtypeStruct((1, columns), jnp.float32)],
        [ANY, ANY],
        (learn_rates, ckpt_order),
        scratch=[
            pltpu.SMEM(learn_rates.shape, learn_rates.dtype),
            pltpu.SMEM(ckpt_order.shape, ckpt_order.dtype),
            pltpu.SemaphoreType.DMA((2,)),
        ],
        after=after,
    )[0]


def score(blocks, train, sums, forward=False, carry=None, after=()):
    count = len(blocks)
    rows, width = blocks[0].shape
    args = [*blocks, train, *(sums or ())]
    specs = [VMEM] * len(args)

    def kernel(*refs):
        given, train_ref, before = refs[:count], refs[count], refs[count + 1 : len(args)]
        outs = refs[-count:] if carry is None else refs[-count - 1 : -1]
        outs = outs if not forward else refs[-count - 1 : -1]
        stacked = given[0][...] if count == 1 else jnp.concatenate([ref[...] for ref in given], axis=0)
        scores = times(stacked, train_ref[...])
        for i in range(count):
            total = scores[i * rows : (i + 1) * rows]
            if sums:
                total = before[i][...] + total
            outs[i][...] = total

    shapes = [jax.ShapeDtypeStruct((rows, train.shape[0]), jnp.float32)] * count
    aliases = {}
    if forward:
        shapes.append(jax.ShapeDtypeStruct(blocks[-1].shape, blocks[-1].dtype))
        aliases[count - 1] = count
    elif carry is not None:
        shapes.append(jax.ShapeDtypeStruct(carry.shape, carry.dtype))
        aliases[len(args)] = count
        args.append(carry)
        specs.append(ANY)
    results = call(
        kernel,
        "score",
        shapes,
        specs,
        args,
        flops=2 * 256 * width * train.shape[0],
        aliases=aliases,
        after=after,
    )
    return list(results[:count]), results[count] if len(shapes) > count else None


def sort_out(sums, rate, shards, groups):
    per_group = shards // groups
    rows, columns = sums[0].shape

    def kernel(*refs):
        given, rate_ref, outs = refs[: len(sums)], refs[len(sums)], refs[len(sums) + 1 :]
        my_place = ring_position(lax.axis_index("shard"), shards)
        my_group = lax.axis_index("ckpt") * lax.axis_size("sub") + lax.axis_index("sub")
        for d in range(groups):
            for k in range(per_group):
                chip = (my_group ^ d) * per_group + k
                step = (my_place - ring_position(chip, shards) + shards) % shards
                at = pl.ds((d // 2 * per_group + k) * rows, rows)
                for s, ref in enumerate(given):

                    @pl.when(step == s)
                    def _():
                        outs[1 - d % 2][at, :] = ref[...] * rate_ref[...]

    shape = jax.ShapeDtypeStruct((groups // 2 * per_group * rows, columns), jnp.float32)
    return call(kernel, "sort_out", [shape] * 2, [VMEM] * (len(sums) + 1), (*sums, rate))


def fold(kept, received, tall):
    pieces = kept.shape[0] // tall

    def kernel(kept_ref, received_ref, *outs):
        if pieces == 1:
            outs[0][...] = kept_ref[...] + received_ref[...]
            return
        for i in range(pieces):
            at = pl.ds(i * tall, tall)
            outs[1 - i % 2][pl.ds(i // 2 * tall, tall), :] = kept_ref[at, :] + received_ref[at, :]

    shapes = [jax.ShapeDtypeStruct((max(pieces // 2, 1) * tall, kept.shape[1]), jnp.float32)] * min(pieces, 2)
    return call(kernel, "fold", shapes, [VMEM] * 2, (kept, received))


def my_pair():
    z = lax.axis_index("shard")
    return z // 2 == lax.axis_index("ckpt"), z % 2 == lax.axis_index("sub")


def score_and_deal(own, far, train, sums, after):
    rows, width = own.shape
    args = [own, far, train, *(sums or ())]

    def kernel(own_ref, far_ref, train_ref, *refs):
        before, (own_sums, far_sums, first, second) = refs[:-4], refs[-4:]
        scores = times(jnp.concatenate([own_ref[...], far_ref[...]], axis=0), train_ref[...])
        for i, out in enumerate((own_sums, far_sums)):
            part = scores[i * rows : (i + 1) * rows]
            out[...] = before[i][...] + part if sums else part
        home, _ = my_pair()

        @pl.when(home)
        def _():
            first[...] = far_ref[...]
            second[...] = own_ref[...]

        @pl.when(jnp.logical_not(home))
        def _():
            first[...] = own_ref[...]
            second[...] = far_ref[...]

    scores = jax.ShapeDtypeStruct((rows, train.shape[0]), jnp.float32)
    block = jax.ShapeDtypeStruct(own.shape, own.dtype)
    return call(
        kernel,
        "score_and_deal",
        [scores, scores, block, block],
        [VMEM] * len(args),
        args,
        flops=2 * 256 * width * train.shape[0],
        after=after,
    )


def score_picked(block, train, if_home, if_not, carry=None, after=()):
    rows, width = block.shape
    args = [block, train, if_home, if_not]

    def kernel(block_ref, train_ref, home_ref, not_ref, *refs):
        out = refs[0] if carry is None else refs[1]
        part = times(block_ref[...], train_ref[...])
        home, _ = my_pair()

        @pl.when(home)
        def _():
            out[...] = home_ref[...] + part

        @pl.when(jnp.logical_not(home))
        def _():
            out[...] = not_ref[...] + part

    scores = jax.ShapeDtypeStruct((rows, train.shape[0]), jnp.float32)
    flops = 2 * 256 * width * train.shape[0]
    if carry is None:
        return call(kernel, "score_picked", [scores], [VMEM] * 4, args, flops=flops, after=after)[0]
    return call(
        kernel,
        "score_picked",
        [scores, jax.ShapeDtypeStruct(carry.shape, carry.dtype)],
        [VMEM] * 4 + [ANY],
        [*args, carry],
        flops=flops,
        after=after,
        aliases={4: 1},
    )


def part_pair(if_home, if_not, other, rate, after=()):
    def kernel(home_ref, not_ref, other_ref, rate_ref, sent, kept):
        home, agree = my_pair()
        for one, ref in ((home, home_ref), (jnp.logical_not(home), not_ref)):

            @pl.when(jnp.logical_and(one, agree))
            def _():
                kept[...] = ref[...] * rate_ref[...]
                sent[...] = other_ref[...] * rate_ref[...]

            @pl.when(jnp.logical_and(one, jnp.logical_not(agree)))
            def _():
                sent[...] = ref[...] * rate_ref[...]
                kept[...] = other_ref[...] * rate_ref[...]

    shape = jax.ShapeDtypeStruct(other.shape, jnp.float32)
    return call(kernel, "part_pair", [shape] * 2, [VMEM] * 4, (if_home, if_not, other, rate), after=after)


def add(*arrays):
    def kernel(*refs):
        total = refs[0][...]
        for ref in refs[1:-1]:
            total = total + ref[...]
        refs[-1][...] = total

    shape = jax.ShapeDtypeStruct(arrays[0].shape, jnp.float32)
    return call(kernel, "add", [shape], [VMEM] * len(arrays), arrays)[0]


def in_pairs(train, query, precond, learn_rates, ckpt_order):
    def swap(array, axis, distance):
        size = lax.axis_size(axis)
        return lax.ppermute(array, axis, [(i, i ^ distance) for i in range(size)])

    unit = query.shape[1] // sum(QUARTERS)
    spans = [(unit * sum(QUARTERS[:j]), unit * c) for j, c in enumerate(QUARTERS)]

    own1 = condition(query, precond, spans[:1])[0]
    one1, two1 = swap(own1, "shard", 1), swap(own1, "shard", 2)
    own2 = condition(query, precond, spans[1:2], [own1])[0]
    one2, two2 = swap(own2, "shard", 1), swap(own2, "shard", 2)
    train1, train2 = fetch(train, spans[:2], [own2])
    totals, two1 = score([own1, one1, two1], train1, None, forward=True)
    three1 = swap(two1, "shard", 1)
    own3, own4 = condition(query, precond, spans[2:], totals[:1])
    two3 = swap(own3, "shard", 2)
    totals, two2 = score([own2, one2, two2], train2, totals, forward=True, after=[own3])
    three2 = swap(two2, "shard", 1)
    own_sums, one_sums, two_sums = totals
    two4 = swap(own4, "shard", 2)
    train3, train4 = fetch(train, spans[2:], totals[:1])
    (three_sums,), _ = score([three1], train1, None, after=[train3])

    own_sums, two_sums, first3, second3 = score_and_deal(own3, two3, train3, [own_sums, two_sums], [three_sums])
    first3 = swap(first3, "shard", 1)
    own_sums, two_sums, first4, second4 = score_and_deal(own4, two4, train4, [own_sums, two_sums], [])
    first4 = swap(first4, "shard", 1)
    (three_sums,), second3 = score([three2], train2, [three_sums], carry=second3, after=[own_sums])
    second3 = swap(second3, "shard", 1)
    rate = rate_row(learn_rates, ckpt_order, train.shape[0], [three_sums])
    first_sums, second4 = score_picked(first3, train3, three_sums, one_sums, second4, [rate])
    second4 = swap(second4, "shard", 1)
    first_sums = score_picked(first4, train4, first_sums, first_sums)

    sent, kept = part_pair(two_sums, own_sums, first_sums, rate)
    across = add(kept, swap(sent, "sub", 1))
    from_far = swap(across, "ckpt", 1)
    second_sums = score_picked(second3, train3, one_sums, three_sums, after=[across])
    second_sums = score_picked(second4, train4, second_sums, second_sums)
    sent, kept = part_pair(own_sums, two_sums, second_sums, rate)
    return add(kept, from_far, swap(sent, "sub", 1))


def in_ring(sizes, train_local, query_local, precond, learn_rates, ckpt_order):
    shards, groups = sizes[0], sizes[1] * sizes[2]
    ring = line_ring(shards)
    hops = [(ring[i], ring[(i + 1) % shards]) for i in range(shards)]

    unit = query_local.shape[1] // sum(CHUNKS)
    spans = [(unit * sum(CHUNKS[:j]), unit * c) for j, c in enumerate(CHUNKS)]
    own = condition(query_local, precond, spans[:1])
    held = fetch(train_local, spans[:1], own)
    for span in spans[1:]:
        own += condition(query_local, precond, [span], [held[0], own[-1]])

    sums = []
    current = own
    for step in range(1, shards):
        current = [lax.ppermute(block, "shard", hops) for block in current]
        total = None
        for j in range(len(CHUNKS)):
            if j >= len(held):
                held += fetch(train_local, spans[j : j + 1], total[:1])
            total, current[j] = score(
                [own[j], current[j]] if step == 1 else [current[j]], held[j], total, step < shards - 1
            )
        sums += total
    rate = rate_row(learn_rates, ckpt_order, train_local.shape[0], sums[:1])

    sent, kept = sort_out(sums, rate, shards, groups)
    tall = kept.shape[0] // (groups // 2)
    for i in range(groups.bit_length() - 1):
        received = lax.ppermute(sent, ("ckpt", "sub"), [(g, g ^ 1 << i) for g in range(groups)])
        *more, kept = fold(kept, received, tall)
        sent = more[0] if more else None
    return kept


def per_device(sizes, train_grads, query_grads, precond, learn_rates, ckpt_order):
    args = [train_grads[0], query_grads[0], precond, learn_rates, ckpt_order]
    args = [pltpu.with_memory_space_constraint(array, pltpu.HBM) for array in args]
    return in_pairs(*args) if sizes == (4, 2, 2) else in_ring(sizes, *args)


def solution(mesh):
    sizes = tuple(mesh.shape[axis] for axis in ("shard", "ckpt", "sub"))

    def run(*args):
        return per_device(sizes, *args)

    return jax.shard_map(
        run,
        mesh=mesh,
        in_specs=(
            P("ckpt", ("parts", "shard"), "sub"),
            P("ckpt", ("parts", "shard"), "sub"),
            P("ckpt", "sub"),
            P(),
            P(),
        ),
        out_specs=P(("ckpt", "sub"), ("parts", "shard")),
        check_vma=False,
    )
```

time: 52.3 us -> 46.3 us (0.89)
  waiting for transfers between devices: 7.99 us -> 4.88 us
  Pallas kernels: 22.4 us -> 20.7 us
  starting transfers between devices: 21.5 us -> 19.9 us
    ppermute x13 -> x15, waiting for transfers between devices: 7.99 us -> 4.88 us  [swap(): return lax.ppermute(array, axis, [(i, i ^ distance) for i in range(size)])]
    ppermute x13 -> x15, starting transfers between devices: 21.5 us -> 19.9 us  [swap(): return lax.ppermute(array, axis, [(i, i ^ distance) for i in range(size)])]
    pallas_call x20, Pallas kernels: 22.4 us -> 20.7 us  [call(): pl.pallas_call(body, in_specs=specs, out_specs=[VMEM] * len(shapes), out_...]
  transfers between devices with their start and end apart: 13 -> 15, of which waited for: 5 -> 3; matrix products, arithmetic and copies ran while one was open for 0% -> 0% of each run, Pallas kernels for 40% -> 42%
where the time goes in v3:
time: 46.3 us; the launch traced here: 45.6 us
  Pallas kernels  20.7 us (45%)
  starting transfers between devices  19.9 us (43%)
  waiting for transfers between devices  4.88 us (11%)
    pallas_call x20, Pallas kernels, call(): pl.pallas_call(body, in_specs=specs, out_specs=[VMEM] * len(shapes), out_...  20.7 us
    ppermute x15, starting transfers between devices, swap(): return lax.ppermute(array, axis, [(i, i ^ distance) for i in range(size)])  19.9 us
    ppermute x15, waiting for transfers between devices, swap(): return lax.ppermute(array, axis, [(i, i ^ distance) for i in range(size)])  4.88 us
  transfers between devices with their start and end apart: 15, of which 3 were waited for; matrix products, arithmetic and copies ran while one was open for 0% of the time, Pallas kernels for 42%

profile of v3, /device:TPU:1, one launch (start us, length us, event | category | flops | bytes accessed | tf_op | source)
XLA Modules:
  0.0 45.6 jit_solution(16856963391532041911)
XLA Ops:
  0.0 1.0 %condition.3.refs_2_.refs_0_ = bf16[32,2048]{1,0:T(8,128)(2,1)S(1)} custom-call(f32[32,8192]{1,0:T(8,128)} %bitcast.4, f32[1,8192]{1,0:T(1,128)} %refs_1_.6), custom_call_target="tpu_custom_call" | custom-call | tf_op jit(solution)/shard_map/condition/pallas_call | solution.py:36
  1.0 2.2 %collective-permute-start = (bf16[32,2048]{1,0:T(8,128)(2,1)S(1)}, bf16[32,2048]{1,0:T(8,128)(2,1)S(1)}, u32[]{:S(2)}, u32[]{:S(2)}) collective-permute-start(bf16[32,2048]{1,0:T(8,128)(2,1)S(1)} %condition.3.refs_2_.refs_0_), channel_id=1, source_target_pairs={{0,4},{4,0},{8,12},{12,8},{1,5},{5,1},{9,13},{13,9},{2,6},{6,2},{1... | collective-permute-start | bytes 393224 | tf_op jit(solution)/shard_map/ppermute | solution.py:336
  3.2 2.3 %collective-permute-start.1 = (bf16[32,2048]{1,0:T(8,128)(2,1)S(1)}, bf16[32,2048]{1,0:T(8,128)(2,1)S(1)}, u32[]{:S(2)}, u32[]{:S(2)}) collective-permute-start(bf16[32,2048]{1,0:T(8,128)(2,1)S(1)} %condition.3.refs_2_.refs_0_), channel_id=1, source_target_pairs={{0,8},{4,12},{8,0},{12,4},{1,9},{5,13},{9,1},{13,5},{2,10},{6,14},... | collective-permute-start | bytes 393224 | tf_op jit(solution)/shard_map/ppermute | solution.py:336
  5.5 1.0 %condition.4.refs_1_.refs_0_ = bf16[32,2048]{1,0:T(8,128)(2,1)S(1)} custom-call(f32[32,8192]{1,0:T(8,128)} %bitcast.5, f32[1,8192]{1,0:T(1,128)} %refs_1_.6, bf16[32,2048]{1,0:T(8,128)(2,1)S(1)} %condition.3.refs_2_.refs_0_), custom_call_target="tpu_custom_call" | custom-call | tf_op jit(solution)/shard_map/condition/pallas_call | solution.py:36
  6.8 2.9 %fetch.2 = (bf16[768,2048]{1,0:T(8,128)(2,1)S(1)}, bf16[768,2048]{1,0:T(8,128)(2,1)S(1)}) custom-call(bf16[768,8192]{1,0:T(8,128)(2,1)} %bitcast.2, bf16[32,2048]{1,0:T(8,128)(2,1)S(1)} %condition.4.refs_1_.refs_0_), custom_call_target="tpu_custom_call" | custom-call | flops 322122560 | tf_op jit(solution)/shard_map/fetch/pallas_call | solution.py:36
  9.7 1.1 %score.4 = (f32[32,768]{1,0:T(8,128)S(1)}, f32[32,768]{1,0:T(8,128)S(1)}, f32[32,768]{1,0:T(8,128)S(1)}, bf16[32,2048]{1,0:T(8,128)(2,1)S(1)}) custom-call(bf16[32,2048]{1,0:T(8,128)(2,1)S(1)} %condition.3.refs_2_.refs_0_, bf16[32,2048]{1,0:T(8,128)(2,1)S(1)} %collective-permute-done.refs_1_, ...), custom_call_target="tpu_custom_call", output_to_operand_aliasing={{3}: (2, {})} | custom-call | flops 80530640 | tf_op jit(solution)/shard_map/score/pallas_call | solution.py:36
  10.7 1.8 %collective-permute-start.6 = (bf16[32,2048]{1,0:T(8,128)(2,1)S(1)}, bf16[32,2048]{1,0:T(8,128)(2,1)S(1)}, u32[]{:S(2)}, u32[]{:S(2)}) collective-permute-start(bf16[32,2048]{1,0:T(8,128)(2,1)S(1)} %get-tuple-element.46), channel_id=1, source_target_pairs={{0,4},{4,0},{8,12},{12,8},{1,5},{5,1},{9,13},{13,9},{2,6},{6,2},{1... | collective-permute-start | bytes 393224 | tf_op jit(solution)/shard_map/ppermute | solution.py:336
  12.5 1.1 %condition.5 = (bf16[32,2048]{1,0:T(8,128)(2,1)S(1)}, bf16[32,2048]{1,0:T(8,128)(2,1)S(1)}) custom-call(f32[32,8192]{1,0:T(8,128)} %bitcast.6, f32[1,8192]{1,0:T(1,128)} %refs_1_.6, f32[32,768]{1,0:T(8,128)S(1)} %get-tuple-element.36.refs_2_.refs_4_), custom_call_target="tpu_custom_call" | custom-call | tf_op jit(solution)/shard_map/condition/pallas_call | solution.py:36
  13.6 2.0 %collective-permute-start.5 = (bf16[32,2048]{1,0:T(8,128)(2,1)S(1)}, bf16[32,2048]{1,0:T(8,128)(2,1)S(1)}, u32[]{:S(2)}, u32[]{:S(2)}) collective-permute-start(bf16[32,2048]{1,0:T(8,128)(2,1)S(1)} %get-tuple-element.41.refs_7_.refs_0_), channel_id=1, source_target_pairs={{0,8},{4,12},{8,0},{12,4},{1,9},{5,13},{9,1},{13,5},{2,10},{6,14},... | collective-permute-start | bytes 393224 | tf_op jit(solution)/shard_map/ppermute | solution.py:336
  16.1 1.1 %score.5 = (f32[32,768]{1,0:T(8,128)S(1)}, f32[32,768]{1,0:T(8,128)S(1)}, f32[32,768]{1,0:T(8,128)S(1)}, bf16[32,2048]{1,0:T(8,128)(2,1)S(1)}) custom-call(bf16[32,2048]{1,0:T(8,128)(2,1)S(1)} %condition.4.refs_1_.refs_0_, bf16[32,2048]{1,0:T(8,128)(2,1)S(1)} %collective-permute-done.3.refs_1_, ...), custom_call_target="tpu_custom_call", output_to_operand_aliasing={{3}: (2, {})} | custom-call | flops 80530640 | tf_op jit(solution)/shard_map/score/pallas_call | solution.py:36
  17.2 1.0 %collective-permute-start.8 = (bf16[32,2048]{1,0:T(8,128)(2,1)S(1)}, bf16[32,2048]{1,0:T(8,128)(2,1)S(1)}, u32[]{:S(2)}, u32[]{:S(2)}) collective-permute-start(bf16[32,2048]{1,0:T(8,128)(2,1)S(1)} %get-tuple-element.52), channel_id=1, source_target_pairs={{0,4},{4,0},{8,12},{12,8},{1,5},{5,1},{9,13},{13,9},{2,6},{6,2},{1... | collective-permute-start | bytes 393224 | tf_op jit(solution)/shard_map/ppermute | solution.py:336
  18.2 2.9 %fetch.3 = (bf16[768,2048]{1,0:T(8,128)(2,1)S(1)}, bf16[768,2048]{1,0:T(8,128)(2,1)S(1)}) custom-call(bf16[768,8192]{1,0:T(8,128)(2,1)} %bitcast.3, f32[32,768]{1,0:T(8,128)S(1)} %get-tuple-element.42.refs_1_.refs_3_), custom_call_target="tpu_custom_call" | custom-call | flops 322122560 | tf_op jit(solution)/shard_map/fetch/pallas_call | solution.py:36
  21.1 1.0 %score.6.refs_5_.refs_2_ = f32[32,768]{1,0:T(8,128)S(1)} custom-call(bf16[32,2048]{1,0:T(8,128)(2,1)S(1)} %collective-permute-done.6.refs_0_, bf16[768,2048]{1,0:T(8,128)(2,1)S(1)} %get-tuple-element.35.refs_3_.refs_1_, bf16[768,2048]{1,0:T(8,128)(2,1)S(1)} %get-tuple-element.44.refs_2_.refs_1_), custom_call_target="tpu_custom_call" | custom-call | flops 80530640 | tf_op jit(solution)/shard_map/score/pallas_call | solution.py:36
  22.1 1.1 %score_and_deal.2 = (f32[32,768]{1,0:T(8,128)S(1)}, f32[32,768]{1,0:T(8,128)S(1)}, bf16[32,2048]{1,0:T(8,128)(2,1)S(1)}, bf16[32,2048]{1,0:T(8,128)(2,1)S(1)}) custom-call(bf16[32,2048]{1,0:T(8,128)(2,1)S(1)} %get-tuple-element.41.refs_7_.refs_0_, bf16[32,2048]{1,0:T(8,128)(2,1)S(1)} %collective-permute-done.5.refs_1_, ...), custom_call_target="tpu_custom_call" | custom-call | flops 80530640 | tf_op jit(solution)/shard_map/score_and_deal/pallas_call | solution.py:36
  23.8 2.9 %collective-permute-done.2.refs_1_ = bf16[32,2048]{1,0:T(8,128)(2,1)S(1)} collective-permute-done((bf16[32,2048]{1,0:T(8,128)(2,1)S(1)}, bf16[32,2048]{1,0:T(8,128)(2,1)S(1)}, u32[]{:S(2)}, u32[]{:S(2)}) %collective-permute-start.2) | collective-permute-done | bytes 131104 | tf_op jit(solution)/shard_map/ppermute | solution.py:336
  26.7 1.1 %score_and_deal.3 = (f32[32,768]{1,0:T(8,128)S(1)}, f32[32,768]{1,0:T(8,128)S(1)}, bf16[32,2048]{1,0:T(8,128)(2,1)S(1)}, bf16[32,2048]{1,0:T(8,128)(2,1)S(1)}) custom-call(bf16[32,2048]{1,0:T(8,128)(2,1)S(1)} %get-tuple-element.37.refs_0_, bf16[32,2048]{1,0:T(8,128)(2,1)S(1)} %collective-permute-done.2.refs_1_, ...), custom_call_target="tpu_custom_call" | custom-call | flops 80530640 | tf_op jit(solution)/shard_map/score_and_deal/pallas_call | solution.py:36
  28.0 1.0 %score.7 = (f32[32,768]{1,0:T(8,128)S(1)}, bf16[32,2048]{1,0:T(8,128)(2,1)S(1)}) custom-call(bf16[32,2048]{1,0:T(8,128)(2,1)S(1)} %collective-permute-done.8.refs_0_, bf16[768,2048]{1,0:T(8,128)(2,1)S(1)} %get-tuple-element.38.refs_3_.refs_1_, f32[32,768]{1,0:T(8,128)S(1)} %score.6.refs_5_.refs_2_, ...), custom_call_target="tpu_custom_call", output_to_operand_aliasing={{1}: (3, {})} | custom-call | flops 80530640 | tf_op jit(solution)/shard_map/score/pallas_call | solution.py:36
  29.1 1.4 %collective-permute-start.10 = (bf16[32,2048]{1,0:T(8,128)(2,1)S(1)}, bf16[32,2048]{1,0:T(8,128)(2,1)S(1)}, u32[]{:S(2)}, u32[]{:S(2)}) collective-permute-start(bf16[32,2048]{1,0:T(8,128)(2,1)S(1)} %get-tuple-element.58), channel_id=1, source_target_pairs={{0,4},{4,0},{8,12},{12,8},{1,5},{5,1},{9,13},{13,9},{2,6},{6,2},{1... | collective-permute-start | bytes 393224 | tf_op jit(solution)/shard_map/ppermute | solution.py:336
  31.2 1.0 %score_picked.4 = (f32[32,768]{1,0:T(8,128)S(1)}, bf16[32,2048]{1,0:T(8,128)(2,1)S(1)}) custom-call(bf16[32,2048]{1,0:T(8,128)(2,1)S(1)} %collective-permute-done.7.refs_0_, bf16[768,2048]{1,0:T(8,128)(2,1)S(1)} %get-tuple-element.44.refs_2_.refs_1_, f32[32,768]{1,0:T(8,128)S(1)} %get-tuple-element.54.refs_2_.refs_3_, ...), custom_call_target="tpu_custom_call", output_to_operand_aliasing={{1}: (4, {})} | custom-call | flops 80530640 | tf_op jit(solution)/shard_map/score_picked/pallas_call | solution.py:36
  32.4 1.0 %score_picked.5.refs_2_ = f32[32,768]{1,0:T(8,128)S(1)} custom-call(bf16[32,2048]{1,0:T(8,128)(2,1)S(1)} %collective-permute-done.11.refs_0_, bf16[768,2048]{1,0:T(8,128)(2,1)S(1)} %get-tuple-element.43.refs_2_.refs_1_, f32[32,768]{1,0:T(8,128)S(1)} %get-tuple-element.60.refs_2_.refs_3_, f32[32,768]{1,0:T(8,128)S(1)} %get-tuple-element.60.refs_2_.refs_3_), custom_call_target="tpu_custom_call" | custom-call | flops 80530640 | tf_op jit(solution)/shard_map/score_picked/pallas_call | solution.py:36
  33.4 5.5 %collective-permute-start.12 = (f32[32,768]{1,0:T(8,128)S(1)}, f32[32,768]{1,0:T(8,128)S(1)}, u32[]{:S(2)}, u32[]{:S(2)}) collective-permute-start(f32[32,768]{1,0:T(8,128)S(1)} %get-tuple-element.62), channel_id=1, source_target_pairs={{0,1},{1,0},{2,3},{3,2},{4,5},{5,4},{6,7},{7,6},{8,9},{9,8},{10,11... | collective-permute-start | bytes 294920 | tf_op jit(solution)/shard_map/ppermute | solution.py:336
  39.9 1.3 %collective-permute-start.13 = (f32[32,768]{1,0:T(8,128)S(1)}, f32[32,768]{1,0:T(8,128)S(1)}, u32[]{:S(2)}, u32[]{:S(2)}) collective-permute-start(f32[32,768]{1,0:T(8,128)S(1)} %add.2.refs_4_), channel_id=1, source_target_pairs={{0,2},{2,0},{1,3},{3,1},{4,6},{6,4},{5,7},{7,5},{8,10},{10,8},{9,1... | collective-permute-start | bytes 294920 | tf_op jit(solution)/shard_map/ppermute | solution.py:336
  41.2 1.0 %score_picked.6.refs_2_.refs_3_ = f32[32,768]{1,0:T(8,128)S(1)} custom-call(bf16[32,2048]{1,0:T(8,128)(2,1)S(1)} %collective-permute-done.10.refs_0_, bf16[768,2048]{1,0:T(8,128)(2,1)S(1)} %get-tuple-element.44.refs_2_.refs_1_, f32[32,768]{1,0:T(8,128)S(1)} %get-tuple-element.55.refs_3_.refs_2_, f32[32,768]{1,0:T(8,128)S(1)} %get-tuple-element.54.refs_2_.refs_3_, ...), custom_call_target="tpu_custom_call" | custom-call | flops 80530640 | tf_op jit(solution)/shard_map/score_picked/pallas_call | solution.py:36
  42.2 1.0 %score_picked.7.refs_2_ = f32[32,768]{1,0:T(8,128)S(1)} custom-call(bf16[32,2048]{1,0:T(8,128)(2,1)S(1)} %collective-permute-done.9.refs_0_, bf16[768,2048]{1,0:T(8,128)(2,1)S(1)} %get-tuple-element.43.refs_2_.refs_1_, f32[32,768]{1,0:T(8,128)S(1)} %score_picked.6.refs_2_.refs_3_, f32[32,768]{1,0:T(8,128)S(1)} %score_picked.6.refs_2_.refs_3_), custom_call_target="tpu_custom_call" | custom-call | flops 80530640 | tf_op jit(solution)/shard_map/score_picked/pallas_call | solution.py:36
  (26 shorter events, 5.8 us)
Async XLA Ops:
  1.0 8.6 %collective-permute-start = (bf16[32,2048]{1,0:T(8,128)(2,1)S(1)}, bf16[32,2048]{1,0:T(8,128)(2,1)S(1)}, u32[]{:S(2)}, u32[]{:S(2)}) collective-permute-start(bf16[32,2048]{1,0:T(8,128)(2,1)S(1)} %condition.3.refs_2_.refs_0_), channel_id=1, source_target_pairs={{0,4},{4,0},{8,12},{12,8},{1,5},{5,1},{9,13},{13,9},{2,6},{6,2},{1... | collective-permute-start | bytes 393224 | tf_op jit(solution)/shard_map/ppermute | solution.py:336
  3.2 6.4 %collective-permute-start.1 = (bf16[32,2048]{1,0:T(8,128)(2,1)S(1)}, bf16[32,2048]{1,0:T(8,128)(2,1)S(1)}, u32[]{:S(2)}, u32[]{:S(2)}) collective-permute-start(bf16[32,2048]{1,0:T(8,128)(2,1)S(1)} %condition.3.refs_2_.refs_0_), channel_id=1, source_target_pairs={{0,8},{4,12},{8,0},{12,4},{1,9},{5,13},{9,1},{13,5},{2,10},{6,14},... | collective-permute-start | bytes 393224 | tf_op jit(solution)/shard_map/ppermute | solution.py:336
  6.5 9.6 %collective-permute-start.3 = (bf16[32,2048]{1,0:T(8,128)(2,1)S(1)}, bf16[32,2048]{1,0:T(8,128)(2,1)S(1)}, u32[]{:S(2)}, u32[]{:S(2)}) collective-permute-start(bf16[32,2048]{1,0:T(8,128)(2,1)S(1)} %condition.4.refs_1_.refs_0_), channel_id=1, source_target_pairs={{0,4},{4,0},{8,12},{12,8},{1,5},{5,1},{9,13},{13,9},{2,6},{6,2},{1... | collective-permute-start | bytes 393224 | tf_op jit(solution)/shard_map/ppermute | solution.py:336
  6.8 9.3 %collective-permute-start.4 = (bf16[32,2048]{1,0:T(8,128)(2,1)S(1)}, bf16[32,2048]{1,0:T(8,128)(2,1)S(1)}, u32[]{:S(2)}, u32[]{:S(2)}) collective-permute-start(bf16[32,2048]{1,0:T(8,128)(2,1)S(1)} %condition.4.refs_1_.refs_0_), channel_id=1, source_target_pairs={{0,8},{4,12},{8,0},{12,4},{1,9},{5,13},{9,1},{13,5},{2,10},{6,14},... | collective-permute-start | bytes 393224 | tf_op jit(solution)/shard_map/ppermute | solution.py:336
  10.7 10.3 %collective-permute-start.6 = (bf16[32,2048]{1,0:T(8,128)(2,1)S(1)}, bf16[32,2048]{1,0:T(8,128)(2,1)S(1)}, u32[]{:S(2)}, u32[]{:S(2)}) collective-permute-start(bf16[32,2048]{1,0:T(8,128)(2,1)S(1)} %get-tuple-element.46), channel_id=1, source_target_pairs={{0,4},{4,0},{8,12},{12,8},{1,5},{5,1},{9,13},{13,9},{2,6},{6,2},{1... | collective-permute-start | bytes 393224 | tf_op jit(solution)/shard_map/ppermute | solution.py:336
  13.6 8.4 %collective-permute-start.5 = (bf16[32,2048]{1,0:T(8,128)(2,1)S(1)}, bf16[32,2048]{1,0:T(8,128)(2,1)S(1)}, u32[]{:S(2)}, u32[]{:S(2)}) collective-permute-start(bf16[32,2048]{1,0:T(8,128)(2,1)S(1)} %get-tuple-element.41.refs_7_.refs_0_), channel_id=1, source_target_pairs={{0,8},{4,12},{8,0},{12,4},{1,9},{5,13},{9,1},{13,5},{2,10},{6,14},... | collective-permute-start | bytes 393224 | tf_op jit(solution)/shard_map/ppermute | solution.py:336
  15.6 11.1 %collective-permute-start.2 = (bf16[32,2048]{1,0:T(8,128)(2,1)S(1)}, bf16[32,2048]{1,0:T(8,128)(2,1)S(1)}, u32[]{:S(2)}, u32[]{:S(2)}) collective-permute-start(bf16[32,2048]{1,0:T(8,128)(2,1)S(1)} %get-tuple-element.37.refs_0_), channel_id=1, source_target_pairs={{0,8},{4,12},{8,0},{12,4},{1,9},{5,13},{9,1},{13,5},{2,10},{6,14},... | collective-permute-start | bytes 393224 | tf_op jit(solution)/shard_map/ppermute | solution.py:336
  17.2 10.9 %collective-permute-start.8 = (bf16[32,2048]{1,0:T(8,128)(2,1)S(1)}, bf16[32,2048]{1,0:T(8,128)(2,1)S(1)}, u32[]{:S(2)}, u32[]{:S(2)}) collective-permute-start(bf16[32,2048]{1,0:T(8,128)(2,1)S(1)} %get-tuple-element.52), channel_id=1, source_target_pairs={{0,4},{4,0},{8,12},{12,8},{1,5},{5,1},{9,13},{13,9},{2,6},{6,2},{1... | collective-permute-start | bytes 393224 | tf_op jit(solution)/shard_map/ppermute | solution.py:336
  23.2 8.0 %collective-permute-start.7 = (bf16[32,2048]{1,0:T(8,128)(2,1)S(1)}, bf16[32,2048]{1,0:T(8,128)(2,1)S(1)}, u32[]{:S(2)}, u32[]{:S(2)}) collective-permute-start(bf16[32,2048]{1,0:T(8,128)(2,1)S(1)} %get-tuple-element.51), channel_id=1, source_target_pairs={{0,4},{4,0},{8,12},{12,8},{1,5},{5,1},{9,13},{13,9},{2,6},{6,2},{1... | collective-permute-start | bytes 393224 | tf_op jit(solution)/shard_map/ppermute | solution.py:336
  27.8 4.5 %collective-permute-start.11 = (bf16[32,2048]{1,0:T(8,128)(2,1)S(1)}, bf16[32,2048]{1,0:T(8,128)(2,1)S(1)}, u32[]{:S(2)}, u32[]{:S(2)}) collective-permute-start(bf16[32,2048]{1,0:T(8,128)(2,1)S(1)} %get-tuple-element.59), channel_id=1, source_target_pairs={{0,4},{4,0},{8,12},{12,8},{1,5},{5,1},{9,13},{13,9},{2,6},{6,2},{1... | collective-permute-start | bytes 393224 | tf_op jit(solution)/shard_map/ppermute | solution.py:336
  29.1 12.1 %collective-permute-start.10 = (bf16[32,2048]{1,0:T(8,128)(2,1)S(1)}, bf16[32,2048]{1,0:T(8,128)(2,1)S(1)}, u32[]{:S(2)}, u32[]{:S(2)}) collective-permute-start(bf16[32,2048]{1,0:T(8,128)(2,1)S(1)} %get-tuple-element.58), channel_id=1, source_target_pairs={{0,4},{4,0},{8,12},{12,8},{1,5},{5,1},{9,13},{13,9},{2,6},{6,2},{1... | collective-permute-start | bytes 393224 | tf_op jit(solution)/shard_map/ppermute | solution.py:336
  32.2 10.1 %collective-permute-start.9 = (bf16[32,2048]{1,0:T(8,128)(2,1)S(1)}, bf16[32,2048]{1,0:T(8,128)(2,1)S(1)}, u32[]{:S(2)}, u32[]{:S(2)}) collective-permute-start(bf16[32,2048]{1,0:T(8,128)(2,1)S(1)} %get-tuple-element.57), channel_id=1, source_target_pairs={{0,4},{4,0},{8,12},{12,8},{1,5},{5,1},{9,13},{13,9},{2,6},{6,2},{1... | collective-permute-start | bytes 393224 | tf_op jit(solution)/shard_map/ppermute | solution.py:336
  33.4 6.5 %collective-permute-start.12 = (f32[32,768]{1,0:T(8,128)S(1)}, f32[32,768]{1,0:T(8,128)S(1)}, u32[]{:S(2)}, u32[]{:S(2)}) collective-permute-start(f32[32,768]{1,0:T(8,128)S(1)} %get-tuple-element.62), channel_id=1, source_target_pairs={{0,1},{1,0},{2,3},{3,2},{4,5},{5,4},{6,7},{7,6},{8,9},{9,8},{10,11... | collective-permute-start | bytes 294920 | tf_op jit(solution)/shard_map/ppermute | solution.py:336
  39.9 4.1 %collective-permute-start.13 = (f32[32,768]{1,0:T(8,128)S(1)}, f32[32,768]{1,0:T(8,128)S(1)}, u32[]{:S(2)}, u32[]{:S(2)}) collective-permute-start(f32[32,768]{1,0:T(8,128)S(1)} %add.2.refs_4_), channel_id=1, source_target_pairs={{0,2},{2,0},{1,3},{3,1},{4,6},{6,4},{5,7},{7,5},{8,10},{10,8},{9,1... | collective-permute-start | bytes 294920 | tf_op jit(solution)/shard_map/ppermute | solution.py:336
  43.3 1.7 %collective-permute-start.14 = (f32[32,768]{1,0:T(8,128)S(1)}, f32[32,768]{1,0:T(8,128)S(1)}, u32[]{:S(2)}, u32[]{:S(2)}) collective-permute-start(f32[32,768]{1,0:T(8,128)S(1)} %get-tuple-element.64), channel_id=1, source_target_pairs={{0,1},{1,0},{2,3},{3,2},{4,5},{5,4},{6,7},{7,6},{8,9},{9,8},{10,11... | collective-permute-start | bytes 294920 | tf_op jit(solution)/shard_map/ppermute | solution.py:336

commit v4 on v3

v4 whole, which is shorter than its diff:
```python
import jax
import jax.numpy as jnp
from jax import lax
from jax.experimental import pallas as pl
from jax.experimental.pallas import tpu as pltpu
from jax.sharding import PartitionSpec as P

CHUNKS = (6, 6, 4)
QUARTERS = (4, 4, 4, 4)
VMEM = pl.BlockSpec(memory_space=pltpu.VMEM)
SMEM = pl.BlockSpec(memory_space=pltpu.SMEM)
HBM = pl.BlockSpec(memory_space=pltpu.HBM)
ANY = pl.BlockSpec(memory_space=pl.ANY)
PIECES = 4
SCALE = 0.1


def line_ring(n):
    odd = list(range(1, n, 2))
    even = list(range(0, n, 2))
    return [0] + odd + even[:0:-1]


def ring_position(z, n):
    return jnp.where(z == 0, 0, jnp.where(z % 2 == 1, (z + 1) // 2, n - z // 2))


def call(kernel, name, shapes, specs, args, limit=8, scratch=(), flops=0, aliases=None, after=()):
    args = (*args, *after)
    specs = [*specs, *[ANY] * len(after)]
    count = len(args) - len(after)

    def body(*refs):
        kernel(*refs[:count], *refs[len(args) :])

    return pl.pallas_call(
        body,
        in_specs=specs,
        out_specs=[VMEM] * len(shapes),
        out_shape=shapes,
        scratch_shapes=scratch,
        input_output_aliases=aliases or {},
        compiler_params=pltpu.CompilerParams(vmem_limit_bytes=limit << 20),
        cost_estimate=pl.CostEstimate(flops=int(SCALE * flops), bytes_accessed=0, transcendentals=0),
        name=name,
    )(*args)


def times(rows, train_part):
    return lax.dot_general(
        rows, train_part, (((1,), (1,)), ((), ())), preferred_element_type=jnp.float32
    )


def fetch(train, spans, after=(), query=None, precond=None, query_spans=()):
    count = train.shape[0]
    tall = count // PIECES
    made = len(query_spans)
    first, total = (query_spans[0][0], sum(width for _, width in query_spans)) if made else (0, 0)

    def kernel(train_ref, *refs):
        copies = []
        if made:
            query_ref, precond_ref, *refs, held, scale, query_sems = refs
            copies.append(pltpu.make_async_copy(precond_ref.at[:, pl.ds(first, total)], scale, query_sems.at[made]))
            copies += [
                pltpu.make_async_copy(
                    query_ref.at[:, pl.ds(start, width)], held.at[:, pl.ds(start - first, width)], query_sems.at[i]
                )
                for i, (start, width) in enumerate(query_spans)
            ]
        blocks, outs, sems = refs[:made], refs[made:-1], refs[-1]
        for copy in copies:
            copy.start()
        train_copies = [
            pltpu.make_async_copy(
                train_ref.at[pl.ds(i * tall, tall), pl.ds(start, width)],
                out.at[pl.ds(i * tall, tall), :],
                sems.at[k, i],
            )
            for k, (out, (start, width)) in enumerate(zip(outs, spans))
            for i in range(PIECES)
        ]
        for copy in train_copies:
            copy.start()
        if made:
            copies[0].wait()
        for i, (start, width) in enumerate(query_spans):
            copies[i + 1].wait()
            at = pl.ds(start - first, width)
            blocks[i][...] = (held[:, at] * scale[:, at]).astype(jnp.bfloat16)
        for copy in train_copies:
            copy.wait()

    rows = query.shape[0] if made else 0
    scratch = [pltpu.SemaphoreType.DMA((max(len(spans), 1), PIECES))]
    if made:
        scratch += [
            pltpu.VMEM((rows, total), jnp.float32),
            pltpu.VMEM((1, total), jnp.float32),
            pltpu.SemaphoreType.DMA((made + 1,)),
        ]
    shapes = [jax.ShapeDtypeStruct((rows, width), jnp.bfloat16) for _, width in query_spans]
    shapes += [pltpu.VMEM((count, width), train.dtype) for _, width in spans]
    return call(
        kernel,
        "fetch" if spans else "condition",
        shapes,
        [ANY] * (3 if made else 1),
        (train, query, precond) if made else (train,),
        scratch=scratch,
        flops=2 * 512 * sum(width for _, width in spans) * count,
        after=after,
    )


def rate_row(learn_rates, ckpt_order, columns, after):
    def kernel(rates_ref, order_ref, row, rates, order, sems):
        copies = [
            pltpu.make_async_copy(rates_ref, rates, sems.at[0]),
            pltpu.make_async_copy(order_ref, order, sems.at[1]),
        ]
        for copy in copies:
            copy.start()
        for copy in copies:
            copy.wait()
        row[...] = jnp.full(row.shape, rates[order[lax.axis_index("ckpt")]], jnp.float32)

    return call(
        kernel,
        "rate_row",
        [jax.ShapeDtypeStruct((1, columns), jnp.float32)],
        [ANY, ANY],
        (learn_rates, ckpt_order),
        scratch=[
            pltpu.SMEM(learn_rates.shape, learn_rates.dtype),
            pltpu.SMEM(ckpt_order.shape, ckpt_order.dtype),
            pltpu.SemaphoreType.DMA((2,)),
        ],
        after=after,
    )[0]


def score(blocks, train, sums=(), picked=(), forward=False, after=()):
    count = len(blocks)
    rows, width = blocks[0].shape
    args = [*blocks, train, *sums, *picked]

    def kernel(*refs):
        given, train_ref, before, outs = refs[:count], refs[count], refs[count + 1 : len(args)], refs[len(args) :]
        stacked = given[0][...] if count == 1 else jnp.concatenate([ref[...] for ref in given], axis=0)
        scores = times(stacked, train_ref[...])
        for i in range(count):
            part = scores[i * rows : (i + 1) * rows]
            if i < len(sums):
                outs[i][...] = before[i][...] + part
            elif picked:
                home, _ = my_pair()

                @pl.when(home)
                def _():
                    outs[i][...] = before[-2][...] + part

                @pl.when(jnp.logical_not(home))
                def _():
                    outs[i][...] = before[-1][...] + part
            else:
                outs[i][...] = part

    shapes = [jax.ShapeDtypeStruct((rows, train.shape[0]), jnp.float32)] * count
    if forward:
        shapes.append(jax.ShapeDtypeStruct(blocks[-1].shape, blocks[-1].dtype))
    return call(
        kernel,
        "score",
        shapes,
        [VMEM] * len(args),
        args,
        flops=2 * 256 * width * train.shape[0],
        aliases={count - 1: count} if forward else None,
        after=after,
    )


def sort_out(sums, rate, shards, groups):
    per_group = shards // groups
    rows, columns = sums[0].shape

    def kernel(*refs):
        given, rate_ref, outs = refs[: len(sums)], refs[len(sums)], refs[len(sums) + 1 :]
        my_place = ring_position(lax.axis_index("shard"), shards)
        my_group = lax.axis_index("ckpt") * lax.axis_size("sub") + lax.axis_index("sub")
        for d in range(groups):
            for k in range(per_group):
                chip = (my_group ^ d) * per_group + k
                step = (my_place - ring_position(chip, shards) + shards) % shards
                at = pl.ds((d // 2 * per_group + k) * rows, rows)
                for s, ref in enumerate(given):

                    @pl.when(step == s)
                    def _():
                        outs[1 - d % 2][at, :] = ref[...] * rate_ref[...]

    shape = jax.ShapeDtypeStruct((groups // 2 * per_group * rows, columns), jnp.float32)
    return call(kernel, "sort_out", [shape] * 2, [VMEM] * (len(sums) + 1), (*sums, rate))


def fold(kept, received, tall):
    pieces = kept.shape[0] // tall

    def kernel(kept_ref, received_ref, *outs):
        if pieces == 1:
            outs[0][...] = kept_ref[...] + received_ref[...]
            return
        for i in range(pieces):
            at = pl.ds(i * tall, tall)
            outs[1 - i % 2][pl.ds(i // 2 * tall, tall), :] = kept_ref[at, :] + received_ref[at, :]

    shapes = [jax.ShapeDtypeStruct((max(pieces // 2, 1) * tall, kept.shape[1]), jnp.float32)] * min(pieces, 2)
    return call(kernel, "fold", shapes, [VMEM] * 2, (kept, received))


def my_pair():
    z = lax.axis_index("shard")
    return z // 2 == lax.axis_index("ckpt"), z % 2 == lax.axis_index("sub")


def deal(own, far, after=()):
    def kernel(own_ref, far_ref, first, second):
        home, _ = my_pair()

        @pl.when(home)
        def _():
            first[...] = far_ref[...]
            second[...] = own_ref[...]

        @pl.when(jnp.logical_not(home))
        def _():
            first[...] = own_ref[...]
            second[...] = far_ref[...]

    shape = jax.ShapeDtypeStruct(own.shape, own.dtype)
    return call(kernel, "deal", [shape] * 2, [VMEM] * 2, (own, far), after=after)


def hand_on(array, after):
    def kernel(_, __):
        pass

    shape = jax.ShapeDtypeStruct(array.shape, array.dtype)
    return call(kernel, "hand_on", [shape], [VMEM], (array,), after=after, aliases={0: 0})[0]


def part_pair(if_home, if_not, other, rate, after=()):
    def kernel(home_ref, not_ref, other_ref, rate_ref, sent, kept):
        home, agree = my_pair()
        for one, ref in ((home, home_ref), (jnp.logical_not(home), not_ref)):

            @pl.when(jnp.logical_and(one, agree))
            def _():
                kept[...] = ref[...] * rate_ref[...]
                sent[...] = other_ref[...] * rate_ref[...]

            @pl.when(jnp.logical_and(one, jnp.logical_not(agree)))
            def _():
                sent[...] = ref[...] * rate_ref[...]
                kept[...] = other_ref[...] * rate_ref[...]

    shape = jax.ShapeDtypeStruct(other.shape, jnp.float32)
    return call(kernel, "part_pair", [shape] * 2, [VMEM] * 4, (if_home, if_not, other, rate), after=after)


def add(*arrays):
    def kernel(*refs):
        total = refs[0][...]
        for ref in refs[1:-1]:
            total = total + ref[...]
        refs[-1][...] = total

    shape = jax.ShapeDtypeStruct(arrays[0].shape, jnp.float32)
    return call(kernel, "add", [shape], [VMEM] * len(arrays), arrays)[0]


def in_pairs(train, query, precond, learn_rates, ckpt_order):
    def swap(array, axis, distance):
        size = lax.axis_size(axis)
        return lax.ppermute(array, axis, [(i, i ^ distance) for i in range(size)])

    unit = query.shape[1] // sum(QUARTERS)
    spans = [(unit * sum(QUARTERS[:j]), unit * c) for j, c in enumerate(QUARTERS)]

    (own1,) = fetch(train, [], [], query, precond, spans[:1])
    two1 = swap(own1, "shard", 2)
    one1 = swap(own1, "shard", 1)
    (own2,) = fetch(train, [], [own1], query, precond, spans[1:2])
    two2 = swap(own2, "shard", 2)
    one2 = swap(own2, "shard", 1)
    own3, own4, train1, train2, train3, train4 = fetch(train, spans, [own2], query, precond, spans[2:])
    two3 = swap(own3, "shard", 2)
    two4 = swap(own4, "shard", 2)
    two1 = hand_on(two1, [own4, one1])
    three1 = swap(two1, "shard", 1)
    two2 = hand_on(two2, [two1, one2])
    three2 = swap(two2, "shard", 1)

    sums = score([own1, one1, two1, three1], train1, after=[two2])
    first3, second3 = deal(own3, two3, [sums[0]])
    first3 = swap(first3, "shard", 1)
    sums = score([own2, one2, two2, three2], train2, sums, after=[second3])
    first4, second4 = deal(own4, two4, [sums[0]])
    first4 = swap(first4, "shard", 1)
    own_sums, one_sums, two_sums, three_sums = sums
    rate = rate_row(learn_rates, ckpt_order, train.shape[0], [second4])
    second3 = swap(hand_on(second3, [first3, rate]), "shard", 1)
    own_sums, two_sums, first_sums = score(
        [own3, two3, first3], train3, [own_sums, two_sums], (three_sums, one_sums), after=[second4]
    )
    second4 = swap(hand_on(second4, [own_sums]), "shard", 1)
    own_sums, two_sums, first_sums = score([own4, two4, first4], train4, [own_sums, two_sums, first_sums])

    sent, kept = part_pair(two_sums, own_sums, first_sums, rate)
    across = add(kept, swap(sent, "sub", 1))
    from_far = swap(across, "ckpt", 1)
    (second_sums,) = score([second3], train3, picked=(one_sums, three_sums), after=[across])
    (second_sums,) = score([second4], train4, [second_sums])
    sent, kept = part_pair(own_sums, two_sums, second_sums, rate)
    return add(kept, from_far, swap(sent, "sub", 1))


def in_ring(sizes, train_local, query_local, precond, learn_rates, ckpt_order):
    shards, groups = sizes[0], sizes[1] * sizes[2]
    ring = line_ring(shards)
    hops = [(ring[i], ring[(i + 1) % shards]) for i in range(shards)]

    unit = query_local.shape[1] // sum(CHUNKS)
    spans = [(unit * sum(CHUNKS[:j]), unit * c) for j, c in enumerate(CHUNKS)]
    own = fetch(train_local, [], [], query_local, precond, spans[:1])
    held = fetch(train_local, spans[:1], own)
    for span in spans[1:]:
        own += fetch(train_local, [], [held[0], own[-1]], query_local, precond, [span])

    sums = []
    current = own
    for step in range(1, shards):
        current = [lax.ppermute(block, "shard", hops) for block in current]
        forward = step < shards - 1
        total = ()
        for j in range(len(CHUNKS)):
            if j >= len(held):
                held += fetch(train_local, spans[j : j + 1], total[:1])
            blocks = [own[j], current[j]] if step == 1 else [current[j]]
            total = score(blocks, held[j], total, forward=forward)
            if forward:
                *total, current[j] = total
        sums += total
    rate = rate_row(learn_rates, ckpt_order, train_local.shape[0], sums[:1])

    sent, kept = sort_out(sums, rate, shards, groups)
    tall = kept.shape[0] // (groups // 2)
    for i in range(groups.bit_length() - 1):
        received = lax.ppermute(sent, ("ckpt", "sub"), [(g, g ^ 1 << i) for g in range(groups)])
        *more, kept = fold(kept, received, tall)
        sent = more[0] if more else None
    return kept


def per_device(sizes, train_grads, query_grads, precond, learn_rates, ckpt_order):
    args = [train_grads[0], query_grads[0], precond, learn_rates, ckpt_order]
    args = [pltpu.with_memory_space_constraint(array, pltpu.HBM) for array in args]
    return in_pairs(*args) if sizes == (4, 2, 2) else in_ring(sizes, *args)


def solution(mesh):
    sizes = tuple(mesh.shape[axis] for axis in ("shard", "ckpt", "sub"))

    def run(*args):
        return per_device(sizes, *args)

    return jax.shard_map(
        run,
        mesh=mesh,
        in_specs=(
            P("ckpt", ("parts", "shard"), "sub"),
            P("ckpt", ("parts", "shard"), "sub"),
            P("ckpt", "sub"),
            P(),
            P(),
        ),
        out_specs=P(("ckpt", "sub"), ("parts", "shard")),
        check_vma=False,
    )
```

time: 46.3 us -> 43.9 us (0.948)
  Pallas kernels: 20.7 us -> 15 us
  starting transfers between devices: 19.9 us -> 22.6 us
  waiting for transfers between devices: 4.88 us -> 5.54 us
    pallas_call x20, Pallas kernels: 20.7 us -> 15 us  [call(): pl.pallas_call(body, in_specs=specs, out_specs=[VMEM] * len(shapes), out_...]
    ppermute x15, starting transfers between devices: 19.9 us -> 22.6 us  [swap(): return lax.ppermute(array, axis, [(i, i ^ distance) for i in range(size)])]
    ppermute x15, waiting for transfers between devices: 4.88 us -> 5.54 us  [swap(): return lax.ppermute(array, axis, [(i, i ^ distance) for i in range(size)])]
  transfers between devices with their start and end apart: 15 -> 15, of which waited for: 3 -> 7; matrix products, arithmetic and copies ran while one was open for 0% -> 0% of each run, Pallas kernels for 42% -> 31%
where the time goes in v4:
time: 43.9 us; the launch traced here: 43.4 us
  starting transfers between devices  22.6 us (51%)
  Pallas kernels  15 us (34%)
  waiting for transfers between devices  5.54 us (13%)
    ppermute x15, starting transfers between devices, swap(): return lax.ppermute(array, axis, [(i, i ^ distance) for i in range(size)])  22.6 us
    pallas_call x20, Pallas kernels, call(): pl.pallas_call(body, in_specs=specs, out_specs=[VMEM] * len(shapes), out_...  15 us
    ppermute x15, waiting for transfers between devices, swap(): return lax.ppermute(array, axis, [(i, i ^ distance) for i in range(size)])  5.54 us
  transfers between devices with their start and end apart: 15, of which 7 were waited for; matrix products, arithmetic and copies ran while one was open for 0% of the time, Pallas kernels for 31%

profile of v4, /device:TPU:1, one launch (start us, length us, event | category | flops | bytes accessed | tf_op | source)
XLA Modules:
  0.0 43.4 jit_solution(15140850783285440798)
XLA Ops:
  0.0 1.0 %condition.2.refs_3_.refs_0_ = bf16[32,2048]{1,0:T(8,128)(2,1)S(1)} custom-call(bf16[768,8192]{1,0:T(8,128)(2,1)} %bitcast.2, f32[32,8192]{1,0:T(8,128)} %bitcast.5, f32[1,8192]{1,0:T(1,128)} %refs_2_.5), custom_call_target="tpu_custom_call" | custom-call | tf_op jit(solution)/shard_map/condition/pallas_call | solution.py:36
  1.0 2.2 %collective-permute-start.4 = (bf16[32,2048]{1,0:T(8,128)(2,1)S(1)}, bf16[32,2048]{1,0:T(8,128)(2,1)S(1)}, u32[]{:S(2)}, u32[]{:S(2)}) collective-permute-start(bf16[32,2048]{1,0:T(8,128)(2,1)S(1)} %condition.2.refs_3_.refs_0_), channel_id=1, source_target_pairs={{0,4},{4,0},{8,12},{12,8},{1,5},{5,1},{9,13},{13,9},{2,6},{6,2},{1... | collective-permute-start | bytes 393224 | tf_op jit(solution)/shard_map/ppermute | solution.py:287
  3.2 2.3 %collective-permute-start.3 = (bf16[32,2048]{1,0:T(8,128)(2,1)S(1)}, bf16[32,2048]{1,0:T(8,128)(2,1)S(1)}, u32[]{:S(2)}, u32[]{:S(2)}) collective-permute-start(bf16[32,2048]{1,0:T(8,128)(2,1)S(1)} %condition.2.refs_3_.refs_0_), channel_id=1, source_target_pairs={{0,8},{4,12},{8,0},{12,4},{1,9},{5,13},{9,1},{13,5},{2,10},{6,14},... | collective-permute-start | bytes 393224 | tf_op jit(solution)/shard_map/ppermute | solution.py:287
  5.5 1.0 %condition.3.refs_3_.refs_0_ = bf16[32,2048]{1,0:T(8,128)(2,1)S(1)} custom-call(bf16[768,8192]{1,0:T(8,128)(2,1)} %bitcast.3, f32[32,8192]{1,0:T(8,128)} %bitcast.6, f32[1,8192]{1,0:T(1,128)} %refs_2_.5, bf16[32,2048]{1,0:T(8,128)(2,1)S(1)} %condition.2.refs_3_.refs_0_), custom_call_target="tpu_custom_call" | custom-call | tf_op jit(solution)/shard_map/condition/pallas_call | solution.py:36
  6.8 4.9 %fetch.1 = (bf16[32,2048]{1,0:T(8,128)(2,1)S(1)}, bf16[32,2048]{1,0:T(8,128)(2,1)S(1)}, bf16[768,2048]{1,0:T(8,128)(2,1)S(1)}, bf16[768,2048]{1,0:T(8,128)(2,1)S...) custom-call(bf16[768,8192]{1,0:T(8,128)(2,1)} %bitcast.4, f32[32,8192]{1,0:T(8,128)} %bitcast.7, ...), custom_call_target="tpu_custom_call" | custom-call | flops 644245120 | tf_op jit(solution)/shard_map/fetch/pallas_call | solution.py:36
  11.8 1.4 %collective-permute-start.6 = (bf16[32,2048]{1,0:T(8,128)(2,1)S(1)}, bf16[32,2048]{1,0:T(8,128)(2,1)S(1)}, u32[]{:S(2)}, u32[]{:S(2)}) collective-permute-start(bf16[32,2048]{1,0:T(8,128)(2,1)S(1)} %hand_on.4.refs_1_.refs_2_), channel_id=1, source_target_pairs={{0,4},{4,0},{8,12},{12,8},{1,5},{5,1},{9,13},{13,9},{2,6},{6,2},{1... | collective-permute-start | bytes 393224 | tf_op jit(solution)/shard_map/ppermute | solution.py:287
  13.2 2.3 %collective-permute-start.7 = (bf16[32,2048]{1,0:T(8,128)(2,1)S(1)}, bf16[32,2048]{1,0:T(8,128)(2,1)S(1)}, u32[]{:S(2)}, u32[]{:S(2)}) collective-permute-start(bf16[32,2048]{1,0:T(8,128)(2,1)S(1)} %get-tuple-element.40.refs_0_), channel_id=1, source_target_pairs={{0,8},{4,12},{8,0},{12,4},{1,9},{5,13},{9,1},{13,5},{2,10},{6,14},... | collective-permute-start | bytes 393224 | tf_op jit(solution)/shard_map/ppermute | solution.py:287
  15.7 1.3 %collective-permute-start.5 = (bf16[32,2048]{1,0:T(8,128)(2,1)S(1)}, bf16[32,2048]{1,0:T(8,128)(2,1)S(1)}, u32[]{:S(2)}, u32[]{:S(2)}) collective-permute-start(bf16[32,2048]{1,0:T(8,128)(2,1)S(1)} %hand_on.5.refs_5_.refs_2_), channel_id=1, source_target_pairs={{0,4},{4,0},{8,12},{12,8},{1,5},{5,1},{9,13},{13,9},{2,6},{6,2},{1... | collective-permute-start | bytes 393224 | tf_op jit(solution)/shard_map/ppermute | solution.py:287
  17.5 0.8 %collective-permute-done.6.refs_3_ = bf16[32,2048]{1,0:T(8,128)(2,1)S(1)} collective-permute-done((bf16[32,2048]{1,0:T(8,128)(2,1)S(1)}, bf16[32,2048]{1,0:T(8,128)(2,1)S(1)}, u32[]{:S(2)}, u32[]{:S(2)}) %collective-permute-start.6) | collective-permute-done | bytes 131104 | tf_op jit(solution)/shard_map/ppermute | solution.py:287
  18.3 1.2 %score.6 = (f32[32,768]{1,0:T(8,128)S(1)}, f32[32,768]{1,0:T(8,128)S(1)}, f32[32,768]{1,0:T(8,128)S(1)}, f32[32,768]{1,0:T(8,128)S(1)}) custom-call(bf16[32,2048]{1,0:T(8,128)(2,1)S(1)} %condition.2.refs_3_.refs_0_, bf16[32,2048]{1,0:T(8,128)(2,1)S(1)} %collective-permute-done.4.refs_2_.refs_1_, bf16[32,2048]{1,0:T(8,128)(2,1)S(1)} %hand_on.4.refs_1_.refs_2_, ...), custom_call_target="tpu_custom_call" | custom-call | flops 80530640 | tf_op jit(solution)/shard_map/score/pallas_call | solution.py:36
  19.7 3.0 %collective-permute-start.9 = (bf16[32,2048]{1,0:T(8,128)(2,1)S(1)}, bf16[32,2048]{1,0:T(8,128)(2,1)S(1)}, u32[]{:S(2)}, u32[]{:S(2)}) collective-permute-start(bf16[32,2048]{1,0:T(8,128)(2,1)S(1)} %get-tuple-element.45), channel_id=1, source_target_pairs={{0,4},{4,0},{8,12},{12,8},{1,5},{5,1},{9,13},{13,9},{2,6},{6,2},{1... | collective-permute-start | bytes 393224 | tf_op jit(solution)/shard_map/ppermute | solution.py:287
  22.8 1.4 %collective-permute-done.5.refs_3_ = bf16[32,2048]{1,0:T(8,128)(2,1)S(1)} collective-permute-done((bf16[32,2048]{1,0:T(8,128)(2,1)S(1)}, bf16[32,2048]{1,0:T(8,128)(2,1)S(1)}, u32[]{:S(2)}, u32[]{:S(2)}) %collective-permute-start.5) | collective-permute-done | bytes 131104 | tf_op jit(solution)/shard_map/ppermute | solution.py:287
  24.2 1.2 %score.7 = (f32[32,768]{1,0:T(8,128)S(1)}, f32[32,768]{1,0:T(8,128)S(1)}, f32[32,768]{1,0:T(8,128)S(1)}, f32[32,768]{1,0:T(8,128)S(1)}) custom-call(bf16[32,2048]{1,0:T(8,128)(2,1)S(1)} %condition.3.refs_3_.refs_0_, bf16[32,2048]{1,0:T(8,128)(2,1)S(1)} %collective-permute-done.1.refs_2_.refs_1_, bf16[32,2048]{1,0:T(8,128)(2,1)S(1)} %hand_on.5.refs_5_.refs_2_, ...), custom_call_target="tpu_custom_call" | custom-call | flops 80530640 | tf_op jit(solution)/shard_map/score/pallas_call | solution.py:36
  25.3 1.0 %collective-permute-done.refs_1_ = bf16[32,2048]{1,0:T(8,128)(2,1)S(1)} collective-permute-done((bf16[32,2048]{1,0:T(8,128)(2,1)S(1)}, bf16[32,2048]{1,0:T(8,128)(2,1)S(1)}, u32[]{:S(2)}, u32[]{:S(2)}) %collective-permute-start) | collective-permute-done | bytes 131104 | tf_op jit(solution)/shard_map/ppermute | solution.py:287
  26.4 2.0 %collective-permute-start.8 = (bf16[32,2048]{1,0:T(8,128)(2,1)S(1)}, bf16[32,2048]{1,0:T(8,128)(2,1)S(1)}, u32[]{:S(2)}, u32[]{:S(2)}) collective-permute-start(bf16[32,2048]{1,0:T(8,128)(2,1)S(1)} %get-tuple-element.43), channel_id=1, source_target_pairs={{0,4},{4,0},{8,12},{12,8},{1,5},{5,1},{9,13},{13,9},{2,6},{6,2},{1... | collective-permute-start | bytes 393224 | tf_op jit(solution)/shard_map/ppermute | solution.py:287
  29.1 1.2 %collective-permute-start.11 = (bf16[32,2048]{1,0:T(8,128)(2,1)S(1)}, bf16[32,2048]{1,0:T(8,128)(2,1)S(1)}, u32[]{:S(2)}, u32[]{:S(2)}) collective-permute-start(bf16[32,2048]{1,0:T(8,128)(2,1)S(1)} %hand_on.7), channel_id=1, source_target_pairs={{0,4},{4,0},{8,12},{12,8},{1,5},{5,1},{9,13},{13,9},{2,6},{6,2},{1... | collective-permute-start | bytes 393224 | tf_op jit(solution)/shard_map/ppermute | solution.py:287
  30.3 1.1 %score.8 = (f32[32,768]{1,0:T(8,128)S(1)}, f32[32,768]{1,0:T(8,128)S(1)}, f32[32,768]{1,0:T(8,128)S(1)}) custom-call(bf16[32,2048]{1,0:T(8,128)(2,1)S(1)} %get-tuple-element.40.refs_0_, bf16[32,2048]{1,0:T(8,128)(2,1)S(1)} %collective-permute-done.7.refs_1_, bf16[32,2048]{1,0:T(8,128)(2,1)S(1)} %collective-permute-done.9.refs_2_.refs_1_, ...), custom_call_target="tpu_custom_call" | custom-call | flops 80530640 | tf_op jit(solution)/shard_map/score/pallas_call | solution.py:36
  31.8 1.1 %score.9 = (f32[32,768]{1,0:T(8,128)S(1)}, f32[32,768]{1,0:T(8,128)S(1)}, f32[32,768]{1,0:T(8,128)S(1)}) custom-call(bf16[32,2048]{1,0:T(8,128)(2,1)S(1)} %get-tuple-element.33.refs_1_.refs_0_, bf16[32,2048]{1,0:T(8,128)(2,1)S(1)} %collective-permute-done.refs_1_, bf16[32,2048]{1,0:T(8,128)(2,1)S(1)} %collective-permute-done.8.refs_2_, ...), custom_call_target="tpu_custom_call" | custom-call | flops 80530640 | tf_op jit(solution)/shard_map/score/pallas_call | solution.py:36
  33.0 3.8 %collective-permute-start.12 = (f32[32,768]{1,0:T(8,128)S(1)}, f32[32,768]{1,0:T(8,128)S(1)}, u32[]{:S(2)}, u32[]{:S(2)}) collective-permute-start(f32[32,768]{1,0:T(8,128)S(1)} %get-tuple-element.58), channel_id=1, source_target_pairs={{0,1},{1,0},{2,3},{3,2},{4,5},{5,4},{6,7},{7,6},{8,9},{9,8},{10,11... | collective-permute-start | bytes 294920 | tf_op jit(solution)/shard_map/ppermute | solution.py:287
  36.7 0.9 %collective-permute-done.12.refs_1_ = f32[32,768]{1,0:T(8,128)S(1)} collective-permute-done((f32[32,768]{1,0:T(8,128)S(1)}, f32[32,768]{1,0:T(8,128)S(1)}, u32[]{:S(2)}, u32[]{:S(2)}) %collective-permute-start.12) | collective-permute-done | bytes 98336 | tf_op jit(solution)/shard_map/ppermute | solution.py:287
  37.7 1.3 %collective-permute-start.13 = (f32[32,768]{1,0:T(8,128)S(1)}, f32[32,768]{1,0:T(8,128)S(1)}, u32[]{:S(2)}, u32[]{:S(2)}) collective-permute-start(f32[32,768]{1,0:T(8,128)S(1)} %add.2.refs_4_), channel_id=1, source_target_pairs={{0,2},{2,0},{1,3},{3,1},{4,6},{6,4},{5,7},{7,5},{8,10},{10,8},{9,1... | collective-permute-start | bytes 294920 | tf_op jit(solution)/shard_map/ppermute | solution.py:287
  39.0 1.0 %score.10.refs_2_ = f32[32,768]{1,0:T(8,128)S(1)} custom-call(bf16[32,2048]{1,0:T(8,128)(2,1)S(1)} %collective-permute-done.11.refs_0_, bf16[768,2048]{1,0:T(8,128)(2,1)S(1)} %get-tuple-element.46.refs_3_.refs_1_, f32[32,768]{1,0:T(8,128)S(1)} %get-tuple-element.49.refs_7_.refs_2_, f32[32,768]{1,0:T(8,128)S(1)} %get-tuple-element.48.refs_6_.refs_3_, ...), custom_call_target="tpu_custom_call" | custom-call | flops 80530640 | tf_op jit(solution)/shard_map/score/pallas_call | solution.py:36
  40.0 1.0 %score.11.refs_2_ = f32[32,768]{1,0:T(8,128)S(1)} custom-call(bf16[32,2048]{1,0:T(8,128)(2,1)S(1)} %collective-permute-done.10.refs_0_, bf16[768,2048]{1,0:T(8,128)(2,1)S(1)} %get-tuple-element.44.refs_3_.refs_1_, f32[32,768]{1,0:T(8,128)S(1)} %score.10.refs_2_), custom_call_target="tpu_custom_call" | custom-call | flops 80530640 | tf_op jit(solution)/shard_map/score/pallas_call | solution.py:36
  41.8 0.9 %collective-permute-done.14.refs_2_ = f32[32,768]{1,0:T(8,128)S(1)} collective-permute-done((f32[32,768]{1,0:T(8,128)S(1)}, f32[32,768]{1,0:T(8,128)S(1)}, u32[]{:S(2)}, u32[]{:S(2)}) %collective-permute-start.14) | collective-permute-done | bytes 98336 | tf_op jit(solution)/shard_map/ppermute | solution.py:287
  (26 shorter events, 3.8 us)
Async XLA Ops:
  1.0 10.7 %collective-permute-start.4 = (bf16[32,2048]{1,0:T(8,128)(2,1)S(1)}, bf16[32,2048]{1,0:T(8,128)(2,1)S(1)}, u32[]{:S(2)}, u32[]{:S(2)}) collective-permute-start(bf16[32,2048]{1,0:T(8,128)(2,1)S(1)} %condition.2.refs_3_.refs_0_), channel_id=1, source_target_pairs={{0,4},{4,0},{8,12},{12,8},{1,5},{5,1},{9,13},{13,9},{2,6},{6,2},{1... | collective-permute-start | bytes 393224 | tf_op jit(solution)/shard_map/ppermute | solution.py:287
  3.2 8.5 %collective-permute-start.3 = (bf16[32,2048]{1,0:T(8,128)(2,1)S(1)}, bf16[32,2048]{1,0:T(8,128)(2,1)S(1)}, u32[]{:S(2)}, u32[]{:S(2)}) collective-permute-start(bf16[32,2048]{1,0:T(8,128)(2,1)S(1)} %condition.2.refs_3_.refs_0_), channel_id=1, source_target_pairs={{0,8},{4,12},{8,0},{12,4},{1,9},{5,13},{9,1},{13,5},{2,10},{6,14},... | collective-permute-start | bytes 393224 | tf_op jit(solution)/shard_map/ppermute | solution.py:287
  6.6 8.9 %collective-permute-start.1 = (bf16[32,2048]{1,0:T(8,128)(2,1)S(1)}, bf16[32,2048]{1,0:T(8,128)(2,1)S(1)}, u32[]{:S(2)}, u32[]{:S(2)}) collective-permute-start(bf16[32,2048]{1,0:T(8,128)(2,1)S(1)} %condition.3.refs_3_.refs_0_), channel_id=1, source_target_pairs={{0,4},{4,0},{8,12},{12,8},{1,5},{5,1},{9,13},{13,9},{2,6},{6,2},{1... | collective-permute-start | bytes 393224 | tf_op jit(solution)/shard_map/ppermute | solution.py:287
  6.8 8.9 %collective-permute-start.2 = (bf16[32,2048]{1,0:T(8,128)(2,1)S(1)}, bf16[32,2048]{1,0:T(8,128)(2,1)S(1)}, u32[]{:S(2)}, u32[]{:S(2)}) collective-permute-start(bf16[32,2048]{1,0:T(8,128)(2,1)S(1)} %condition.3.refs_3_.refs_0_), channel_id=1, source_target_pairs={{0,8},{4,12},{8,0},{12,4},{1,9},{5,13},{9,1},{13,5},{2,10},{6,14},... | collective-permute-start | bytes 393224 | tf_op jit(solution)/shard_map/ppermute | solution.py:287
  11.8 6.5 %collective-permute-start.6 = (bf16[32,2048]{1,0:T(8,128)(2,1)S(1)}, bf16[32,2048]{1,0:T(8,128)(2,1)S(1)}, u32[]{:S(2)}, u32[]{:S(2)}) collective-permute-start(bf16[32,2048]{1,0:T(8,128)(2,1)S(1)} %hand_on.4.refs_1_.refs_2_), channel_id=1, source_target_pairs={{0,4},{4,0},{8,12},{12,8},{1,5},{5,1},{9,13},{13,9},{2,6},{6,2},{1... | collective-permute-start | bytes 393224 | tf_op jit(solution)/shard_map/ppermute | solution.py:287
  13.2 6.5 %collective-permute-start.7 = (bf16[32,2048]{1,0:T(8,128)(2,1)S(1)}, bf16[32,2048]{1,0:T(8,128)(2,1)S(1)}, u32[]{:S(2)}, u32[]{:S(2)}) collective-permute-start(bf16[32,2048]{1,0:T(8,128)(2,1)S(1)} %get-tuple-element.40.refs_0_), channel_id=1, source_target_pairs={{0,8},{4,12},{8,0},{12,4},{1,9},{5,13},{9,1},{13,5},{2,10},{6,14},... | collective-permute-start | bytes 393224 | tf_op jit(solution)/shard_map/ppermute | solution.py:287
  15.7 8.5 %collective-permute-start.5 = (bf16[32,2048]{1,0:T(8,128)(2,1)S(1)}, bf16[32,2048]{1,0:T(8,128)(2,1)S(1)}, u32[]{:S(2)}, u32[]{:S(2)}) collective-permute-start(bf16[32,2048]{1,0:T(8,128)(2,1)S(1)} %hand_on.5.refs_5_.refs_2_), channel_id=1, source_target_pairs={{0,4},{4,0},{8,12},{12,8},{1,5},{5,1},{9,13},{13,9},{2,6},{6,2},{1... | collective-permute-start | bytes 393224 | tf_op jit(solution)/shard_map/ppermute | solution.py:287
  17.0 9.3 %collective-permute-start = (bf16[32,2048]{1,0:T(8,128)(2,1)S(1)}, bf16[32,2048]{1,0:T(8,128)(2,1)S(1)}, u32[]{:S(2)}, u32[]{:S(2)}) collective-permute-start(bf16[32,2048]{1,0:T(8,128)(2,1)S(1)} %get-tuple-element.33.refs_1_.refs_0_), channel_id=1, source_target_pairs={{0,8},{4,12},{8,0},{12,4},{1,9},{5,13},{9,1},{13,5},{2,10},{6,14},... | collective-permute-start | bytes 393224 | tf_op jit(solution)/shard_map/ppermute | solution.py:287
  19.7 9.3 %collective-permute-start.9 = (bf16[32,2048]{1,0:T(8,128)(2,1)S(1)}, bf16[32,2048]{1,0:T(8,128)(2,1)S(1)}, u32[]{:S(2)}, u32[]{:S(2)}) collective-permute-start(bf16[32,2048]{1,0:T(8,128)(2,1)S(1)} %get-tuple-element.45), channel_id=1, source_target_pairs={{0,4},{4,0},{8,12},{12,8},{1,5},{5,1},{9,13},{13,9},{2,6},{6,2},{1... | collective-permute-start | bytes 393224 | tf_op jit(solution)/shard_map/ppermute | solution.py:287
  26.4 5.4 %collective-permute-start.8 = (bf16[32,2048]{1,0:T(8,128)(2,1)S(1)}, bf16[32,2048]{1,0:T(8,128)(2,1)S(1)}, u32[]{:S(2)}, u32[]{:S(2)}) collective-permute-start(bf16[32,2048]{1,0:T(8,128)(2,1)S(1)} %get-tuple-element.43), channel_id=1, source_target_pairs={{0,4},{4,0},{8,12},{12,8},{1,5},{5,1},{9,13},{13,9},{2,6},{6,2},{1... | collective-permute-start | bytes 393224 | tf_op jit(solution)/shard_map/ppermute | solution.py:287
  29.1 9.9 %collective-permute-start.11 = (bf16[32,2048]{1,0:T(8,128)(2,1)S(1)}, bf16[32,2048]{1,0:T(8,128)(2,1)S(1)}, u32[]{:S(2)}, u32[]{:S(2)}) collective-permute-start(bf16[32,2048]{1,0:T(8,128)(2,1)S(1)} %hand_on.7), channel_id=1, source_target_pairs={{0,4},{4,0},{8,12},{12,8},{1,5},{5,1},{9,13},{13,9},{2,6},{6,2},{1... | collective-permute-start | bytes 393224 | tf_op jit(solution)/shard_map/ppermute | solution.py:287
  31.4 8.6 %collective-permute-start.10 = (bf16[32,2048]{1,0:T(8,128)(2,1)S(1)}, bf16[32,2048]{1,0:T(8,128)(2,1)S(1)}, u32[]{:S(2)}, u32[]{:S(2)}) collective-permute-start(bf16[32,2048]{1,0:T(8,128)(2,1)S(1)} %hand_on.6), channel_id=1, source_target_pairs={{0,4},{4,0},{8,12},{12,8},{1,5},{5,1},{9,13},{13,9},{2,6},{6,2},{1... | collective-permute-start | bytes 393224 | tf_op jit(solution)/shard_map/ppermute | solution.py:287
  33.0 4.7 %collective-permute-start.12 = (f32[32,768]{1,0:T(8,128)S(1)}, f32[32,768]{1,0:T(8,128)S(1)}, u32[]{:S(2)}, u32[]{:S(2)}) collective-permute-start(f32[32,768]{1,0:T(8,128)S(1)} %get-tuple-element.58), channel_id=1, source_target_pairs={{0,1},{1,0},{2,3},{3,2},{4,5},{5,4},{6,7},{7,6},{8,9},{9,8},{10,11... | collective-permute-start | bytes 294920 | tf_op jit(solution)/shard_map/ppermute | solution.py:287
  37.7 4.1 %collective-permute-start.13 = (f32[32,768]{1,0:T(8,128)S(1)}, f32[32,768]{1,0:T(8,128)S(1)}, u32[]{:S(2)}, u32[]{:S(2)}) collective-permute-start(f32[32,768]{1,0:T(8,128)S(1)} %add.2.refs_4_), channel_id=1, source_target_pairs={{0,2},{2,0},{1,3},{3,1},{4,6},{6,4},{5,7},{7,5},{8,10},{10,8},{9,1... | collective-permute-start | bytes 294920 | tf_op jit(solution)/shard_map/ppermute | solution.py:287
  41.1 1.7 %collective-permute-start.14 = (f32[32,768]{1,0:T(8,128)S(1)}, f32[32,768]{1,0:T(8,128)S(1)}, u32[]{:S(2)}, u32[]{:S(2)}) collective-permute-start(f32[32,768]{1,0:T(8,128)S(1)} %get-tuple-element.60), channel_id=1, source_target_pairs={{0,1},{1,0},{2,3},{3,2},{4,5},{5,4},{6,7},{7,6},{8,9},{9,8},{10,11... | collective-permute-start | bytes 294920 | tf_op jit(solution)/shard_map/ppermute | solution.py:287

commit v5 on v4

--- a/solution.py
+++ b/solution.py
@@ -25,7 +25,7 @@
     return jnp.where(z == 0, 0, jnp.where(z % 2 == 1, (z + 1) // 2, n - z // 2))
 
 
-def call(kernel, name, shapes, specs, args, limit=8, scratch=(), flops=0, aliases=None, after=()):
+def call(kernel, name, shapes, specs, args, limit=8, scratch=(), flops=0, aliases=None, after=(), out_specs=None):
     args = (*args, *after)
     specs = [*specs, *[ANY] * len(after)]
     count = len(args) - len(after)
@@ -36,7 +36,7 @@
     return pl.pallas_call(
         body,
         in_specs=specs,
-        out_specs=[VMEM] * len(shapes),
+        out_specs=out_specs or [VMEM] * len(shapes),
         out_shape=shapes,
         scratch_shapes=scratch,
         input_output_aliases=aliases or {},
@@ -52,7 +52,7 @@
     )
 
 
-def fetch(train, spans, after=(), query=None, precond=None, query_spans=()):
+def fetch(train, spans, after=(), query=None, precond=None, query_spans=(), rates=()):
     count = train.shape[0]
     tall = count // PIECES
     made = len(query_spans)
@@ -60,6 +60,15 @@
 
     def kernel(train_ref, *refs):
         copies = []
+        if rates:
+            *refs, plan, order, rate_sems = refs
+            plan_ref, order_ref, *refs = refs
+            rate_copies = [
+                pltpu.make_async_copy(plan_ref, plan, rate_sems.at[0]),
+                pltpu.make_async_copy(order_ref, order, rate_sems.at[1]),
+            ]
+            for copy in rate_copies:
+                copy.start()
         if made:
             query_ref, precond_ref, *refs, held, scale, query_sems = refs
             copies.append(pltpu.make_async_copy(precond_ref.at[:, pl.ds(first, total)], scale, query_sems.at[made]))
@@ -69,7 +78,7 @@
                 )
                 for i, (start, width) in enumerate(query_spans)
             ]
-        blocks, outs, sems = refs[:made], refs[made:-1], refs[-1]
+        blocks, outs, sems = refs[:made], refs[made : made + len(spans)], refs[-1]
         for copy in copies:
             copy.start()
         train_copies = [
@@ -89,6 +98,11 @@
             copies[i + 1].wait()
             at = pl.ds(start - first, width)
             blocks[i][...] = (held[:, at] * scale[:, at]).astype(jnp.bfloat16)
+        if rates:
+            for copy in rate_copies:
+                copy.wait()
+            row = refs[made + len(spans)]
+            row[...] = jnp.full(row.shape, plan[order[lax.axis_index("ckpt")]], jnp.float32)
         for copy in train_copies:
             copy.wait()
 
@@ -102,43 +116,20 @@
         ]
     shapes = [jax.ShapeDtypeStruct((rows, width), jnp.bfloat16) for _, width in query_spans]
     shapes += [pltpu.VMEM((count, width), train.dtype) for _, width in spans]
+    if rates:
+        shapes.append(jax.ShapeDtypeStruct((1, count), jnp.float32))
+        scratch += [pltpu.SMEM(array.shape, array.dtype) for array in rates]
+        scratch.append(pltpu.SemaphoreType.DMA((2,)))
     return call(
         kernel,
         "fetch" if spans else "condition",
         shapes,
-        [ANY] * (3 if made else 1),
-        (train, query, precond) if made else (train,),
+        [ANY] * (1 + len(rates) + (2 if made else 0)),
+        (train, *rates, *((query, precond) if made else ())),
         scratch=scratch,
         flops=2 * 512 * sum(width for _, width in spans) * count,
         after=after,
     )
-
-
-def rate_row(learn_rates, ckpt_order, columns, after):
-    def kernel(rates_ref, order_ref, row, rates, order, sems):
-        copies = [
-            pltpu.make_async_copy(rates_ref, rates, sems.at[0]),
-            pltpu.make_async_copy(order_ref, order, sems.at[1]),
-        ]
-        for copy in copies:
-            copy.start()
-        for copy in copies:
-            copy.wait()
-        row[...] = jnp.full(row.shape, rates[order[lax.axis_index("ckpt")]], jnp.float32)
-
-    return call(
-        kernel,
-        "rate_row",
-        [jax.ShapeDtypeStruct((1, columns), jnp.float32)],
-        [ANY, ANY],
-        (learn_rates, ckpt_order),
-        scratch=[
-            pltpu.SMEM(learn_rates.shape, learn_rates.dtype),
-            pltpu.SMEM(ckpt_order.shape, ckpt_order.dtype),
-            pltpu.SemaphoreType.DMA((2,)),
-        ],
-        after=after,
-    )[0]
 
 
 def score(blocks, train, sums=(), picked=(), forward=False, after=()):
@@ -166,6 +157,8 @@
                     outs[i][...] = before[-1][...] + part
             else:
                 outs[i][...] = part
+        if forward:
+            outs[count][...] = given[-1][...]
 
     shapes = [jax.ShapeDtypeStruct((rows, train.shape[0]), jnp.float32)] * count
     if forward:
@@ -248,7 +241,7 @@
         pass
 
     shape = jax.ShapeDtypeStruct(array.shape, array.dtype)
-    return call(kernel, "hand_on", [shape], [VMEM], (array,), after=after, aliases={0: 0})[0]
+    return call(kernel, "hand_on", [shape], [ANY], (array,), after=after, aliases={0: 0}, out_specs=[ANY])[0]
 
 
 def part_pair(if_home, if_not, other, rate, after=()):
@@ -289,13 +282,14 @@
     unit = query.shape[1] // sum(QUARTERS)
     spans = [(unit * sum(QUARTERS[:j]), unit * c) for j, c in enumerate(QUARTERS)]
 
-    (own1,) = fetch(train, [], [], query, precond, spans[:1])
+    own1, own2 = fetch(train, [], [], query, precond, spans[:2])
     two1 = swap(own1, "shard", 2)
     one1 = swap(own1, "shard", 1)
-    (own2,) = fetch(train, [], [own1], query, precond, spans[1:2])
     two2 = swap(own2, "shard", 2)
     one2 = swap(own2, "shard", 1)
-    own3, own4, train1, train2, train3, train4 = fetch(train, spans, [own2], query, precond, spans[2:])
+    own3, own4, train1, train2, train3, train4, rate = fetch(
+        train, spans, [own2], query, precond, spans[2:], (learn_rates, ckpt_order)
+    )
     two3 = swap(own3, "shard", 2)
     two4 = swap(own4, "shard", 2)
     two1 = hand_on(two1, [own4, one1])
@@ -310,8 +304,7 @@
     first4, second4 = deal(own4, two4, [sums[0]])
     first4 = swap(first4, "shard", 1)
     own_sums, one_sums, two_sums, three_sums = sums
-    rate = rate_row(learn_rates, ckpt_order, train.shape[0], [second4])
-    second3 = swap(hand_on(second3, [first3, rate]), "shard", 1)
+    second3 = swap(hand_on(second3, [first3, second4]), "shard", 1)
     own_sums, two_sums, first_sums = score(
         [own3, two3, first3], train3, [own_sums, two_sums], (three_sums, one_sums), after=[second4]
     )
@@ -335,7 +328,7 @@
     unit = query_local.shape[1] // sum(CHUNKS)
     spans = [(unit * sum(CHUNKS[:j]), unit * c) for j, c in enumerate(CHUNKS)]
     own = fetch(train_local, [], [], query_local, precond, spans[:1])
-    held = fetch(train_local, spans[:1], own)
+    *held, rate = fetch(train_local, spans[:1], own, rates=(learn_rates, ckpt_order))
     for span in spans[1:]:
         own += fetch(train_local, [], [held[0], own[-1]], query_local, precond, [span])
 
@@ -353,8 +346,6 @@
             if forward:
                 *total, current[j] = total
         sums += total
-    rate = rate_row(learn_rates, ckpt_order, train_local.shape[0], sums[:1])
-
     sent, kept = sort_out(sums, rate, shards, groups)
     tall = kept.shape[0] // (groups // 2)
     for i in range(groups.bit_length() - 1):

time: 43.9 us -> 43.7 us (level)
  Pallas kernels: 15 us -> 13.4 us
  waiting for transfers between devices: 5.54 us -> 6.52 us
  starting transfers between devices: 22.6 us -> 23.1 us
    pallas_call x20 -> x18, Pallas kernels: 15 us -> 13.4 us  [call(): pl.pallas_call(body, in_specs=specs, out_specs=out_specs or [VMEM] * len(...]
    ppermute x15, waiting for transfers between devices: 5.54 us -> 6.52 us  [swap(): return lax.ppermute(array, axis, [(i, i ^ distance) for i in range(size)])]
    ppermute x15, starting transfers between devices: 22.6 us -> 23.1 us  [swap(): return lax.ppermute(array, axis, [(i, i ^ distance) for i in range(size)])]
  transfers between devices with their start and end apart: 15 -> 15, of which waited for: 7 -> 7; matrix products, arithmetic and copies ran while one was open for 0% -> 0% of each run, Pallas kernels for 31% -> 27%
where the time goes in v5:
time: 43.7 us; the launch traced here: 43.2 us
  starting transfers between devices  23.1 us (53%)
  Pallas kernels  13.4 us (31%)
  waiting for transfers between devices  6.52 us (15%)
    ppermute x15, starting transfers between devices, swap(): return lax.ppermute(array, axis, [(i, i ^ distance) for i in range(size)])  23.1 us
    pallas_call x18, Pallas kernels, call(): pl.pallas_call(body, in_specs=specs, out_specs=out_specs or [VMEM] * len(...  13.4 us
    ppermute x15, waiting for transfers between devices, swap(): return lax.ppermute(array, axis, [(i, i ^ distance) for i in range(size)])  6.52 us
  transfers between devices with their start and end apart: 15, of which 7 were waited for; matrix products, arithmetic and copies ran while one was open for 0% of the time, Pallas kernels for 27%

profile of v5, /device:TPU:1, one launch (start us, length us, event | category | flops | bytes accessed | tf_op | source)
XLA Modules:
  0.0 43.2 jit_solution(5469825950159295280)
XLA Ops:
  0.0 1.1 %condition.1 = (bf16[32,2048]{1,0:T(8,128)(2,1)S(1)}, bf16[32,2048]{1,0:T(8,128)(2,1)S(1)}) custom-call(bf16[768,8192]{1,0:T(8,128)(2,1)} %bitcast.2, f32[32,8192]{1,0:T(8,128)} %bitcast.4, f32[1,8192]{1,0:T(1,128)} %refs_4_.1), custom_call_target="tpu_custom_call" | custom-call | tf_op jit(solution)/shard_map/condition/pallas_call | solution.py:36
  1.1 2.2 %collective-permute-start.4 = (bf16[32,2048]{1,0:T(8,128)(2,1)S(1)}, bf16[32,2048]{1,0:T(8,128)(2,1)S(1)}, u32[]{:S(2)}, u32[]{:S(2)}) collective-permute-start(bf16[32,2048]{1,0:T(8,128)(2,1)S(1)} %get-tuple-element.38.refs_0_), channel_id=1, source_target_pairs={{0,4},{4,0},{8,12},{12,8},{1,5},{5,1},{9,13},{13,9},{2,6},{6,2},{1... | collective-permute-start | bytes 393224 | tf_op jit(solution)/shard_map/ppermute | solution.py:280
  3.3 2.3 %collective-permute-start.3 = (bf16[32,2048]{1,0:T(8,128)(2,1)S(1)}, bf16[32,2048]{1,0:T(8,128)(2,1)S(1)}, u32[]{:S(2)}, u32[]{:S(2)}) collective-permute-start(bf16[32,2048]{1,0:T(8,128)(2,1)S(1)} %get-tuple-element.38.refs_0_), channel_id=1, source_target_pairs={{0,8},{4,12},{8,0},{12,4},{1,9},{5,13},{9,1},{13,5},{2,10},{6,14},... | collective-permute-start | bytes 393224 | tf_op jit(solution)/shard_map/ppermute | solution.py:280
  5.8 4.9 %fetch.1 = (bf16[32,2048]{1,0:T(8,128)(2,1)S(1)}, bf16[32,2048]{1,0:T(8,128)(2,1)S(1)}, bf16[768,2048]{1,0:T(8,128)(2,1)S(1)}, bf16[768,2048]{1,0:T(8,128)(2,1)S...) custom-call(bf16[768,8192]{1,0:T(8,128)(2,1)} %bitcast.3, f32[64]{0:T(128)} %refs_1_.1, ...), custom_call_target="tpu_custom_call" | custom-call | flops 644245120 | tf_op jit(solution)/shard_map/fetch/pallas_call | solution.py:36
  10.8 1.4 %collective-permute-start.6 = (bf16[32,2048]{1,0:T(8,128)(2,1)S(1)}, bf16[32,2048]{1,0:T(8,128)(2,1)S(1)}, u32[]{:S(2)}, u32[]{:S(2)}) collective-permute-start(bf16[32,2048]{1,0:T(8,128)(2,1)S(1)} %hand_on.4.refs_1_.refs_2_), channel_id=1, source_target_pairs={{0,4},{4,0},{8,12},{12,8},{1,5},{5,1},{9,13},{13,9},{2,6},{6,2},{1... | collective-permute-start | bytes 393224 | tf_op jit(solution)/shard_map/ppermute | solution.py:280
  12.2 2.3 %collective-permute-start.7 = (bf16[32,2048]{1,0:T(8,128)(2,1)S(1)}, bf16[32,2048]{1,0:T(8,128)(2,1)S(1)}, u32[]{:S(2)}, u32[]{:S(2)}) collective-permute-start(bf16[32,2048]{1,0:T(8,128)(2,1)S(1)} %get-tuple-element.45.refs_0_), channel_id=1, source_target_pairs={{0,8},{4,12},{8,0},{12,4},{1,9},{5,13},{9,1},{13,5},{2,10},{6,14},... | collective-permute-start | bytes 393224 | tf_op jit(solution)/shard_map/ppermute | solution.py:280
  15.0 2.1 %collective-permute-start.5 = (bf16[32,2048]{1,0:T(8,128)(2,1)S(1)}, bf16[32,2048]{1,0:T(8,128)(2,1)S(1)}, u32[]{:S(2)}, u32[]{:S(2)}) collective-permute-start(bf16[32,2048]{1,0:T(8,128)(2,1)S(1)} %hand_on.5.refs_5_.refs_2_), channel_id=1, source_target_pairs={{0,4},{4,0},{8,12},{12,8},{1,5},{5,1},{9,13},{13,9},{2,6},{6,2},{1... | collective-permute-start | bytes 393224 | tf_op jit(solution)/shard_map/ppermute | solution.py:280
  17.6 1.2 %score.6 = (f32[32,768]{1,0:T(8,128)S(1)}, f32[32,768]{1,0:T(8,128)S(1)}, f32[32,768]{1,0:T(8,128)S(1)}, f32[32,768]{1,0:T(8,128)S(1)}) custom-call(bf16[32,2048]{1,0:T(8,128)(2,1)S(1)} %get-tuple-element.38.refs_0_, bf16[32,2048]{1,0:T(8,128)(2,1)S(1)} %collective-permute-done.4.refs_2_.refs_1_, bf16[32,2048]{1,0:T(8,128)(2,1)S(1)} %hand_on.4.refs_1_.refs_2_, ...), custom_call_target="tpu_custom_call" | custom-call | flops 80530640 | tf_op jit(solution)/shard_map/score/pallas_call | solution.py:36
  18.8 1.6 %collective-permute-done.7.refs_1_ = bf16[32,2048]{1,0:T(8,128)(2,1)S(1)} collective-permute-done((bf16[32,2048]{1,0:T(8,128)(2,1)S(1)}, bf16[32,2048]{1,0:T(8,128)(2,1)S(1)}, u32[]{:S(2)}, u32[]{:S(2)}) %collective-permute-start.7) | collective-permute-done | bytes 131104 | tf_op jit(solution)/shard_map/ppermute | solution.py:280
  20.5 2.4 %collective-permute-start.9 = (bf16[32,2048]{1,0:T(8,128)(2,1)S(1)}, bf16[32,2048]{1,0:T(8,128)(2,1)S(1)}, u32[]{:S(2)}, u32[]{:S(2)}) collective-permute-start(bf16[32,2048]{1,0:T(8,128)(2,1)S(1)} %get-tuple-element.50), channel_id=1, source_target_pairs={{0,4},{4,0},{8,12},{12,8},{1,5},{5,1},{9,13},{13,9},{2,6},{6,2},{1... | collective-permute-start | bytes 393224 | tf_op jit(solution)/shard_map/ppermute | solution.py:280
  22.8 1.3 %collective-permute-done.5.refs_3_ = bf16[32,2048]{1,0:T(8,128)(2,1)S(1)} collective-permute-done((bf16[32,2048]{1,0:T(8,128)(2,1)S(1)}, bf16[32,2048]{1,0:T(8,128)(2,1)S(1)}, u32[]{:S(2)}, u32[]{:S(2)}) %collective-permute-start.5) | collective-permute-done | bytes 131104 | tf_op jit(solution)/shard_map/ppermute | solution.py:280
  24.1 1.2 %score.7 = (f32[32,768]{1,0:T(8,128)S(1)}, f32[32,768]{1,0:T(8,128)S(1)}, f32[32,768]{1,0:T(8,128)S(1)}, f32[32,768]{1,0:T(8,128)S(1)}) custom-call(bf16[32,2048]{1,0:T(8,128)(2,1)S(1)} %get-tuple-element.36.refs_5_.refs_0_, bf16[32,2048]{1,0:T(8,128)(2,1)S(1)} %collective-permute-done.1.refs_2_.refs_1_, bf16[32,2048]{1,0:T(8,128)(2,1)S(1)} %hand_on.5.refs_5_.refs_2_, ...), custom_call_target="tpu_custom_call" | custom-call | flops 80530640 | tf_op jit(solution)/shard_map/score/pallas_call | solution.py:36
  25.3 1.0 %collective-permute-done.refs_1_ = bf16[32,2048]{1,0:T(8,128)(2,1)S(1)} collective-permute-done((bf16[32,2048]{1,0:T(8,128)(2,1)S(1)}, bf16[32,2048]{1,0:T(8,128)(2,1)S(1)}, u32[]{:S(2)}, u32[]{:S(2)}) %collective-permute-start) | collective-permute-done | bytes 131104 | tf_op jit(solution)/shard_map/ppermute | solution.py:280
  26.3 2.2 %collective-permute-start.8 = (bf16[32,2048]{1,0:T(8,128)(2,1)S(1)}, bf16[32,2048]{1,0:T(8,128)(2,1)S(1)}, u32[]{:S(2)}, u32[]{:S(2)}) collective-permute-start(bf16[32,2048]{1,0:T(8,128)(2,1)S(1)} %get-tuple-element.48), channel_id=1, source_target_pairs={{0,4},{4,0},{8,12},{12,8},{1,5},{5,1},{9,13},{13,9},{2,6},{6,2},{1... | collective-permute-start | bytes 393224 | tf_op jit(solution)/shard_map/ppermute | solution.py:280
  28.6 1.7 %collective-permute-start.11 = (bf16[32,2048]{1,0:T(8,128)(2,1)S(1)}, bf16[32,2048]{1,0:T(8,128)(2,1)S(1)}, u32[]{:S(2)}, u32[]{:S(2)}) collective-permute-start(bf16[32,2048]{1,0:T(8,128)(2,1)S(1)} %hand_on.7), channel_id=1, source_target_pairs={{0,4},{4,0},{8,12},{12,8},{1,5},{5,1},{9,13},{13,9},{2,6},{6,2},{1... | collective-permute-start | bytes 393224 | tf_op jit(solution)/shard_map/ppermute | solution.py:280
  30.4 1.1 %score.8 = (f32[32,768]{1,0:T(8,128)S(1)}, f32[32,768]{1,0:T(8,128)S(1)}, f32[32,768]{1,0:T(8,128)S(1)}) custom-call(bf16[32,2048]{1,0:T(8,128)(2,1)S(1)} %get-tuple-element.45.refs_0_, bf16[32,2048]{1,0:T(8,128)(2,1)S(1)} %collective-permute-done.7.refs_1_, bf16[32,2048]{1,0:T(8,128)(2,1)S(1)} %collective-permute-done.9.refs_2_.refs_1_, ...), custom_call_target="tpu_custom_call" | custom-call | flops 80530640 | tf_op jit(solution)/shard_map/score/pallas_call | solution.py:36
  31.6 1.1 %score.9 = (f32[32,768]{1,0:T(8,128)S(1)}, f32[32,768]{1,0:T(8,128)S(1)}, f32[32,768]{1,0:T(8,128)S(1)}) custom-call(bf16[32,2048]{1,0:T(8,128)(2,1)S(1)} %get-tuple-element.37.refs_1_.refs_0_, bf16[32,2048]{1,0:T(8,128)(2,1)S(1)} %collective-permute-done.refs_1_, bf16[32,2048]{1,0:T(8,128)(2,1)S(1)} %collective-permute-done.8.refs_2_, ...), custom_call_target="tpu_custom_call" | custom-call | flops 80530640 | tf_op jit(solution)/shard_map/score/pallas_call | solution.py:36
  32.7 3.8 %collective-permute-start.12 = (f32[32,768]{1,0:T(8,128)S(1)}, f32[32,768]{1,0:T(8,128)S(1)}, u32[]{:S(2)}, u32[]{:S(2)}) collective-permute-start(f32[32,768]{1,0:T(8,128)S(1)} %get-tuple-element.64), channel_id=1, source_target_pairs={{0,1},{1,0},{2,3},{3,2},{4,5},{5,4},{6,7},{7,6},{8,9},{9,8},{10,11... | collective-permute-start | bytes 294920 | tf_op jit(solution)/shard_map/ppermute | solution.py:280
  36.6 0.9 %collective-permute-done.12.refs_1_ = f32[32,768]{1,0:T(8,128)S(1)} collective-permute-done((f32[32,768]{1,0:T(8,128)S(1)}, f32[32,768]{1,0:T(8,128)S(1)}, u32[]{:S(2)}, u32[]{:S(2)}) %collective-permute-start.12) | collective-permute-done | bytes 98336 | tf_op jit(solution)/shard_map/ppermute | solution.py:280
  37.5 1.3 %collective-permute-start.13 = (f32[32,768]{1,0:T(8,128)S(1)}, f32[32,768]{1,0:T(8,128)S(1)}, u32[]{:S(2)}, u32[]{:S(2)}) collective-permute-start(f32[32,768]{1,0:T(8,128)S(1)} %add.2.refs_4_), channel_id=1, source_target_pairs={{0,2},{2,0},{1,3},{3,1},{4,6},{6,4},{5,7},{7,5},{8,10},{10,8},{9,1... | collective-permute-start | bytes 294920 | tf_op jit(solution)/shard_map/ppermute | solution.py:280
  38.8 1.0 %score.10.refs_2_ = f32[32,768]{1,0:T(8,128)S(1)} custom-call(bf16[32,2048]{1,0:T(8,128)(2,1)S(1)} %collective-permute-done.11.refs_0_, bf16[768,2048]{1,0:T(8,128)(2,1)S(1)} %get-tuple-element.51.refs_3_.refs_1_, f32[32,768]{1,0:T(8,128)S(1)} %get-tuple-element.54.refs_7_.refs_2_, f32[32,768]{1,0:T(8,128)S(1)} %get-tuple-element.53.refs_6_.refs_3_, ...), custom_call_target="tpu_custom_call" | custom-call | flops 80530640 | tf_op jit(solution)/shard_map/score/pallas_call | solution.py:36
  39.8 1.0 %score.11.refs_2_ = f32[32,768]{1,0:T(8,128)S(1)} custom-call(bf16[32,2048]{1,0:T(8,128)(2,1)S(1)} %collective-permute-done.10.refs_0_, bf16[768,2048]{1,0:T(8,128)(2,1)S(1)} %get-tuple-element.49.refs_3_.refs_1_, f32[32,768]{1,0:T(8,128)S(1)} %score.10.refs_2_), custom_call_target="tpu_custom_call" | custom-call | flops 80530640 | tf_op jit(solution)/shard_map/score/pallas_call | solution.py:36
  40.9 0.7 %collective-permute-start.14 = (f32[32,768]{1,0:T(8,128)S(1)}, f32[32,768]{1,0:T(8,128)S(1)}, u32[]{:S(2)}, u32[]{:S(2)}) collective-permute-start(f32[32,768]{1,0:T(8,128)S(1)} %get-tuple-element.66), channel_id=1, source_target_pairs={{0,1},{1,0},{2,3},{3,2},{4,5},{5,4},{6,7},{7,6},{8,9},{9,8},{10,11... | collective-permute-start | bytes 294920 | tf_op jit(solution)/shard_map/ppermute | solution.py:280
  41.6 0.9 %collective-permute-done.14.refs_2_ = f32[32,768]{1,0:T(8,128)S(1)} collective-permute-done((f32[32,768]{1,0:T(8,128)S(1)}, f32[32,768]{1,0:T(8,128)S(1)}, u32[]{:S(2)}, u32[]{:S(2)}) %collective-permute-start.14) | collective-permute-done | bytes 98336 | tf_op jit(solution)/shard_map/ppermute | solution.py:280
  (24 shorter events, 2.3 us)
Async XLA Ops:
  1.1 9.6 %collective-permute-start.4 = (bf16[32,2048]{1,0:T(8,128)(2,1)S(1)}, bf16[32,2048]{1,0:T(8,128)(2,1)S(1)}, u32[]{:S(2)}, u32[]{:S(2)}) collective-permute-start(bf16[32,2048]{1,0:T(8,128)(2,1)S(1)} %get-tuple-element.38.refs_0_), channel_id=1, source_target_pairs={{0,4},{4,0},{8,12},{12,8},{1,5},{5,1},{9,13},{13,9},{2,6},{6,2},{1... | collective-permute-start | bytes 393224 | tf_op jit(solution)/shard_map/ppermute | solution.py:280
  3.3 7.4 %collective-permute-start.3 = (bf16[32,2048]{1,0:T(8,128)(2,1)S(1)}, bf16[32,2048]{1,0:T(8,128)(2,1)S(1)}, u32[]{:S(2)}, u32[]{:S(2)}) collective-permute-start(bf16[32,2048]{1,0:T(8,128)(2,1)S(1)} %get-tuple-element.38.refs_0_), channel_id=1, source_target_pairs={{0,8},{4,12},{8,0},{12,4},{1,9},{5,13},{9,1},{13,5},{2,10},{6,14},... | collective-permute-start | bytes 393224 | tf_op jit(solution)/shard_map/ppermute | solution.py:280
  5.6 8.9 %collective-permute-start.1 = (bf16[32,2048]{1,0:T(8,128)(2,1)S(1)}, bf16[32,2048]{1,0:T(8,128)(2,1)S(1)}, u32[]{:S(2)}, u32[]{:S(2)}) collective-permute-start(bf16[32,2048]{1,0:T(8,128)(2,1)S(1)} %get-tuple-element.36.refs_5_.refs_0_), channel_id=1, source_target_pairs={{0,4},{4,0},{8,12},{12,8},{1,5},{5,1},{9,13},{13,9},{2,6},{6,2},{1... | collective-permute-start | bytes 393224 | tf_op jit(solution)/shard_map/ppermute | solution.py:280
  5.8 9.2 %collective-permute-start.2 = (bf16[32,2048]{1,0:T(8,128)(2,1)S(1)}, bf16[32,2048]{1,0:T(8,128)(2,1)S(1)}, u32[]{:S(2)}, u32[]{:S(2)}) collective-permute-start(bf16[32,2048]{1,0:T(8,128)(2,1)S(1)} %get-tuple-element.36.refs_5_.refs_0_), channel_id=1, source_target_pairs={{0,8},{4,12},{8,0},{12,4},{1,9},{5,13},{9,1},{13,5},{2,10},{6,14},... | collective-permute-start | bytes 393224 | tf_op jit(solution)/shard_map/ppermute | solution.py:280
  10.8 6.8 %collective-permute-start.6 = (bf16[32,2048]{1,0:T(8,128)(2,1)S(1)}, bf16[32,2048]{1,0:T(8,128)(2,1)S(1)}, u32[]{:S(2)}, u32[]{:S(2)}) collective-permute-start(bf16[32,2048]{1,0:T(8,128)(2,1)S(1)} %hand_on.4.refs_1_.refs_2_), channel_id=1, source_target_pairs={{0,4},{4,0},{8,12},{12,8},{1,5},{5,1},{9,13},{13,9},{2,6},{6,2},{1... | collective-permute-start | bytes 393224 | tf_op jit(solution)/shard_map/ppermute | solution.py:280
  12.2 8.2 %collective-permute-start.7 = (bf16[32,2048]{1,0:T(8,128)(2,1)S(1)}, bf16[32,2048]{1,0:T(8,128)(2,1)S(1)}, u32[]{:S(2)}, u32[]{:S(2)}) collective-permute-start(bf16[32,2048]{1,0:T(8,128)(2,1)S(1)} %get-tuple-element.45.refs_0_), channel_id=1, source_target_pairs={{0,8},{4,12},{8,0},{12,4},{1,9},{5,13},{9,1},{13,5},{2,10},{6,14},... | collective-permute-start | bytes 393224 | tf_op jit(solution)/shard_map/ppermute | solution.py:280
  15.0 9.1 %collective-permute-start.5 = (bf16[32,2048]{1,0:T(8,128)(2,1)S(1)}, bf16[32,2048]{1,0:T(8,128)(2,1)S(1)}, u32[]{:S(2)}, u32[]{:S(2)}) collective-permute-start(bf16[32,2048]{1,0:T(8,128)(2,1)S(1)} %hand_on.5.refs_5_.refs_2_), channel_id=1, source_target_pairs={{0,4},{4,0},{8,12},{12,8},{1,5},{5,1},{9,13},{13,9},{2,6},{6,2},{1... | collective-permute-start | bytes 393224 | tf_op jit(solution)/shard_map/ppermute | solution.py:280
  17.1 9.1 %collective-permute-start = (bf16[32,2048]{1,0:T(8,128)(2,1)S(1)}, bf16[32,2048]{1,0:T(8,128)(2,1)S(1)}, u32[]{:S(2)}, u32[]{:S(2)}) collective-permute-start(bf16[32,2048]{1,0:T(8,128)(2,1)S(1)} %get-tuple-element.37.refs_1_.refs_0_), channel_id=1, source_target_pairs={{0,8},{4,12},{8,0},{12,4},{1,9},{5,13},{9,1},{13,5},{2,10},{6,14},... | collective-permute-start | bytes 393224 | tf_op jit(solution)/shard_map/ppermute | solution.py:280
  20.5 8.2 %collective-permute-start.9 = (bf16[32,2048]{1,0:T(8,128)(2,1)S(1)}, bf16[32,2048]{1,0:T(8,128)(2,1)S(1)}, u32[]{:S(2)}, u32[]{:S(2)}) collective-permute-start(bf16[32,2048]{1,0:T(8,128)(2,1)S(1)} %get-tuple-element.50), channel_id=1, source_target_pairs={{0,4},{4,0},{8,12},{12,8},{1,5},{5,1},{9,13},{13,9},{2,6},{6,2},{1... | collective-permute-start | bytes 393224 | tf_op jit(solution)/shard_map/ppermute | solution.py:280
  26.3 5.3 %collective-permute-start.8 = (bf16[32,2048]{1,0:T(8,128)(2,1)S(1)}, bf16[32,2048]{1,0:T(8,128)(2,1)S(1)}, u32[]{:S(2)}, u32[]{:S(2)}) collective-permute-start(bf16[32,2048]{1,0:T(8,128)(2,1)S(1)} %get-tuple-element.48), channel_id=1, source_target_pairs={{0,4},{4,0},{8,12},{12,8},{1,5},{5,1},{9,13},{13,9},{2,6},{6,2},{1... | collective-permute-start | bytes 393224 | tf_op jit(solution)/shard_map/ppermute | solution.py:280
  28.6 10.1 %collective-permute-start.11 = (bf16[32,2048]{1,0:T(8,128)(2,1)S(1)}, bf16[32,2048]{1,0:T(8,128)(2,1)S(1)}, u32[]{:S(2)}, u32[]{:S(2)}) collective-permute-start(bf16[32,2048]{1,0:T(8,128)(2,1)S(1)} %hand_on.7), channel_id=1, source_target_pairs={{0,4},{4,0},{8,12},{12,8},{1,5},{5,1},{9,13},{13,9},{2,6},{6,2},{1... | collective-permute-start | bytes 393224 | tf_op jit(solution)/shard_map/ppermute | solution.py:280
  31.5 8.3 %collective-permute-start.10 = (bf16[32,2048]{1,0:T(8,128)(2,1)S(1)}, bf16[32,2048]{1,0:T(8,128)(2,1)S(1)}, u32[]{:S(2)}, u32[]{:S(2)}) collective-permute-start(bf16[32,2048]{1,0:T(8,128)(2,1)S(1)} %hand_on.6), channel_id=1, source_target_pairs={{0,4},{4,0},{8,12},{12,8},{1,5},{5,1},{9,13},{13,9},{2,6},{6,2},{1... | collective-permute-start | bytes 393224 | tf_op jit(solution)/shard_map/ppermute | solution.py:280
  32.7 4.8 %collective-permute-start.12 = (f32[32,768]{1,0:T(8,128)S(1)}, f32[32,768]{1,0:T(8,128)S(1)}, u32[]{:S(2)}, u32[]{:S(2)}) collective-permute-start(f32[32,768]{1,0:T(8,128)S(1)} %get-tuple-element.64), channel_id=1, source_target_pairs={{0,1},{1,0},{2,3},{3,2},{4,5},{5,4},{6,7},{7,6},{8,9},{9,8},{10,11... | collective-permute-start | bytes 294920 | tf_op jit(solution)/shard_map/ppermute | solution.py:280
  37.5 4.1 %collective-permute-start.13 = (f32[32,768]{1,0:T(8,128)S(1)}, f32[32,768]{1,0:T(8,128)S(1)}, u32[]{:S(2)}, u32[]{:S(2)}) collective-permute-start(f32[32,768]{1,0:T(8,128)S(1)} %add.2.refs_4_), channel_id=1, source_target_pairs={{0,2},{2,0},{1,3},{3,1},{4,6},{6,4},{5,7},{7,5},{8,10},{10,8},{9,1... | collective-permute-start | bytes 294920 | tf_op jit(solution)/shard_map/ppermute | solution.py:280
  40.9 1.7 %collective-permute-start.14 = (f32[32,768]{1,0:T(8,128)S(1)}, f32[32,768]{1,0:T(8,128)S(1)}, u32[]{:S(2)}, u32[]{:S(2)}) collective-permute-start(f32[32,768]{1,0:T(8,128)S(1)} %get-tuple-element.66), channel_id=1, source_target_pairs={{0,1},{1,0},{2,3},{3,2},{4,5},{5,4},{6,7},{7,6},{8,9},{9,8},{10,11... | collective-permute-start | bytes 294920 | tf_op jit(solution)/shard_map/ppermute | solution.py:280

commit v6 on v5

--- a/solution.py
+++ b/solution.py
@@ -244,23 +244,38 @@
     return call(kernel, "hand_on", [shape], [ANY], (array,), after=after, aliases={0: 0}, out_specs=[ANY])[0]
 
 
-def part_pair(if_home, if_not, other, rate, after=()):
-    def kernel(home_ref, not_ref, other_ref, rate_ref, sent, kept):
+def score_and_part(blocks, train, sums, rate, near=(), after=()):
+    count = len(blocks)
+    rows = blocks[0].shape[0]
+    args = [*blocks, train, *sums, rate, *near]
+
+    def kernel(*refs):
+        given, train_ref, before = refs[:count], refs[count], refs[count + 1 : 2 * count + 1]
+        rate_ref, pair, outs = refs[2 * count + 1], refs[2 * count + 2 : len(args)], refs[len(args) :]
+        *totals_out, sent, kept = outs
+        stacked = given[0][...] if count == 1 else jnp.concatenate([ref[...] for ref in given], axis=0)
+        scores = times(stacked, train_ref[...])
+        for i, out in enumerate(totals_out):
+            out[...] = before[i][...] + scores[i * rows : (i + 1) * rows]
+        last = (before[-1][...] + scores[(count - 1) * rows :]) * rate_ref[...]
         home, agree = my_pair()
-        for one, ref in ((home, home_ref), (jnp.logical_not(home), not_ref)):
+        at_home, elsewhere = pair or (totals_out[1], totals_out[0])
+        for one, ref in ((home, at_home), (jnp.logical_not(home), elsewhere)):
 
             @pl.when(jnp.logical_and(one, agree))
             def _():
                 kept[...] = ref[...] * rate_ref[...]
-                sent[...] = other_ref[...] * rate_ref[...]
+                sent[...] = last
 
             @pl.when(jnp.logical_and(one, jnp.logical_not(agree)))
             def _():
                 sent[...] = ref[...] * rate_ref[...]
-                kept[...] = other_ref[...] * rate_ref[...]
-
-    shape = jax.ShapeDtypeStruct(other.shape, jnp.float32)
-    return call(kernel, "part_pair", [shape] * 2, [VMEM] * 4, (if_home, if_not, other, rate), after=after)
+                kept[...] = last
+
+    shape = jax.ShapeDtypeStruct((rows, train.shape[0]), jnp.float32)
+    flops = 2 * 256 * train.shape[1] * train.shape[0]
+    shapes = [shape] * (2 + (0 if near else count - 1))
+    return call(kernel, "score_and_part", shapes, [VMEM] * len(args), args, flops=flops, after=after)
 
 
 def add(*arrays):
@@ -309,14 +324,13 @@
         [own3, two3, first3], train3, [own_sums, two_sums], (three_sums, one_sums), after=[second4]
     )
     second4 = swap(hand_on(second4, [own_sums]), "shard", 1)
-    own_sums, two_sums, first_sums = score([own4, two4, first4], train4, [own_sums, two_sums, first_sums])
-
-    sent, kept = part_pair(two_sums, own_sums, first_sums, rate)
+    own_sums, two_sums, sent, kept = score_and_part(
+        [own4, two4, first4], train4, [own_sums, two_sums, first_sums], rate
+    )
     across = add(kept, swap(sent, "sub", 1))
     from_far = swap(across, "ckpt", 1)
     (second_sums,) = score([second3], train3, picked=(one_sums, three_sums), after=[across])
-    (second_sums,) = score([second4], train4, [second_sums])
-    sent, kept = part_pair(own_sums, two_sums, second_sums, rate)
+    sent, kept = score_and_part([second4], train4, [second_sums], rate, (own_sums, two_sums))
     return add(kept, from_far, swap(sent, "sub", 1))
 
 

time: 43.7 us -> 43.7 us (level)
    pallas_call x18 -> x16, Pallas kernels: 13.4 us -> 13.4 us  [call(): pl.pallas_call(body, in_specs=specs, out_specs=out_specs or [VMEM] * len(...]
where the time goes in v6:
time: 43.7 us; the launch traced here: 43.2 us
  starting transfers between devices  23.1 us (53%)
  Pallas kernels  13.4 us (31%)
  waiting for transfers between devices  6.52 us (15%)
    ppermute x15, starting transfers between devices, swap(): return lax.ppermute(array, axis, [(i, i ^ distance) for i in range(size)])  23.1 us
    pallas_call x16, Pallas kernels, call(): pl.pallas_call(body, in_specs=specs, out_specs=out_specs or [VMEM] * len(...  13.4 us
    ppermute x15, waiting for transfers between devices, swap(): return lax.ppermute(array, axis, [(i, i ^ distance) for i in range(size)])  6.52 us
  transfers between devices with their start and end apart: 15, of which 7 were waited for; matrix products, arithmetic and copies ran while one was open for 0% of the time, Pallas kernels for 27%

profile of v6, /device:TPU:1, one launch (start us, length us, event | category | flops | bytes accessed | tf_op | source)
XLA Modules:
  0.0 43.2 jit_solution(15500089004893085711)
XLA Ops:
  0.0 1.1 %condition.1 = (bf16[32,2048]{1,0:T(8,128)(2,1)S(1)}, bf16[32,2048]{1,0:T(8,128)(2,1)S(1)}) custom-call(bf16[768,8192]{1,0:T(8,128)(2,1)} %bitcast.2, f32[32,8192]{1,0:T(8,128)} %bitcast.4, f32[1,8192]{1,0:T(1,128)} %refs_4_.1), custom_call_target="tpu_custom_call" | custom-call | tf_op jit(solution)/shard_map/condition/pallas_call | solution.py:36
  1.1 2.2 %collective-permute-start.4 = (bf16[32,2048]{1,0:T(8,128)(2,1)S(1)}, bf16[32,2048]{1,0:T(8,128)(2,1)S(1)}, u32[]{:S(2)}, u32[]{:S(2)}) collective-permute-start(bf16[32,2048]{1,0:T(8,128)(2,1)S(1)} %get-tuple-element.37.refs_0_), channel_id=1, source_target_pairs={{0,4},{4,0},{8,12},{12,8},{1,5},{5,1},{9,13},{13,9},{2,6},{6,2},{1... | collective-permute-start | bytes 393224 | tf_op jit(solution)/shard_map/ppermute | solution.py:295
  3.3 2.3 %collective-permute-start.3 = (bf16[32,2048]{1,0:T(8,128)(2,1)S(1)}, bf16[32,2048]{1,0:T(8,128)(2,1)S(1)}, u32[]{:S(2)}, u32[]{:S(2)}) collective-permute-start(bf16[32,2048]{1,0:T(8,128)(2,1)S(1)} %get-tuple-element.37.refs_0_), channel_id=1, source_target_pairs={{0,8},{4,12},{8,0},{12,4},{1,9},{5,13},{9,1},{13,5},{2,10},{6,14},... | collective-permute-start | bytes 393224 | tf_op jit(solution)/shard_map/ppermute | solution.py:295
  5.8 4.9 %fetch.1 = (bf16[32,2048]{1,0:T(8,128)(2,1)S(1)}, bf16[32,2048]{1,0:T(8,128)(2,1)S(1)}, bf16[768,2048]{1,0:T(8,128)(2,1)S(1)}, bf16[768,2048]{1,0:T(8,128)(2,1)S...) custom-call(bf16[768,8192]{1,0:T(8,128)(2,1)} %bitcast.3, f32[64]{0:T(128)} %refs_1_.1, ...), custom_call_target="tpu_custom_call" | custom-call | flops 644245120 | tf_op jit(solution)/shard_map/fetch/pallas_call | solution.py:36
  10.8 1.4 %collective-permute-start.6 = (bf16[32,2048]{1,0:T(8,128)(2,1)S(1)}, bf16[32,2048]{1,0:T(8,128)(2,1)S(1)}, u32[]{:S(2)}, u32[]{:S(2)}) collective-permute-start(bf16[32,2048]{1,0:T(8,128)(2,1)S(1)} %hand_on.4.refs_1_.refs_2_), channel_id=1, source_target_pairs={{0,4},{4,0},{8,12},{12,8},{1,5},{5,1},{9,13},{13,9},{2,6},{6,2},{1... | collective-permute-start | bytes 393224 | tf_op jit(solution)/shard_map/ppermute | solution.py:295
  12.2 2.3 %collective-permute-start.7 = (bf16[32,2048]{1,0:T(8,128)(2,1)S(1)}, bf16[32,2048]{1,0:T(8,128)(2,1)S(1)}, u32[]{:S(2)}, u32[]{:S(2)}) collective-permute-start(bf16[32,2048]{1,0:T(8,128)(2,1)S(1)} %get-tuple-element.44.refs_0_), channel_id=1, source_target_pairs={{0,8},{4,12},{8,0},{12,4},{1,9},{5,13},{9,1},{13,5},{2,10},{6,14},... | collective-permute-start | bytes 393224 | tf_op jit(solution)/shard_map/ppermute | solution.py:295
  15.0 2.1 %collective-permute-start.5 = (bf16[32,2048]{1,0:T(8,128)(2,1)S(1)}, bf16[32,2048]{1,0:T(8,128)(2,1)S(1)}, u32[]{:S(2)}, u32[]{:S(2)}) collective-permute-start(bf16[32,2048]{1,0:T(8,128)(2,1)S(1)} %hand_on.5.refs_5_.refs_2_), channel_id=1, source_target_pairs={{0,4},{4,0},{8,12},{12,8},{1,5},{5,1},{9,13},{13,9},{2,6},{6,2},{1... | collective-permute-start | bytes 393224 | tf_op jit(solution)/shard_map/ppermute | solution.py:295
  17.6 1.2 %score.4 = (f32[32,768]{1,0:T(8,128)S(1)}, f32[32,768]{1,0:T(8,128)S(1)}, f32[32,768]{1,0:T(8,128)S(1)}, f32[32,768]{1,0:T(8,128)S(1)}) custom-call(bf16[32,2048]{1,0:T(8,128)(2,1)S(1)} %get-tuple-element.37.refs_0_, bf16[32,2048]{1,0:T(8,128)(2,1)S(1)} %collective-permute-done.4.refs_2_.refs_1_, bf16[32,2048]{1,0:T(8,128)(2,1)S(1)} %hand_on.4.refs_1_.refs_2_, ...), custom_call_target="tpu_custom_call" | custom-call | flops 80530640 | tf_op jit(solution)/shard_map/score/pallas_call | solution.py:36
  18.8 1.6 %collective-permute-done.7.refs_1_ = bf16[32,2048]{1,0:T(8,128)(2,1)S(1)} collective-permute-done((bf16[32,2048]{1,0:T(8,128)(2,1)S(1)}, bf16[32,2048]{1,0:T(8,128)(2,1)S(1)}, u32[]{:S(2)}, u32[]{:S(2)}) %collective-permute-start.7) | collective-permute-done | bytes 131104 | tf_op jit(solution)/shard_map/ppermute | solution.py:295
  20.5 2.4 %collective-permute-start.8 = (bf16[32,2048]{1,0:T(8,128)(2,1)S(1)}, bf16[32,2048]{1,0:T(8,128)(2,1)S(1)}, u32[]{:S(2)}, u32[]{:S(2)}) collective-permute-start(bf16[32,2048]{1,0:T(8,128)(2,1)S(1)} %get-tuple-element.48), channel_id=1, source_target_pairs={{0,4},{4,0},{8,12},{12,8},{1,5},{5,1},{9,13},{13,9},{2,6},{6,2},{1... | collective-permute-start | bytes 393224 | tf_op jit(solution)/shard_map/ppermute | solution.py:295
  22.8 1.3 %collective-permute-done.5.refs_3_ = bf16[32,2048]{1,0:T(8,128)(2,1)S(1)} collective-permute-done((bf16[32,2048]{1,0:T(8,128)(2,1)S(1)}, bf16[32,2048]{1,0:T(8,128)(2,1)S(1)}, u32[]{:S(2)}, u32[]{:S(2)}) %collective-permute-start.5) | collective-permute-done | bytes 131104 | tf_op jit(solution)/shard_map/ppermute | solution.py:295
  24.1 1.2 %score.5 = (f32[32,768]{1,0:T(8,128)S(1)}, f32[32,768]{1,0:T(8,128)S(1)}, f32[32,768]{1,0:T(8,128)S(1)}, f32[32,768]{1,0:T(8,128)S(1)}) custom-call(bf16[32,2048]{1,0:T(8,128)(2,1)S(1)} %get-tuple-element.35.refs_5_.refs_0_, bf16[32,2048]{1,0:T(8,128)(2,1)S(1)} %collective-permute-done.1.refs_2_.refs_1_, bf16[32,2048]{1,0:T(8,128)(2,1)S(1)} %hand_on.5.refs_5_.refs_2_, ...), custom_call_target="tpu_custom_call" | custom-call | flops 80530640 | tf_op jit(solution)/shard_map/score/pallas_call | solution.py:36
  25.3 1.0 %collective-permute-done.refs_1_ = bf16[32,2048]{1,0:T(8,128)(2,1)S(1)} collective-permute-done((bf16[32,2048]{1,0:T(8,128)(2,1)S(1)}, bf16[32,2048]{1,0:T(8,128)(2,1)S(1)}, u32[]{:S(2)}, u32[]{:S(2)}) %collective-permute-start) | collective-permute-done | bytes 131104 | tf_op jit(solution)/shard_map/ppermute | solution.py:295
  26.3 2.2 %collective-permute-start.11 = (bf16[32,2048]{1,0:T(8,128)(2,1)S(1)}, bf16[32,2048]{1,0:T(8,128)(2,1)S(1)}, u32[]{:S(2)}, u32[]{:S(2)}) collective-permute-start(bf16[32,2048]{1,0:T(8,128)(2,1)S(1)} %get-tuple-element.55), channel_id=1, source_target_pairs={{0,4},{4,0},{8,12},{12,8},{1,5},{5,1},{9,13},{13,9},{2,6},{6,2},{1... | collective-permute-start | bytes 393224 | tf_op jit(solution)/shard_map/ppermute | solution.py:295
  28.6 1.7 %collective-permute-start.10 = (bf16[32,2048]{1,0:T(8,128)(2,1)S(1)}, bf16[32,2048]{1,0:T(8,128)(2,1)S(1)}, u32[]{:S(2)}, u32[]{:S(2)}) collective-permute-start(bf16[32,2048]{1,0:T(8,128)(2,1)S(1)} %hand_on.7), channel_id=1, source_target_pairs={{0,4},{4,0},{8,12},{12,8},{1,5},{5,1},{9,13},{13,9},{2,6},{6,2},{1... | collective-permute-start | bytes 393224 | tf_op jit(solution)/shard_map/ppermute | solution.py:295
  30.4 1.1 %score.6 = (f32[32,768]{1,0:T(8,128)S(1)}, f32[32,768]{1,0:T(8,128)S(1)}, f32[32,768]{1,0:T(8,128)S(1)}) custom-call(bf16[32,2048]{1,0:T(8,128)(2,1)S(1)} %get-tuple-element.44.refs_0_, bf16[32,2048]{1,0:T(8,128)(2,1)S(1)} %collective-permute-done.7.refs_1_, bf16[32,2048]{1,0:T(8,128)(2,1)S(1)} %collective-permute-done.8.refs_2_.refs_1_, ...), custom_call_target="tpu_custom_call" | custom-call | flops 80530640 | tf_op jit(solution)/shard_map/score/pallas_call | solution.py:36
  31.6 1.1 %score_and_part.2 = (f32[32,768]{1,0:T(8,128)S(1)}, f32[32,768]{1,0:T(8,128)S(1)}, f32[32,768]{1,0:T(8,128)S(1)}, f32[32,768]{1,0:T(8,128)S(1)}) custom-call(bf16[32,2048]{1,0:T(8,128)(2,1)S(1)} %get-tuple-element.36.refs_1_.refs_0_, bf16[32,2048]{1,0:T(8,128)(2,1)S(1)} %collective-permute-done.refs_1_, ...), custom_call_target="tpu_custom_call" | custom-call | flops 80530640 | tf_op jit(solution)/shard_map/score_and_part/pallas_call | solution.py:36
  32.7 3.8 %collective-permute-start.12 = (f32[32,768]{1,0:T(8,128)S(1)}, f32[32,768]{1,0:T(8,128)S(1)}, u32[]{:S(2)}, u32[]{:S(2)}) collective-permute-start(f32[32,768]{1,0:T(8,128)S(1)} %get-tuple-element.60), channel_id=1, source_target_pairs={{0,1},{1,0},{2,3},{3,2},{4,5},{5,4},{6,7},{7,6},{8,9},{9,8},{10,11... | collective-permute-start | bytes 294920 | tf_op jit(solution)/shard_map/ppermute | solution.py:295
  36.5 0.9 %collective-permute-done.12.refs_1_ = f32[32,768]{1,0:T(8,128)S(1)} collective-permute-done((f32[32,768]{1,0:T(8,128)S(1)}, f32[32,768]{1,0:T(8,128)S(1)}, u32[]{:S(2)}, u32[]{:S(2)}) %collective-permute-start.12) | collective-permute-done | bytes 98336 | tf_op jit(solution)/shard_map/ppermute | solution.py:295
  37.5 1.3 %collective-permute-start.13 = (f32[32,768]{1,0:T(8,128)S(1)}, f32[32,768]{1,0:T(8,128)S(1)}, u32[]{:S(2)}, u32[]{:S(2)}) collective-permute-start(f32[32,768]{1,0:T(8,128)S(1)} %add.2.refs_4_), channel_id=1, source_target_pairs={{0,2},{2,0},{1,3},{3,1},{4,6},{6,4},{5,7},{7,5},{8,10},{10,8},{9,1... | collective-permute-start | bytes 294920 | tf_op jit(solution)/shard_map/ppermute | solution.py:295
  38.8 1.0 %score.7.refs_2_ = f32[32,768]{1,0:T(8,128)S(1)} custom-call(bf16[32,2048]{1,0:T(8,128)(2,1)S(1)} %collective-permute-done.10.refs_0_, bf16[768,2048]{1,0:T(8,128)(2,1)S(1)} %get-tuple-element.49.refs_3_.refs_1_, f32[32,768]{1,0:T(8,128)S(1)} %get-tuple-element.52.refs_7_.refs_2_, f32[32,768]{1,0:T(8,128)S(1)} %get-tuple-element.51.refs_6_.refs_3_, ...), custom_call_target="tpu_custom_call" | custom-call | flops 80530640 | tf_op jit(solution)/shard_map/score/pallas_call | solution.py:36
  39.8 1.1 %score_and_part.3 = (f32[32,768]{1,0:T(8,128)S(1)}, f32[32,768]{1,0:T(8,128)S(1)}) custom-call(bf16[32,2048]{1,0:T(8,128)(2,1)S(1)} %collective-permute-done.9.refs_0_, bf16[768,2048]{1,0:T(8,128)(2,1)S(1)} %get-tuple-element.54.refs_3_.refs_1_, f32[32,768]{1,0:T(8,128)S(1)} %score.7.refs_2_, f32[1,768]{1,0:T(1,128)S(1)} %get-tuple-element.58.refs_7_.refs_3_, ...), custom_call_target="tpu_custom_call" | custom-call | flops 80530640 | tf_op jit(solution)/shard_map/score_and_part/pallas_call | solution.py:36
  40.9 0.7 %collective-permute-start.14 = (f32[32,768]{1,0:T(8,128)S(1)}, f32[32,768]{1,0:T(8,128)S(1)}, u32[]{:S(2)}, u32[]{:S(2)}) collective-permute-start(f32[32,768]{1,0:T(8,128)S(1)} %get-tuple-element.64), channel_id=1, source_target_pairs={{0,1},{1,0},{2,3},{3,2},{4,5},{5,4},{6,7},{7,6},{8,9},{9,8},{10,11... | collective-permute-start | bytes 294920 | tf_op jit(solution)/shard_map/ppermute | solution.py:295
  41.6 0.9 %collective-permute-done.14.refs_2_ = f32[32,768]{1,0:T(8,128)S(1)} collective-permute-done((f32[32,768]{1,0:T(8,128)S(1)}, f32[32,768]{1,0:T(8,128)S(1)}, u32[]{:S(2)}, u32[]{:S(2)}) %collective-permute-start.14) | collective-permute-done | bytes 98336 | tf_op jit(solution)/shard_map/ppermute | solution.py:295
  (22 shorter events, 2.2 us)
Async XLA Ops:
  1.1 9.6 %collective-permute-start.4 = (bf16[32,2048]{1,0:T(8,128)(2,1)S(1)}, bf16[32,2048]{1,0:T(8,128)(2,1)S(1)}, u32[]{:S(2)}, u32[]{:S(2)}) collective-permute-start(bf16[32,2048]{1,0:T(8,128)(2,1)S(1)} %get-tuple-element.37.refs_0_), channel_id=1, source_target_pairs={{0,4},{4,0},{8,12},{12,8},{1,5},{5,1},{9,13},{13,9},{2,6},{6,2},{1... | collective-permute-start | bytes 393224 | tf_op jit(solution)/shard_map/ppermute | solution.py:295
  3.3 7.4 %collective-permute-start.3 = (bf16[32,2048]{1,0:T(8,128)(2,1)S(1)}, bf16[32,2048]{1,0:T(8,128)(2,1)S(1)}, u32[]{:S(2)}, u32[]{:S(2)}) collective-permute-start(bf16[32,2048]{1,0:T(8,128)(2,1)S(1)} %get-tuple-element.37.refs_0_), channel_id=1, source_target_pairs={{0,8},{4,12},{8,0},{12,4},{1,9},{5,13},{9,1},{13,5},{2,10},{6,14},... | collective-permute-start | bytes 393224 | tf_op jit(solution)/shard_map/ppermute | solution.py:295
  5.6 8.9 %collective-permute-start.1 = (bf16[32,2048]{1,0:T(8,128)(2,1)S(1)}, bf16[32,2048]{1,0:T(8,128)(2,1)S(1)}, u32[]{:S(2)}, u32[]{:S(2)}) collective-permute-start(bf16[32,2048]{1,0:T(8,128)(2,1)S(1)} %get-tuple-element.35.refs_5_.refs_0_), channel_id=1, source_target_pairs={{0,4},{4,0},{8,12},{12,8},{1,5},{5,1},{9,13},{13,9},{2,6},{6,2},{1... | collective-permute-start | bytes 393224 | tf_op jit(solution)/shard_map/ppermute | solution.py:295
  5.8 9.2 %collective-permute-start.2 = (bf16[32,2048]{1,0:T(8,128)(2,1)S(1)}, bf16[32,2048]{1,0:T(8,128)(2,1)S(1)}, u32[]{:S(2)}, u32[]{:S(2)}) collective-permute-start(bf16[32,2048]{1,0:T(8,128)(2,1)S(1)} %get-tuple-element.35.refs_5_.refs_0_), channel_id=1, source_target_pairs={{0,8},{4,12},{8,0},{12,4},{1,9},{5,13},{9,1},{13,5},{2,10},{6,14},... | collective-permute-start | bytes 393224 | tf_op jit(solution)/shard_map/ppermute | solution.py:295
  10.8 6.8 %collective-permute-start.6 = (bf16[32,2048]{1,0:T(8,128)(2,1)S(1)}, bf16[32,2048]{1,0:T(8,128)(2,1)S(1)}, u32[]{:S(2)}, u32[]{:S(2)}) collective-permute-start(bf16[32,2048]{1,0:T(8,128)(2,1)S(1)} %hand_on.4.refs_1_.refs_2_), channel_id=1, source_target_pairs={{0,4},{4,0},{8,12},{12,8},{1,5},{5,1},{9,13},{13,9},{2,6},{6,2},{1... | collective-permute-start | bytes 393224 | tf_op jit(solution)/shard_map/ppermute | solution.py:295
  12.2 8.2 %collective-permute-start.7 = (bf16[32,2048]{1,0:T(8,128)(2,1)S(1)}, bf16[32,2048]{1,0:T(8,128)(2,1)S(1)}, u32[]{:S(2)}, u32[]{:S(2)}) collective-permute-start(bf16[32,2048]{1,0:T(8,128)(2,1)S(1)} %get-tuple-element.44.refs_0_), channel_id=1, source_target_pairs={{0,8},{4,12},{8,0},{12,4},{1,9},{5,13},{9,1},{13,5},{2,10},{6,14},... | collective-permute-start | bytes 393224 | tf_op jit(solution)/shard_map/ppermute | solution.py:295
  15.0 9.1 %collective-permute-start.5 = (bf16[32,2048]{1,0:T(8,128)(2,1)S(1)}, bf16[32,2048]{1,0:T(8,128)(2,1)S(1)}, u32[]{:S(2)}, u32[]{:S(2)}) collective-permute-start(bf16[32,2048]{1,0:T(8,128)(2,1)S(1)} %hand_on.5.refs_5_.refs_2_), channel_id=1, source_target_pairs={{0,4},{4,0},{8,12},{12,8},{1,5},{5,1},{9,13},{13,9},{2,6},{6,2},{1... | collective-permute-start | bytes 393224 | tf_op jit(solution)/shard_map/ppermute | solution.py:295
  17.1 9.1 %collective-permute-start = (bf16[32,2048]{1,0:T(8,128)(2,1)S(1)}, bf16[32,2048]{1,0:T(8,128)(2,1)S(1)}, u32[]{:S(2)}, u32[]{:S(2)}) collective-permute-start(bf16[32,2048]{1,0:T(8,128)(2,1)S(1)} %get-tuple-element.36.refs_1_.refs_0_), channel_id=1, source_target_pairs={{0,8},{4,12},{8,0},{12,4},{1,9},{5,13},{9,1},{13,5},{2,10},{6,14},... | collective-permute-start | bytes 393224 | tf_op jit(solution)/shard_map/ppermute | solution.py:295
  20.5 8.2 %collective-permute-start.8 = (bf16[32,2048]{1,0:T(8,128)(2,1)S(1)}, bf16[32,2048]{1,0:T(8,128)(2,1)S(1)}, u32[]{:S(2)}, u32[]{:S(2)}) collective-permute-start(bf16[32,2048]{1,0:T(8,128)(2,1)S(1)} %get-tuple-element.48), channel_id=1, source_target_pairs={{0,4},{4,0},{8,12},{12,8},{1,5},{5,1},{9,13},{13,9},{2,6},{6,2},{1... | collective-permute-start | bytes 393224 | tf_op jit(solution)/shard_map/ppermute | solution.py:295
  26.3 5.3 %collective-permute-start.11 = (bf16[32,2048]{1,0:T(8,128)(2,1)S(1)}, bf16[32,2048]{1,0:T(8,128)(2,1)S(1)}, u32[]{:S(2)}, u32[]{:S(2)}) collective-permute-start(bf16[32,2048]{1,0:T(8,128)(2,1)S(1)} %get-tuple-element.55), channel_id=1, source_target_pairs={{0,4},{4,0},{8,12},{12,8},{1,5},{5,1},{9,13},{13,9},{2,6},{6,2},{1... | collective-permute-start | bytes 393224 | tf_op jit(solution)/shard_map/ppermute | solution.py:295
  28.6 10.1 %collective-permute-start.10 = (bf16[32,2048]{1,0:T(8,128)(2,1)S(1)}, bf16[32,2048]{1,0:T(8,128)(2,1)S(1)}, u32[]{:S(2)}, u32[]{:S(2)}) collective-permute-start(bf16[32,2048]{1,0:T(8,128)(2,1)S(1)} %hand_on.7), channel_id=1, source_target_pairs={{0,4},{4,0},{8,12},{12,8},{1,5},{5,1},{9,13},{13,9},{2,6},{6,2},{1... | collective-permute-start | bytes 393224 | tf_op jit(solution)/shard_map/ppermute | solution.py:295
  31.5 8.3 %collective-permute-start.9 = (bf16[32,2048]{1,0:T(8,128)(2,1)S(1)}, bf16[32,2048]{1,0:T(8,128)(2,1)S(1)}, u32[]{:S(2)}, u32[]{:S(2)}) collective-permute-start(bf16[32,2048]{1,0:T(8,128)(2,1)S(1)} %hand_on.6), channel_id=1, source_target_pairs={{0,4},{4,0},{8,12},{12,8},{1,5},{5,1},{9,13},{13,9},{2,6},{6,2},{1... | collective-permute-start | bytes 393224 | tf_op jit(solution)/shard_map/ppermute | solution.py:295
  32.7 4.8 %collective-permute-start.12 = (f32[32,768]{1,0:T(8,128)S(1)}, f32[32,768]{1,0:T(8,128)S(1)}, u32[]{:S(2)}, u32[]{:S(2)}) collective-permute-start(f32[32,768]{1,0:T(8,128)S(1)} %get-tuple-element.60), channel_id=1, source_target_pairs={{0,1},{1,0},{2,3},{3,2},{4,5},{5,4},{6,7},{7,6},{8,9},{9,8},{10,11... | collective-permute-start | bytes 294920 | tf_op jit(solution)/shard_map/ppermute | solution.py:295
  37.5 4.1 %collective-permute-start.13 = (f32[32,768]{1,0:T(8,128)S(1)}, f32[32,768]{1,0:T(8,128)S(1)}, u32[]{:S(2)}, u32[]{:S(2)}) collective-permute-start(f32[32,768]{1,0:T(8,128)S(1)} %add.2.refs_4_), channel_id=1, source_target_pairs={{0,2},{2,0},{1,3},{3,1},{4,6},{6,4},{5,7},{7,5},{8,10},{10,8},{9,1... | collective-permute-start | bytes 294920 | tf_op jit(solution)/shard_map/ppermute | solution.py:295
  40.9 1.6 %collective-permute-start.14 = (f32[32,768]{1,0:T(8,128)S(1)}, f32[32,768]{1,0:T(8,128)S(1)}, u32[]{:S(2)}, u32[]{:S(2)}) collective-permute-start(f32[32,768]{1,0:T(8,128)S(1)} %get-tuple-element.64), channel_id=1, source_target_pairs={{0,1},{1,0},{2,3},{3,2},{4,5},{5,4},{6,7},{7,6},{8,9},{9,8},{10,11... | collective-permute-start | bytes 294920 | tf_op jit(solution)/shard_map/ppermute | solution.py:295

commit v7 on v6

--- a/solution.py
+++ b/solution.py
@@ -6,7 +6,7 @@
 from jax.sharding import PartitionSpec as P
 
 CHUNKS = (6, 6, 4)
-QUARTERS = (4, 4, 4, 4)
+QUARTERS = (17, 16, 16, 15)
 VMEM = pl.BlockSpec(memory_space=pltpu.VMEM)
 SMEM = pl.BlockSpec(memory_space=pltpu.SMEM)
 HBM = pl.BlockSpec(memory_space=pltpu.HBM)
@@ -329,7 +329,7 @@
     )
     across = add(kept, swap(sent, "sub", 1))
     from_far = swap(across, "ckpt", 1)
-    (second_sums,) = score([second3], train3, picked=(one_sums, three_sums), after=[across])
+    (second_sums,) = score([second3], train3, picked=(one_sums, three_sums), after=[sent])
     sent, kept = score_and_part([second4], train4, [second_sums], rate, (own_sums, two_sums))
     return add(kept, from_far, swap(sent, "sub", 1))
 

time: 43.7 us -> 43.5 us (level)
  starting transfers between devices: 23.1 us -> 24.7 us
  waiting for transfers between devices: 6.52 us -> 5.09 us
    ppermute x15, starting transfers between devices: 23.1 us -> 24.7 us  [swap(): return lax.ppermute(array, axis, [(i, i ^ distance) for i in range(size)])]
    ppermute x15, waiting for transfers between devices: 6.52 us -> 5.09 us  [swap(): return lax.ppermute(array, axis, [(i, i ^ distance) for i in range(size)])]
  transfers between devices with their start and end apart: 15 -> 15, of which waited for: 7 -> 8; matrix products, arithmetic and copies ran while one was open for 0% -> 0% of each run, Pallas kernels for 27% -> 26%
where the time goes in v7:
time: 43.5 us; the launch traced here: 43.1 us
  starting transfers between devices  24.7 us (57%)
  Pallas kernels  13.1 us (30%)
  waiting for transfers between devices  5.09 us (12%)
    ppermute x15, starting transfers between devices, swap(): return lax.ppermute(array, axis, [(i, i ^ distance) for i in range(size)])  24.7 us
    pallas_call x16, Pallas kernels, call(): pl.pallas_call(body, in_specs=specs, out_specs=out_specs or [VMEM] * len(...  13.1 us
    ppermute x15, waiting for transfers between devices, swap(): return lax.ppermute(array, axis, [(i, i ^ distance) for i in range(size)])  5.09 us
  transfers between devices with their start and end apart: 15, of which 8 were waited for; matrix products, arithmetic and copies ran while one was open for 0% of the time, Pallas kernels for 26%

profile of v7, /device:TPU:1, one launch (start us, length us, event | category | flops | bytes accessed | tf_op | source)
XLA Modules:
  0.0 43.1 jit_solution(8945335299664212792)
XLA Ops:
  0.0 1.1 %condition.1 = (bf16[32,2176]{1,0:T(8,128)(2,1)S(1)}, bf16[32,2048]{1,0:T(8,128)(2,1)S(1)}) custom-call(bf16[768,8192]{1,0:T(8,128)(2,1)} %bitcast.2, f32[32,8192]{1,0:T(8,128)} %bitcast.4, f32[1,8192]{1,0:T(1,128)} %refs_4_.1), custom_call_target="tpu_custom_call" | custom-call | tf_op jit(solution)/shard_map/condition/pallas_call | solution.py:36
  1.1 2.2 %collective-permute-start.4 = (bf16[32,2176]{1,0:T(8,128)(2,1)S(1)}, bf16[32,2176]{1,0:T(8,128)(2,1)S(1)}, u32[]{:S(2)}, u32[]{:S(2)}) collective-permute-start(bf16[32,2176]{1,0:T(8,128)(2,1)S(1)} %get-tuple-element.37.refs_0_), channel_id=1, source_target_pairs={{0,4},{4,0},{8,12},{12,8},{1,5},{5,1},{9,13},{13,9},{2,6},{6,2},{1... | collective-permute-start | bytes 417800 | tf_op jit(solution)/shard_map/ppermute | solution.py:295
  3.3 2.3 %collective-permute-start.3 = (bf16[32,2176]{1,0:T(8,128)(2,1)S(1)}, bf16[32,2176]{1,0:T(8,128)(2,1)S(1)}, u32[]{:S(2)}, u32[]{:S(2)}) collective-permute-start(bf16[32,2176]{1,0:T(8,128)(2,1)S(1)} %get-tuple-element.37.refs_0_), channel_id=1, source_target_pairs={{0,8},{4,12},{8,0},{12,4},{1,9},{5,13},{9,1},{13,5},{2,10},{6,14},... | collective-permute-start | bytes 417800 | tf_op jit(solution)/shard_map/ppermute | solution.py:295
  5.8 4.9 %fetch.1 = (bf16[32,2048]{1,0:T(8,128)(2,1)S(1)}, bf16[32,1920]{1,0:T(8,128)(2,1)S(1)}, bf16[768,2176]{1,0:T(8,128)(2,1)S(1)}, bf16[768,2048]{1,0:T(8,128)(2,1)S...) custom-call(bf16[768,8192]{1,0:T(8,128)(2,1)} %bitcast.3, f32[64]{0:T(128)} %refs_1_.1, ...), custom_call_target="tpu_custom_call" | custom-call | flops 644245120 | tf_op jit(solution)/shard_map/fetch/pallas_call | solution.py:36
  10.8 1.4 %collective-permute-start.6 = (bf16[32,2176]{1,0:T(8,128)(2,1)S(1)}, bf16[32,2176]{1,0:T(8,128)(2,1)S(1)}, u32[]{:S(2)}, u32[]{:S(2)}) collective-permute-start(bf16[32,2176]{1,0:T(8,128)(2,1)S(1)} %hand_on.4.refs_1_.refs_2_), channel_id=1, source_target_pairs={{0,4},{4,0},{8,12},{12,8},{1,5},{5,1},{9,13},{13,9},{2,6},{6,2},{1... | collective-permute-start | bytes 417800 | tf_op jit(solution)/shard_map/ppermute | solution.py:295
  12.2 2.3 %collective-permute-start.7 = (bf16[32,2048]{1,0:T(8,128)(2,1)S(1)}, bf16[32,2048]{1,0:T(8,128)(2,1)S(1)}, u32[]{:S(2)}, u32[]{:S(2)}) collective-permute-start(bf16[32,2048]{1,0:T(8,128)(2,1)S(1)} %get-tuple-element.44.refs_0_), channel_id=1, source_target_pairs={{0,8},{4,12},{8,0},{12,4},{1,9},{5,13},{9,1},{13,5},{2,10},{6,14},... | collective-permute-start | bytes 393224 | tf_op jit(solution)/shard_map/ppermute | solution.py:295
  14.5 0.7 %collective-permute-done.2.refs_0_ = bf16[32,2048]{1,0:T(8,128)(2,1)S(1)} collective-permute-done((bf16[32,2048]{1,0:T(8,128)(2,1)S(1)}, bf16[32,2048]{1,0:T(8,128)(2,1)S(1)}, u32[]{:S(2)}, u32[]{:S(2)}) %collective-permute-start.2) | collective-permute-done | bytes 131104 | tf_op jit(solution)/shard_map/ppermute | solution.py:295
  15.2 2.3 %collective-permute-start.5 = (bf16[32,2048]{1,0:T(8,128)(2,1)S(1)}, bf16[32,2048]{1,0:T(8,128)(2,1)S(1)}, u32[]{:S(2)}, u32[]{:S(2)}) collective-permute-start(bf16[32,2048]{1,0:T(8,128)(2,1)S(1)} %hand_on.5.refs_5_.refs_2_), channel_id=1, source_target_pairs={{0,4},{4,0},{8,12},{12,8},{1,5},{5,1},{9,13},{13,9},{2,6},{6,2},{1... | collective-permute-start | bytes 393224 | tf_op jit(solution)/shard_map/ppermute | solution.py:295
  17.5 1.6 %collective-permute-start = (bf16[32,1920]{1,0:T(8,128)(2,1)S(1)}, bf16[32,1920]{1,0:T(8,128)(2,1)S(1)}, u32[]{:S(2)}, u32[]{:S(2)}) collective-permute-start(bf16[32,1920]{1,0:T(8,128)(2,1)S(1)} %get-tuple-element.36.refs_1_.refs_0_), channel_id=1, source_target_pairs={{0,8},{4,12},{8,0},{12,4},{1,9},{5,13},{9,1},{13,5},{2,10},{6,14},... | collective-permute-start | bytes 368648 | tf_op jit(solution)/shard_map/ppermute | solution.py:295
  19.1 1.1 %score.4 = (f32[32,768]{1,0:T(8,128)S(1)}, f32[32,768]{1,0:T(8,128)S(1)}, f32[32,768]{1,0:T(8,128)S(1)}, f32[32,768]{1,0:T(8,128)S(1)}) custom-call(bf16[32,2176]{1,0:T(8,128)(2,1)S(1)} %get-tuple-element.37.refs_0_, bf16[32,2176]{1,0:T(8,128)(2,1)S(1)} %collective-permute-done.4.refs_2_.refs_1_, bf16[32,2176]{1,0:T(8,128)(2,1)S(1)} %hand_on.4.refs_1_.refs_2_, ...), custom_call_target="tpu_custom_call" | custom-call | flops 85563800 | tf_op jit(solution)/shard_map/score/pallas_call | solution.py:36
  20.7 2.6 %collective-permute-start.8 = (bf16[32,2048]{1,0:T(8,128)(2,1)S(1)}, bf16[32,2048]{1,0:T(8,128)(2,1)S(1)}, u32[]{:S(2)}, u32[]{:S(2)}) collective-permute-start(bf16[32,2048]{1,0:T(8,128)(2,1)S(1)} %get-tuple-element.48), channel_id=1, source_target_pairs={{0,4},{4,0},{8,12},{12,8},{1,5},{5,1},{9,13},{13,9},{2,6},{6,2},{1... | collective-permute-start | bytes 393224 | tf_op jit(solution)/shard_map/ppermute | solution.py:295
  23.4 1.2 %collective-permute-done.5.refs_3_ = bf16[32,2048]{1,0:T(8,128)(2,1)S(1)} collective-permute-done((bf16[32,2048]{1,0:T(8,128)(2,1)S(1)}, bf16[32,2048]{1,0:T(8,128)(2,1)S(1)}, u32[]{:S(2)}, u32[]{:S(2)}) %collective-permute-start.5) | collective-permute-done | bytes 131104 | tf_op jit(solution)/shard_map/ppermute | solution.py:295
  24.6 1.2 %score.5 = (f32[32,768]{1,0:T(8,128)S(1)}, f32[32,768]{1,0:T(8,128)S(1)}, f32[32,768]{1,0:T(8,128)S(1)}, f32[32,768]{1,0:T(8,128)S(1)}) custom-call(bf16[32,2048]{1,0:T(8,128)(2,1)S(1)} %get-tuple-element.35.refs_5_.refs_0_, bf16[32,2048]{1,0:T(8,128)(2,1)S(1)} %collective-permute-done.1.refs_2_.refs_1_, bf16[32,2048]{1,0:T(8,128)(2,1)S(1)} %hand_on.5.refs_5_.refs_2_, ...), custom_call_target="tpu_custom_call" | custom-call | flops 80530640 | tf_op jit(solution)/shard_map/score/pallas_call | solution.py:36
  26.0 2.8 %collective-permute-start.11 = (bf16[32,1920]{1,0:T(8,128)(2,1)S(1)}, bf16[32,1920]{1,0:T(8,128)(2,1)S(1)}, u32[]{:S(2)}, u32[]{:S(2)}) collective-permute-start(bf16[32,1920]{1,0:T(8,128)(2,1)S(1)} %get-tuple-element.55), channel_id=1, source_target_pairs={{0,4},{4,0},{8,12},{12,8},{1,5},{5,1},{9,13},{13,9},{2,6},{6,2},{1... | collective-permute-start | bytes 368648 | tf_op jit(solution)/shard_map/ppermute | solution.py:295
  29.4 1.7 %collective-permute-start.10 = (bf16[32,2048]{1,0:T(8,128)(2,1)S(1)}, bf16[32,2048]{1,0:T(8,128)(2,1)S(1)}, u32[]{:S(2)}, u32[]{:S(2)}) collective-permute-start(bf16[32,2048]{1,0:T(8,128)(2,1)S(1)} %hand_on.7), channel_id=1, source_target_pairs={{0,4},{4,0},{8,12},{12,8},{1,5},{5,1},{9,13},{13,9},{2,6},{6,2},{1... | collective-permute-start | bytes 393224 | tf_op jit(solution)/shard_map/ppermute | solution.py:295
  31.1 1.1 %score.6 = (f32[32,768]{1,0:T(8,128)S(1)}, f32[32,768]{1,0:T(8,128)S(1)}, f32[32,768]{1,0:T(8,128)S(1)}) custom-call(bf16[32,2048]{1,0:T(8,128)(2,1)S(1)} %get-tuple-element.44.refs_0_, bf16[32,2048]{1,0:T(8,128)(2,1)S(1)} %collective-permute-done.7.refs_1_, bf16[32,2048]{1,0:T(8,128)(2,1)S(1)} %collective-permute-done.8.refs_2_.refs_1_, ...), custom_call_target="tpu_custom_call" | custom-call | flops 80530640 | tf_op jit(solution)/shard_map/score/pallas_call | solution.py:36
  32.3 1.0 %score_and_part.2 = (f32[32,768]{1,0:T(8,128)S(1)}, f32[32,768]{1,0:T(8,128)S(1)}, f32[32,768]{1,0:T(8,128)S(1)}, f32[32,768]{1,0:T(8,128)S(1)}) custom-call(bf16[32,1920]{1,0:T(8,128)(2,1)S(1)} %get-tuple-element.36.refs_1_.refs_0_, bf16[32,1920]{1,0:T(8,128)(2,1)S(1)} %collective-permute-done.refs_1_, ...), custom_call_target="tpu_custom_call" | custom-call | flops 75497472 | tf_op jit(solution)/shard_map/score_and_part/pallas_call | solution.py:36
  33.2 3.3 %collective-permute-start.12 = (f32[32,768]{1,0:T(8,128)S(1)}, f32[32,768]{1,0:T(8,128)S(1)}, u32[]{:S(2)}, u32[]{:S(2)}) collective-permute-start(f32[32,768]{1,0:T(8,128)S(1)} %get-tuple-element.59.refs_4_), channel_id=1, source_target_pairs={{0,1},{1,0},{2,3},{3,2},{4,5},{5,4},{6,7},{7,6},{8,9},{9,8},{10,11... | collective-permute-start | bytes 294920 | tf_op jit(solution)/shard_map/ppermute | solution.py:295
  36.5 0.9 %collective-permute-done.12.refs_1_ = f32[32,768]{1,0:T(8,128)S(1)} collective-permute-done((f32[32,768]{1,0:T(8,128)S(1)}, f32[32,768]{1,0:T(8,128)S(1)}, u32[]{:S(2)}, u32[]{:S(2)}) %collective-permute-start.12) | collective-permute-done | bytes 98336 | tf_op jit(solution)/shard_map/ppermute | solution.py:295
  37.5 1.3 %collective-permute-start.13 = (f32[32,768]{1,0:T(8,128)S(1)}, f32[32,768]{1,0:T(8,128)S(1)}, u32[]{:S(2)}, u32[]{:S(2)}) collective-permute-start(f32[32,768]{1,0:T(8,128)S(1)} %add.2), channel_id=1, source_target_pairs={{0,2},{2,0},{1,3},{3,1},{4,6},{6,4},{5,7},{7,5},{8,10},{10,8},{9,1... | collective-permute-start | bytes 294920 | tf_op jit(solution)/shard_map/ppermute | solution.py:295
  38.8 1.0 %score.7.refs_2_ = f32[32,768]{1,0:T(8,128)S(1)} custom-call(bf16[32,2048]{1,0:T(8,128)(2,1)S(1)} %collective-permute-done.10.refs_0_, bf16[768,2048]{1,0:T(8,128)(2,1)S(1)} %get-tuple-element.49.refs_3_.refs_1_, f32[32,768]{1,0:T(8,128)S(1)} %get-tuple-element.52.refs_7_.refs_2_, f32[32,768]{1,0:T(8,128)S(1)} %get-tuple-element.51.refs_6_.refs_3_, ...), custom_call_target="tpu_custom_call" | custom-call | flops 80530640 | tf_op jit(solution)/shard_map/score/pallas_call | solution.py:36
  39.8 1.0 %score_and_part.3 = (f32[32,768]{1,0:T(8,128)S(1)}, f32[32,768]{1,0:T(8,128)S(1)}) custom-call(bf16[32,1920]{1,0:T(8,128)(2,1)S(1)} %collective-permute-done.9.refs_0_, bf16[768,1920]{1,0:T(8,128)(2,1)S(1)} %get-tuple-element.54.refs_3_.refs_1_, f32[32,768]{1,0:T(8,128)S(1)} %score.7.refs_2_, f32[1,768]{1,0:T(1,128)S(1)} %get-tuple-element.58.refs_7_.refs_3_, ...), custom_call_target="tpu_custom_call" | custom-call | flops 75497472 | tf_op jit(solution)/shard_map/score_and_part/pallas_call | solution.py:36
  40.8 0.7 %collective-permute-start.14 = (f32[32,768]{1,0:T(8,128)S(1)}, f32[32,768]{1,0:T(8,128)S(1)}, u32[]{:S(2)}, u32[]{:S(2)}) collective-permute-start(f32[32,768]{1,0:T(8,128)S(1)} %get-tuple-element.64), channel_id=1, source_target_pairs={{0,1},{1,0},{2,3},{3,2},{4,5},{5,4},{6,7},{7,6},{8,9},{9,8},{10,11... | collective-permute-start | bytes 294920 | tf_op jit(solution)/shard_map/ppermute | solution.py:295
  41.6 0.8 %collective-permute-done.14.refs_2_ = f32[32,768]{1,0:T(8,128)S(1)} collective-permute-done((f32[32,768]{1,0:T(8,128)S(1)}, f32[32,768]{1,0:T(8,128)S(1)}, u32[]{:S(2)}, u32[]{:S(2)}) %collective-permute-start.14) | collective-permute-done | bytes 98336 | tf_op jit(solution)/shard_map/ppermute | solution.py:295
  (22 shorter events, 2.4 us)
Async XLA Ops:
  1.1 9.6 %collective-permute-start.4 = (bf16[32,2176]{1,0:T(8,128)(2,1)S(1)}, bf16[32,2176]{1,0:T(8,128)(2,1)S(1)}, u32[]{:S(2)}, u32[]{:S(2)}) collective-permute-start(bf16[32,2176]{1,0:T(8,128)(2,1)S(1)} %get-tuple-element.37.refs_0_), channel_id=1, source_target_pairs={{0,4},{4,0},{8,12},{12,8},{1,5},{5,1},{9,13},{13,9},{2,6},{6,2},{1... | collective-permute-start | bytes 417800 | tf_op jit(solution)/shard_map/ppermute | solution.py:295
  3.3 7.4 %collective-permute-start.3 = (bf16[32,2176]{1,0:T(8,128)(2,1)S(1)}, bf16[32,2176]{1,0:T(8,128)(2,1)S(1)}, u32[]{:S(2)}, u32[]{:S(2)}) collective-permute-start(bf16[32,2176]{1,0:T(8,128)(2,1)S(1)} %get-tuple-element.37.refs_0_), channel_id=1, source_target_pairs={{0,8},{4,12},{8,0},{12,4},{1,9},{5,13},{9,1},{13,5},{2,10},{6,14},... | collective-permute-start | bytes 417800 | tf_op jit(solution)/shard_map/ppermute | solution.py:295
  5.6 8.9 %collective-permute-start.1 = (bf16[32,2048]{1,0:T(8,128)(2,1)S(1)}, bf16[32,2048]{1,0:T(8,128)(2,1)S(1)}, u32[]{:S(2)}, u32[]{:S(2)}) collective-permute-start(bf16[32,2048]{1,0:T(8,128)(2,1)S(1)} %get-tuple-element.35.refs_5_.refs_0_), channel_id=1, source_target_pairs={{0,4},{4,0},{8,12},{12,8},{1,5},{5,1},{9,13},{13,9},{2,6},{6,2},{1... | collective-permute-start | bytes 393224 | tf_op jit(solution)/shard_map/ppermute | solution.py:295
  5.8 9.4 %collective-permute-start.2 = (bf16[32,2048]{1,0:T(8,128)(2,1)S(1)}, bf16[32,2048]{1,0:T(8,128)(2,1)S(1)}, u32[]{:S(2)}, u32[]{:S(2)}) collective-permute-start(bf16[32,2048]{1,0:T(8,128)(2,1)S(1)} %get-tuple-element.35.refs_5_.refs_0_), channel_id=1, source_target_pairs={{0,8},{4,12},{8,0},{12,4},{1,9},{5,13},{9,1},{13,5},{2,10},{6,14},... | collective-permute-start | bytes 393224 | tf_op jit(solution)/shard_map/ppermute | solution.py:295
  10.8 8.3 %collective-permute-start.6 = (bf16[32,2176]{1,0:T(8,128)(2,1)S(1)}, bf16[32,2176]{1,0:T(8,128)(2,1)S(1)}, u32[]{:S(2)}, u32[]{:S(2)}) collective-permute-start(bf16[32,2176]{1,0:T(8,128)(2,1)S(1)} %hand_on.4.refs_1_.refs_2_), channel_id=1, source_target_pairs={{0,4},{4,0},{8,12},{12,8},{1,5},{5,1},{9,13},{13,9},{2,6},{6,2},{1... | collective-permute-start | bytes 417800 | tf_op jit(solution)/shard_map/ppermute | solution.py:295
  12.2 8.5 %collective-permute-start.7 = (bf16[32,2048]{1,0:T(8,128)(2,1)S(1)}, bf16[32,2048]{1,0:T(8,128)(2,1)S(1)}, u32[]{:S(2)}, u32[]{:S(2)}) collective-permute-start(bf16[32,2048]{1,0:T(8,128)(2,1)S(1)} %get-tuple-element.44.refs_0_), channel_id=1, source_target_pairs={{0,8},{4,12},{8,0},{12,4},{1,9},{5,13},{9,1},{13,5},{2,10},{6,14},... | collective-permute-start | bytes 393224 | tf_op jit(solution)/shard_map/ppermute | solution.py:295
  15.2 9.3 %collective-permute-start.5 = (bf16[32,2048]{1,0:T(8,128)(2,1)S(1)}, bf16[32,2048]{1,0:T(8,128)(2,1)S(1)}, u32[]{:S(2)}, u32[]{:S(2)}) collective-permute-start(bf16[32,2048]{1,0:T(8,128)(2,1)S(1)} %hand_on.5.refs_5_.refs_2_), channel_id=1, source_target_pairs={{0,4},{4,0},{8,12},{12,8},{1,5},{5,1},{9,13},{13,9},{2,6},{6,2},{1... | collective-permute-start | bytes 393224 | tf_op jit(solution)/shard_map/ppermute | solution.py:295
  17.5 8.5 %collective-permute-start = (bf16[32,1920]{1,0:T(8,128)(2,1)S(1)}, bf16[32,1920]{1,0:T(8,128)(2,1)S(1)}, u32[]{:S(2)}, u32[]{:S(2)}) collective-permute-start(bf16[32,1920]{1,0:T(8,128)(2,1)S(1)} %get-tuple-element.36.refs_1_.refs_0_), channel_id=1, source_target_pairs={{0,8},{4,12},{8,0},{12,4},{1,9},{5,13},{9,1},{13,5},{2,10},{6,14},... | collective-permute-start | bytes 368648 | tf_op jit(solution)/shard_map/ppermute | solution.py:295
  20.7 8.6 %collective-permute-start.8 = (bf16[32,2048]{1,0:T(8,128)(2,1)S(1)}, bf16[32,2048]{1,0:T(8,128)(2,1)S(1)}, u32[]{:S(2)}, u32[]{:S(2)}) collective-permute-start(bf16[32,2048]{1,0:T(8,128)(2,1)S(1)} %get-tuple-element.48), channel_id=1, source_target_pairs={{0,4},{4,0},{8,12},{12,8},{1,5},{5,1},{9,13},{13,9},{2,6},{6,2},{1... | collective-permute-start | bytes 393224 | tf_op jit(solution)/shard_map/ppermute | solution.py:295
  26.0 6.2 %collective-permute-start.11 = (bf16[32,1920]{1,0:T(8,128)(2,1)S(1)}, bf16[32,1920]{1,0:T(8,128)(2,1)S(1)}, u32[]{:S(2)}, u32[]{:S(2)}) collective-permute-start(bf16[32,1920]{1,0:T(8,128)(2,1)S(1)} %get-tuple-element.55), channel_id=1, source_target_pairs={{0,4},{4,0},{8,12},{12,8},{1,5},{5,1},{9,13},{13,9},{2,6},{6,2},{1... | collective-permute-start | bytes 368648 | tf_op jit(solution)/shard_map/ppermute | solution.py:295
  29.4 9.4 %collective-permute-start.10 = (bf16[32,2048]{1,0:T(8,128)(2,1)S(1)}, bf16[32,2048]{1,0:T(8,128)(2,1)S(1)}, u32[]{:S(2)}, u32[]{:S(2)}) collective-permute-start(bf16[32,2048]{1,0:T(8,128)(2,1)S(1)} %hand_on.7), channel_id=1, source_target_pairs={{0,4},{4,0},{8,12},{12,8},{1,5},{5,1},{9,13},{13,9},{2,6},{6,2},{1... | collective-permute-start | bytes 393224 | tf_op jit(solution)/shard_map/ppermute | solution.py:295
  32.2 7.6 %collective-permute-start.9 = (bf16[32,1920]{1,0:T(8,128)(2,1)S(1)}, bf16[32,1920]{1,0:T(8,128)(2,1)S(1)}, u32[]{:S(2)}, u32[]{:S(2)}) collective-permute-start(bf16[32,1920]{1,0:T(8,128)(2,1)S(1)} %hand_on.6), channel_id=1, source_target_pairs={{0,4},{4,0},{8,12},{12,8},{1,5},{5,1},{9,13},{13,9},{2,6},{6,2},{1... | collective-permute-start | bytes 368648 | tf_op jit(solution)/shard_map/ppermute | solution.py:295
  33.2 4.2 %collective-permute-start.12 = (f32[32,768]{1,0:T(8,128)S(1)}, f32[32,768]{1,0:T(8,128)S(1)}, u32[]{:S(2)}, u32[]{:S(2)}) collective-permute-start(f32[32,768]{1,0:T(8,128)S(1)} %get-tuple-element.59.refs_4_), channel_id=1, source_target_pairs={{0,1},{1,0},{2,3},{3,2},{4,5},{5,4},{6,7},{7,6},{8,9},{9,8},{10,11... | collective-permute-start | bytes 294920 | tf_op jit(solution)/shard_map/ppermute | solution.py:295
  37.5 4.1 %collective-permute-start.13 = (f32[32,768]{1,0:T(8,128)S(1)}, f32[32,768]{1,0:T(8,128)S(1)}, u32[]{:S(2)}, u32[]{:S(2)}) collective-permute-start(f32[32,768]{1,0:T(8,128)S(1)} %add.2), channel_id=1, source_target_pairs={{0,2},{2,0},{1,3},{3,1},{4,6},{6,4},{5,7},{7,5},{8,10},{10,8},{9,1... | collective-permute-start | bytes 294920 | tf_op jit(solution)/shard_map/ppermute | solution.py:295
  40.8 1.6 %collective-permute-start.14 = (f32[32,768]{1,0:T(8,128)S(1)}, f32[32,768]{1,0:T(8,128)S(1)}, u32[]{:S(2)}, u32[]{:S(2)}) collective-permute-start(f32[32,768]{1,0:T(8,128)S(1)} %get-tuple-element.64), channel_id=1, source_target_pairs={{0,1},{1,0},{2,3},{3,2},{4,5},{5,4},{6,7},{7,6},{8,9},{9,8},{10,11... | collective-permute-start | bytes 294920 | tf_op jit(solution)/shard_map/ppermute | solution.py:295
